TPU v7x, 512 devices: a whole 4x4x16 slice. The times are simulated.
512 devices in a mesh: dp: 64 (over x_hi, z, core), pipe: 8 (over y, x_lo).
Axes of the slice: x: 4 (x_hi: 2, x_lo: 2; x = x_hi * 2 + x_lo), y: 4, z: 16, core: 2. Of those that a mesh axis runs over, the one named last changes fastest.
Arguments:
- hidden: bfloat16 [128, 64, 8192], P('dp', None, 'pipe'), may hold values from -14 to 14
- gain: float32 [8192], P('pipe'), may hold values from 0.5 to 1.5
- keys: bfloat16 [128, 8192], P('dp', 'pipe'), may hold values from -0.0625 to 0.0625
- queue: bfloat16 [16384, 8192], P('dp', 'pipe'), may hold values from -1 to 1
- positive: int32 [128], replicated, may hold values from 0 to 127, each once
- mix_rows: int32 [128, 16], replicated, may hold values from 0 to 16383
- mix_weight: float32 [128, 16], replicated, may hold values from 0 to 0.5
Outputs:
- hidden_grad: float32 [128, 64, 8192], P('dp', None, 'pipe')
Inputs may be any that keep to these rules, and one draw needn't show every extreme that they name: Every row of keys is the positive of exactly one query.
All inputs are finite; a program needn't handle non-finite values.
Results may differ from a plain program's by a relative error of at most 0.0018.
Values may be sent and summed in bfloat16 or wider, within the bound.
No kernel may reach another device: no remote copies, remote signals or barrier semaphores. Data moves between devices by JAX's collectives and lax.ppermute only.
A program may use at most 64 MiB of HBM per device.

v0:
```python
import jax
import jax.numpy as jnp
from jax import lax
from jax.sharding import PartitionSpec as P

COLDNESS_DIVISOR = 0.05
OBJECTIVE_FACTOR = 2048.0
NORM_EPS = 1e-05
MIX_EPS = 1e-06


def against_bank(piece, bank):
    return lax.dot_general(
        piece, bank, (((1,), (1,)), ((), ())), preferred_element_type=jnp.float32
    )


def coefficients(summed, queue_square, positive, mix_rows, mix_weight, queue_rows):
    count = summed.shape[0]
    shard = lax.axis_index("dp")
    memory_bank_cosine = summed[:, :queue_rows]
    positive_cosine = summed[:, queue_rows:]
    key_count = positive_cosine.shape[1]
    picks = mix_rows - shard * queue_rows
    owners = positive - shard * key_count
    present = (picks >= 0) & (picks < queue_rows)
    safe = jnp.clip(picks, 0, queue_rows - 1)
    cosine = jnp.take_along_axis(memory_bank_cosine, safe, axis=1)
    upper_part_amount = mix_weight + (1.0 - mix_weight) * cosine
    ball_extent_power_two = (
        mix_weight * mix_weight
        + (1.0 - mix_weight) ** 2 * queue_square[safe]
        + 2.0 * mix_weight * (1.0 - mix_weight) * cosine
        + MIX_EPS
    )
    ball_extent = jnp.sqrt(ball_extent_power_two)
    combined_energies = upper_part_amount / (COLDNESS_DIVISOR * ball_extent)
    positive_energies = positive_cosine / COLDNESS_DIVISOR
    memory_bank_energies = memory_bank_cosine / COLDNESS_DIVISOR
    masked = jnp.where(present, combined_energies, -jnp.inf)
    local_top = jnp.maximum(
        jnp.maximum(jnp.max(positive_energies, 1), jnp.max(memory_bank_energies, 1)),
        jnp.max(masked, 1),
    )
    row_top = lax.pmax(local_top, "dp")
    shifted = row_top[:, None]
    total = lax.psum(
        jnp.sum(jnp.exp(positive_energies - shifted), 1)
        + jnp.sum(jnp.exp(memory_bank_energies - shifted), 1)
        + jnp.sum(jnp.exp(masked - shifted), 1),
        "dp",
    )
    log_norm = (row_top + jnp.log(total))[:, None]
    target = (owners[:, None] == jnp.arange(key_count, dtype=jnp.int32)[None, :]).astype(
        jnp.float32
    )
    positive_chance = jnp.exp(positive_energies - log_norm) - target
    memory_bank_chance = jnp.exp(memory_bank_energies - log_norm)
    mixed_prob = jnp.where(present, jnp.exp(combined_energies - log_norm), 0.0)
    derivative_rate = (
        1.0
        - mix_weight
        - upper_part_amount * mix_weight * (1.0 - mix_weight) / ball_extent_power_two
    ) / (COLDNESS_DIVISOR * ball_extent)
    row_index = jnp.arange(count, dtype=jnp.int32)[:, None]
    extra_summand = (
        jnp.zeros_like(memory_bank_chance).at[row_index, safe].add(mixed_prob * derivative_rate)
    )
    memory_bank_factor = (
        OBJECTIVE_FACTOR * (memory_bank_chance / COLDNESS_DIVISOR + extra_summand)
    ).astype(jnp.bfloat16)
    positive_factor = (OBJECTIVE_FACTOR / COLDNESS_DIVISOR * positive_chance).astype(jnp.bfloat16)
    return jnp.concatenate([memory_bank_factor, positive_factor], 1)


def shards(hidden, gain, keys, queue, positive, mix_rows, mix_weight):
    queries, seq, width = hidden.shape
    full_width = width * lax.axis_size("pipe")
    queue_rows = queue.shape[0]
    states = hidden.astype(jnp.float32)
    squares = jnp.sum(states * states, axis=-1)
    mean_square = lax.psum(squares, "pipe") / full_width
    inverse_rms = lax.rsqrt(mean_square + NORM_EPS)[:, :, None]
    normed = states * inverse_rms
    pooled = jnp.mean(normed * gain, axis=1)
    length = jnp.sqrt(lax.psum(jnp.sum(pooled * pooled, -1), "pipe"))[:, None]
    query = pooled / length
    query_half = query.astype(jnp.bfloat16)
    bank = jnp.concatenate([queue, keys], 0)
    queue_square = jnp.sum(jnp.square(queue.astype(jnp.float32)), -1)
    partial_value = against_bank(lax.all_gather(query_half, "dp", axis=0, tiled=True), bank)
    summed, queue_square = lax.psum((partial_value, queue_square), "pipe")
    coef = coefficients(summed, queue_square, positive, mix_rows, mix_weight, queue_rows)
    query_grad = lax.psum_scatter(
        jnp.dot(coef, bank, preferred_element_type=jnp.float32),
        "dp",
        scatter_dimension=0,
        tiled=True,
    )
    along = lax.psum(jnp.sum(query * query_grad, -1), "pipe")[:, None]
    scaled_grad = gain * (query_grad - along * query) / length
    token_sum = jnp.sum(scaled_grad[:, None, :] * normed, -1)
    inner = lax.psum(token_sum, "pipe")[:, :, None] / full_width
    return inverse_rms * (scaled_grad[:, None, :] - normed * inner) / seq


def solution(mesh):
    placed = (P("dp", None, "pipe"), P("pipe"), P("dp", "pipe"), P("dp", "pipe"), P(), P(), P())
    return jax.shard_map(
        shards, mesh=mesh, in_specs=placed, out_specs=P("dp", None, "pipe"), check_vma=False
    )
```

profile of v0, /device:TPU:2, one launch (start us, length us, event | category | flops | bytes accessed | tf_op | source)
XLA Modules:
  0.0 1046.4 jit_solution(1743065120044868139)
XLA Ops:
  6.5 1.2 fusion.8
  7.7 21.9 %psum.49 = f32[2,64]{1,0:T(2,128)S(1)} all-reduce(f32[2,64]{1,0:T(2,128)S(1)} %fusion.8), channel_id=1, replica_groups=mesh['dp'=64,'pipe'=8] {'pipe'}, use_global_device_ids=true, to_apply=%region_1.0 | all-reduce | flops 128 | bytes 1024 | tf_op jit(solution)/shard_map/psum | solution.py:82
  29.6 0.8 fusion.3
  30.4 0.1 multiply_reduce_fusion.4
  30.6 1.2 multiply_reduce_fusion
  31.8 16.0 %all-reduce.1 = (f32[2]{0:T(128)S(1)}, f32[256]{0:T(256)S(1)}) all-reduce(f32[2]{0:T(128)S(1)} %multiply_reduce_fusion.4, f32[256]{0:T(256)S(1)} %multiply_reduce_fusion), channel_id=1, replica_groups=mesh['dp'=64,'pipe'=8] {'pipe'}, use_global_device_ids=true, to_apply=%region_4.0 | all-reduce | flops 258 | bytes 2064 | tf_op jit(solution)/shard_map/psum | solution.py:86
  47.9 0.1 convert_bitcast_fusion
  48.0 81.6 %all-gather = bf16[64,2,1024]{2,1,0:T(2,128)(2,1)S(1)} all-gather(bf16[1,2,1024]{2,1,0:T(2,128)(2,1)S(1)} %get-tuple-element.12), channel_id=1, replica_groups=mesh['dp'=64,'pipe'=8] {'dp'}, dimensions={0}, use_global_device_ids=true | all-gather | bytes 266240 | tf_op jit(solution)/shard_map/all_gather | solution.py:91
  129.5 0.1 reshape.53
  129.6 0.6 copy-done.6
  130.2 1.0 fusion.22
  131.3 0.6 copy-done.3
  131.9 0.1 copy.46
  132.0 0.1 reshape.32
  132.1 13.1 %gather_fusion = f32[2048]{0:T(1024)S(1)} fusion(f32[256]{0:T(256)S(1)} %get-tuple-element.6, s32[2048]{0:T(1024)S(1)} %broadcast_clamp_fusion), kind=kCustom, calls=%fused_computation | custom fusion | bytes 24576 | tf_op jit(solution)/shard_map/gather | solution.py:32
  145.3 0.1 reshape.31
  145.4 0.1 copy.44
  145.5 0.1 reshape.38
  145.6 0.6 copy-done.8
  146.3 0.1 and_reduce_fusion
  146.4 0.6 copy-done.7
  146.9 0.1 multiply_reduce_fusion.2
  147.0 0.1 copy.49
  147.1 0.1 reshape.44
  147.2 0.6 copy-done.9
  147.8 56.1 %all-reduce.5.cloned.1.call-done = f32[128,258]{0,1:T(8,128)} async-done(((f32[128,258]{0,1:T(8,128)}), f32[128,258]{0,1:T(8,128)}) %all-reduce.5.cloned.1.call-update) | async-done | bytes 132112 | tf_op jit(solution)/shard_map/psum | solution.py:92
  203.9 1.0 multiply_reduce_fusion.1
  204.9 13.5 %gather_fusion.1 = f32[2048]{0:T(1024)S(1)} fusion(f32[128,256]{0,1:T(8,128)S(1)} %get-tuple-element.15, s32[2048]{0:T(1024)S(1)} %reshape.38), kind=kCustom, calls=%fused_computation.1 | custom fusion | bytes 32768 | tf_op jit(solution)/shard_map/jit(take_along_axis)/gather | solution.py:28
  218.4 0.1 reshape.41
  218.5 0.6 copy-done.4
  219.2 0.1 copy-done.2
  219.3 128.9 %pmax.7 = f32[128]{0:T(128)S(1)} all-reduce(f32[128]{0:T(128)S(1)} %maximum_maximum_fusion), channel_id=1, replica_groups=mesh['dp'=64,'pipe'=8] {'dp'}, use_global_device_ids=true, to_apply=%region_11.12 | all-reduce | flops 128 | bytes 1024 | tf_op jit(solution)/shard_map/pmax | solution.py:45
  348.3 129.1 %psum.53 = f32[128]{0:T(128)S(1)} all-reduce(f32[128]{0:T(128)S(1)} %add_add_fusion.1), channel_id=1, replica_groups=mesh['dp'=64,'pipe'=8] {'dp'}, use_global_device_ids=true, to_apply=%region_15.16 | all-reduce | flops 128 | bytes 1024 | tf_op jit(solution)/shard_map/psum | solution.py:47
  477.4 0.1 copy.51
  477.6 0.1 copy.48
  477.7 0.1 copy.52
  477.8 0.1 copy.50
  477.9 0.1 reshape.46
  478.0 14.7 %scatter_fusion = f32[32768]{0:T(1024)S(1)} fusion(f32[32768]{0:T(1024)S(1)} %bitcast.12, s32[2048]{0:T(1024)S(1)} %reshape.44, f32[2048]{0:T(1024)S(1)} %reshape.46), kind=kCustom, calls=%fused_computation.2 | custom fusion | flops 2048 | bytes 32768
  492.7 1.1 fusion.9
  493.9 1.4 dynamic-slice
  495.9 504.4 %all-reduce.7.cloned.1.call-done = f32[128,1024]{1,0:T(8,128)} async-done(((f32[128,1024]{1,0:T(8,128)}), f32[128,1024]{1,0:T(8,128)}) %all-reduce.7.cloned.1.call-update) | async-done | bytes 524304
  1000.4 0.9 multiply_reduce_fusion.3
  1001.2 17.5 %psum.54 = f32[2]{0:T(128)S(1)} all-reduce(f32[2]{0:T(128)S(1)} %multiply_reduce_fusion.3), channel_id=1, replica_groups=mesh['dp'=64,'pipe'=8] {'pipe'}, use_global_device_ids=true, to_apply=%region_19.20 | all-reduce | flops 2 | bytes 16 | tf_op jit(solution)/shard_map/psum | solution.py:100
  1018.8 0.8 multiply_divide_fusion
  1019.6 0.2 fusion.4
  1019.8 18.7 %psum.55 = f32[2,64]{1,0:T(2,128)S(1)} all-reduce(f32[2,64]{1,0:T(2,128)S(1)} %fusion.4), channel_id=1, replica_groups=mesh['dp'=64,'pipe'=8] {'pipe'}, use_global_device_ids=true, to_apply=%region_21.22 | all-reduce | flops 128 | bytes 1024 | tf_op jit(solution)/shard_map/psum | solution.py:103
  1038.5 1.0 fusion.7
  (42 shorter events, 0.6 us)
Async XLA Ops:
  6.5 23.1 %copy-start = (bf16[2,64,1024]{2,1,0:T(8,128)(2,1)S(1)}, bf16[2,64,1024]{2,1,0:T(8,128)(2,1)}, u32[]{:S(2)}) copy-start(bf16[2,64,1024]{2,1,0:T(8,128)(2,1)} %param.7) | copy-start | bytes 786436
  6.5 25.3 %copy-start.1 = (bf16[256,1024]{1,0:T(8,128)(2,1)S(1)}, bf16[256,1024]{1,0:T(8,128)(2,1)}, u32[]{:S(2)}) copy-start(bf16[256,1024]{1,0:T(8,128)(2,1)} %param.10) | copy-start | bytes 1572868
  6.5 197.4 %all-reduce.5.cloned.1.call-start = ((), (), s32[]{:S(2)}) async-start(), calls=%async_computation | async-start | bytes 270336 | tf_op jit(solution)/shard_map/psum | solution.py:92
  129.5 0.7 copy-start.6
  131.2 0.7 copy-start.3
  131.2 869.1 %all-reduce.7.cloned.1.call-start = ((), (), s32[]{:S(2)}) async-start(), calls=%async_computation.1 | async-start | bytes 1048576
  145.6 0.7 copy-start.8
  146.3 0.7 copy-start.7
  147.1 0.7 copy-start.9
  218.4 0.9 copy-start.2
  218.5 0.7 copy-start.4
  478.0 540.8 %copy-start.5 = (f32[1024]{0:T(1024)S(1)}, f32[1024]{0:T(1024)}, u32[]{:S(2)}) copy-start(f32[1024]{0:T(1024)} %param.8) | copy-start | bytes 12292
Sparse Core Ops, SparseCore 0:
  131.4 72.4 all-reduce.4
  494.0 506.3 all-reduce.6
where the time goes:
time: 1050 us
  waiting for transfers between devices  561 us (53%)
  blocking collectives  414 us (39%)
  local copies, waits for them, and re-layouts  33.2 us (3%)
  other arithmetic  22.5 us (2%)
  between operations  14.3 us (1%)
    unnamed x3, waiting for transfers between devices  504 us
    psum x1, blocking collectives, coefficients(): lax.psum(jnp.sum(jnp.exp(positive_energies - shifted), 1) + jnp.sum(jnp.e...  129 us
    pmax x1, blocking collectives, coefficients(): row_top = lax.pmax(local_top, 'dp')  129 us
    all_gather x1, blocking collectives, shards(): lax.all_gather(query_half, 'dp', axis=0, tiled=True)  81.6 us
    psum x1, waiting for transfers between devices, shards(): summed, queue_square = lax.psum((partial_value, queue_square), 'pipe')  56.1 us
    psum x1, blocking collectives, shards(): mean_square = lax.psum(squares, 'pipe') / full_width  21.9 us
  transfers between devices with their start and end apart: 2, of which 2 were waited for; matrix products, arithmetic and copies ran while one was open for 1% of the time, Pallas kernels for 0%

commit v1 on v0

v1 whole, which is shorter than its diff:
```python
import functools

import jax
import jax.numpy as jnp
from jax import lax
from jax.experimental import pallas as pl
from jax.experimental.pallas import tpu as pltpu
from jax.sharding import Mesh, PartitionSpec as P

NORM_EPS = 1e-05
MIX_EPS = 1e-06
INV_TEMP = 20.0
LOSS_SCALE = 2048.0
WIDTH = 8192
PART = 1024
CHUNKS = 8
SEQ = 64
TOKENS = 128
QUERIES = 128
ROWS = 256
BANK = 264
SLOTS = 16
EXT = 1152
PIPE = ("y", "xl")
VMEM = 24 << 20

f32 = jnp.float32
bf16 = jnp.bfloat16


def dot_t(a, b):
    return lax.dot_general(a, b, (((1,), (1,)), ((), ())), preferred_element_type=f32)


def split(a):
    hi = a.astype(bf16)
    return hi, (a - hi.astype(f32)).astype(bf16)


def iota(shape, dim):
    return lax.broadcasted_iota(jnp.int32, shape, dim)


def diagonal(square):
    n = square.shape[0]
    on = iota((n, n), 0) == iota((n, n), 1)
    return jnp.sum(jnp.where(on, square, 0.0), axis=0, keepdims=True)


def column(row):
    on = iota((128, 128), 0) == iota((128, 128), 1)
    return jnp.sum(jnp.where(on, row, 0.0), axis=1, keepdims=True)


def fold(row):
    return jnp.concatenate([row[:, c * 128:(c + 1) * 128] for c in range(CHUNKS)], axis=0)


def unfold(block):
    return jnp.concatenate([block[c:c + 1] for c in range(CHUNKS)], axis=1)


def call(kernel, outs, *args, smem=(), scratch=()):
    specs = [
        pl.BlockSpec(memory_space=pltpu.SMEM if i in smem else pltpu.VMEM) for i in range(len(args))
    ]
    many = isinstance(outs, (list, tuple))
    out_specs = [pl.BlockSpec(memory_space=pltpu.VMEM)] * len(outs) if many else pl.BlockSpec(memory_space=pltpu.VMEM)
    return pl.pallas_call(
        kernel,
        out_shape=outs,
        in_specs=specs,
        out_specs=out_specs,
        scratch_shapes=scratch,
        compiler_params=pltpu.CompilerParams(vmem_limit_bytes=VMEM),
    )(*args)


def squares_kernel(hidden_ref, queue_ref, gain_ref, out_ref):
    x = hidden_ref[...]
    weighted = x.astype(f32) * (gain_ref[...] * gain_ref[...])
    hi, lo = split(weighted)
    gram = dot_t(x, hi) + dot_t(x, lo)
    packed = jnp.where(iota((SEQ, 128), 1) < SEQ, gram[:SEQ], gram[SEQ:])
    token = diagonal(dot_t(x, x))
    low = queue_ref[:128]
    high = queue_ref[128:]
    first = diagonal(dot_t(low, low))
    second = diagonal(dot_t(high, high))
    row = iota((8, 128), 0)
    sums = jnp.where(row == 0, token, jnp.where(row == 1, first, jnp.where(row == 2, second, 0.0)))
    for peer in range(8):
        out_ref[peer, :SEQ] = packed
        out_ref[peer, SEQ:] = sums


def query_kernel(sums_ref, hidden_ref, gain_ref, keys_ref, payload_ref, query_ref, stat_ref):
    total = sums_ref[0]
    for peer in range(1, 8):
        total = total + sums_ref[peer]
    token = total[SEQ:SEQ + 1]
    inverse = lax.rsqrt(token / WIDTH + NORM_EPS)
    inverse_column = column(inverse)
    lane = iota((SEQ, 128), 1)
    pair = jnp.where(lane < SEQ, inverse_column[:SEQ], inverse_column[SEQ:]) * inverse
    square = jnp.sum(pair * total[:SEQ], axis=0, keepdims=True)
    first = iota((1, 128), 1) < SEQ
    lengths = [
        jnp.sqrt(jnp.sum(jnp.where(first, square, 0.0), axis=1, keepdims=True)) / SEQ,
        jnp.sqrt(jnp.sum(jnp.where(first, 0.0, square), axis=1, keepdims=True)) / SEQ,
    ]
    weighted = hidden_ref[...].astype(f32) * inverse_column
    gain = gain_ref[...]
    blocks = []
    for q in range(2):
        pooled = jnp.sum(weighted[q * SEQ:(q + 1) * SEQ], axis=0, keepdims=True) * gain / SEQ
        query = pooled / lengths[q]
        query_ref[q:q + 1] = query
        blocks.append(fold(query))
    half = jnp.concatenate(blocks, axis=0).astype(bf16)
    for z in range(16):
        payload_ref[z, :16] = half
        payload_ref[z, 16:] = keys_ref[...]
    length_row = jnp.where(first, lengths[0], lengths[1])
    row = iota((8, 128), 0)
    stat_ref[...] = jnp.where(
        row == 0,
        inverse,
        jnp.where(
            row == 1, total[SEQ + 1:SEQ + 2], jnp.where(row == 2, total[SEQ + 2:SEQ + 3], length_row)
        ),
    )


def score_kernel(gathered_ref, queue_ref, keys_ref, out_ref, rows_ref):
    rows_ref[...] = gathered_ref[:, :16, :].astype(f32).reshape(QUERIES * CHUNKS, 128)
    queries = jnp.concatenate(
        [rows_ref[pl.ds(c, QUERIES, stride=CHUNKS), :].astype(bf16) for c in range(CHUNKS)], axis=1
    )
    queue_dots = dot_t(queue_ref[...], queries)
    key_dots = dot_t(keys_ref[...], queries)[:8]
    for peer in range(8):
        out_ref[peer, :ROWS] = queue_dots
        out_ref[peer, ROWS:] = key_dots


def grad_kernel(dots_ref, stat_ref, queue_ref, keys_ref, pick_ref, weight_ref, target_ref, out_ref):
    dots = dots_ref[0]
    for peer in range(1, 8):
        dots = dots + dots_ref[peer]
    queue_dots = dots[:ROWS]
    key_dots = dots[ROWS:]
    square = jnp.concatenate([column(stat_ref[1:2]), column(stat_ref[2:3])], axis=0)
    index = iota((ROWS, 128), 0)
    pick = pick_ref[...]
    cosines, squares = [], []
    for h in range(SLOTS):
        on = index == pick[h:h + 1]
        cosines.append(jnp.sum(jnp.where(on, queue_dots, 0.0), axis=0, keepdims=True))
        squares.append(jnp.sum(jnp.where(on, square, 0.0), axis=0, keepdims=True))
    cosine = jnp.concatenate(cosines, axis=0)
    picked = jnp.concatenate(squares, axis=0)
    present = (pick >= 0) & (pick < ROWS)
    beta = weight_ref[...]
    rest = 1.0 - beta
    numer = beta + rest * cosine
    radius_sq = beta * beta + rest * rest * picked + 2.0 * beta * rest * cosine + MIX_EPS
    radius_sq = jnp.where(present, radius_sq, 1.0)
    radius = jnp.sqrt(radius_sq)
    mixed = numer * INV_TEMP / radius
    slope = (rest - numer * beta * rest / radius_sq) * INV_TEMP / radius
    low = -1e30
    mixed = jnp.where(present, mixed, low)
    queue_scores = queue_dots * INV_TEMP
    key_row = iota((8, 128), 0)
    key_scores = jnp.where(key_row < 2, key_dots * INV_TEMP, low)
    top = jnp.maximum(
        jnp.maximum(
            jnp.max(queue_scores, axis=0, keepdims=True), jnp.max(key_scores, axis=0, keepdims=True)
        ),
        jnp.max(mixed, axis=0, keepdims=True),
    )
    queue_exp = jnp.exp(queue_scores - top)
    key_exp = jnp.where(key_row < 2, jnp.exp(key_scores - top), 0.0)
    own = key_row == target_ref[...]
    positive = jnp.sum(jnp.where(own, key_exp, 0.0), axis=0, keepdims=True)
    key_exp = jnp.where(own, 0.0, key_exp)
    mixed_exp = jnp.where(present, jnp.exp(mixed - top), 0.0)
    mass = (
        jnp.sum(queue_exp, axis=0, keepdims=True)
        + jnp.sum(key_exp, axis=0, keepdims=True)
        + jnp.sum(mixed_exp, axis=0, keepdims=True)
    )
    extra = jnp.where(present, mixed_exp * slope, 0.0)
    coef = queue_exp * INV_TEMP
    for h in range(SLOTS):
        coef = coef + jnp.where(index == pick[h:h + 1], extra[h:h + 1], 0.0)
    key_coef = jnp.concatenate([key_exp * INV_TEMP, jnp.zeros((8, 128), f32)], axis=0)
    hi, lo = split(jnp.transpose(coef))
    key_hi, key_lo = split(jnp.transpose(jnp.concatenate([key_coef, jnp.zeros((112, 128), f32)], axis=0)))
    bank = queue_ref[...]
    keys = keys_ref[...]
    product = functools.partial(jnp.dot, preferred_element_type=f32)
    out_ref[:, :PART] = (
        product(hi, bank) + product(lo, bank)
        + (product(key_hi[:, :16], keys) + product(key_lo[:, :16], keys))
    )
    lane = iota((128, 128), 1)
    out_ref[:, PART:] = jnp.where(
        lane == 0, column(top), jnp.where(lane == 1, column(mass), jnp.where(lane == 2, column(positive), 0.0))
    )


def merge_kernel(core_ref, pair_ref, out_ref):
    start = pl.multiple_of(core_ref[0] * 64, 64)
    one = pair_ref[0, pl.ds(start, 64), :]
    two = pair_ref[1, pl.ds(start, 64), :]
    top_one = one[:, PART:PART + 1]
    top_two = two[:, PART:PART + 1]
    top = jnp.maximum(top_one, top_two)
    merged = one * jnp.exp(top_one - top) + two * jnp.exp(top_two - top)
    lane = iota((64, EXT), 1)
    merged = jnp.where(lane == PART, top, merged)
    for peer in range(32):
        out_ref[peer] = merged[2 * peer:2 * peer + 2]


def inner_kernel(place_ref, parts_ref, query_ref, gathered_ref, hidden_ref, gain_ref, out_ref, grad_ref):
    stats = parts_ref[:, :, PART:]
    tops = stats[:, :, 0:1]
    top = jnp.max(tops, axis=0, keepdims=True)
    scale = jnp.exp(tops - top)
    total = jnp.sum(parts_ref[...] * scale, axis=0)
    others = total[:, PART + 1:PART + 2]
    full = others + total[:, PART + 2:PART + 3]
    share = others / full
    sums = total[:, :PART] / full
    keys = []
    for q in range(2):
        block = gathered_ref[place_ref[2 * q]].astype(f32)
        keys.append(unfold(jnp.where(place_ref[2 * q + 1] == 0, block[16:24], block[24:32])))
    key = jnp.concatenate(keys, axis=0)
    grad = LOSS_SCALE * (sums - key * (share * INV_TEMP))
    grad_ref[...] = grad
    query = query_ref[...]
    gain = gain_ref[...]
    along = jnp.sum(query * grad, axis=1, keepdims=True)
    rows = jnp.concatenate([grad * gain, query * gain, jnp.zeros((4, PART), f32)], axis=0)
    hi = rows.astype(bf16)
    rest = rows - hi.astype(f32)
    mid = rest.astype(bf16)
    low = (rest - mid.astype(f32)).astype(bf16)
    x = hidden_ref[...]
    dots = dot_t(hi, x) + (dot_t(mid, x) + dot_t(low, x))
    first = iota((1, 128), 1) < SEQ
    of_grad = jnp.where(first, dots[0:1], dots[1:2])
    of_query = jnp.where(first, dots[2:3], dots[3:4])
    of_along = jnp.where(first, along[0:1], along[1:2])
    row = iota((8, 128), 0)
    block = jnp.where(row == 0, of_grad, jnp.where(row == 1, of_query, of_along))
    for peer in range(8):
        out_ref[peer] = block


def output_kernel(sums_ref, grad_ref, query_ref, stat_ref, hidden_ref, gain_ref, out_ref):
    total = sums_ref[0]
    for peer in range(1, 8):
        total = total + sums_ref[peer]
    inverse = stat_ref[0:1]
    length = stat_ref[3:4]
    along = total[2:3]
    inner = inverse * (total[0:1] - along * total[1:2]) / (length * WIDTH)
    inverse_column = column(inverse)
    slide = column(inverse * inverse * inner) / SEQ
    gain = gain_ref[...]
    for q in range(2):
        at = q * SEQ
        scaled = (
            gain * (grad_ref[q:q + 1] - along[:, at:at + 1] * query_ref[q:q + 1])
            / (length[:, at:at + 1] * SEQ)
        )
        out_ref[at:at + SEQ] = (
            inverse_column[at:at + SEQ] * scaled
            - hidden_ref[at:at + SEQ].astype(f32) * slide[at:at + SEQ]
        )


def shape(dims, kind=f32):
    return jax.ShapeDtypeStruct(dims, kind)


def by_device(array):
    rest = array.shape[1:]
    cut = array.reshape((2, 16, 2, 2) + rest)
    order = (2, 0, 1, 3) + tuple(range(4, cut.ndim))
    return cut.transpose(order).reshape((QUERIES,) + rest)


def shards(hidden, gain, keys, queue, positive, mix_rows, mix_weight):
    xh, z, core = lax.axis_index("xh"), lax.axis_index("z"), lax.axis_index("c")
    shard = (xh * 16 + z) * 2 + core
    tokens = hidden.reshape(TOKENS, PART)
    gain = gain.reshape(1, PART)
    pick = by_device(mix_rows).T - shard * ROWS
    weight = by_device(mix_weight).T
    target = by_device(positive).reshape(1, QUERIES) - shard * 2
    mine = lax.dynamic_slice(positive, (shard * 2,), (2,))
    source = mine // 2
    slot = (source % 2) * 32 + source // 2
    place = jnp.stack([slot, mine % 2], axis=1).reshape(4)
    keys_folded = keys.reshape(16, 128)
    keys_padded = jnp.pad(keys, ((0, 14), (0, 0)))

    squares = call(squares_kernel, shape((8, 72, 128)), tokens, queue, gain)
    squares = lax.all_to_all(squares, PIPE, 0, 0)
    payload, query, stat = call(
        query_kernel,
        [shape((16, 32, 128), bf16), shape((2, PART)), shape((8, 128))],
        squares, tokens, gain, keys_folded,
    )
    payload = lax.all_to_all(payload, "z", 0, 0)
    payload = lax.all_gather(payload, "xh")
    gathered = lax.all_gather(payload, "c").reshape(64, 32, 128)
    dots = call(
        score_kernel, shape((8, BANK, 128)), gathered, queue, keys_padded,
        scratch=[pltpu.VMEM((QUERIES * CHUNKS, 128), f32)],
    )
    dots = lax.all_to_all(dots, PIPE, 0, 0)
    parts = call(
        grad_kernel, shape((QUERIES, EXT)), dots, stat, queue, keys_padded, pick, weight, target
    )
    pair = lax.all_gather(parts, "c")
    parts = call(merge_kernel, shape((32, 2, EXT)), core.reshape(1).astype(jnp.int32), pair, smem=(0,))
    parts = lax.all_to_all(parts, ("xh", "z"), 0, 0)
    sums, grad = call(
        inner_kernel,
        [shape((8, 8, 128)), shape((2, PART))],
        place.astype(jnp.int32), parts, query, gathered, tokens, gain, smem=(0,),
    )
    sums = lax.all_to_all(sums, PIPE, 0, 0)
    out = call(output_kernel, shape((TOKENS, PART)), sums, grad, query, stat, tokens, gain)
    return out.reshape(2, SEQ, PART)


def solution(mesh):
    fine = Mesh(mesh.devices.reshape(2, 16, 2, 4, 2), ("xh", "z", "c", "y", "xl"))
    dp = ("xh", "z", "c")
    placed = (P(dp, None, PIPE), P(PIPE), P(dp, PIPE), P(dp, PIPE), P(), P(), P())
    return jax.shard_map(
        shards, mesh=fine, in_specs=placed, out_specs=P(dp, None, PIPE), check_vma=False
    )
```

time: 1050 us -> 159 us (0.15)
  the two profiles are of different devices: /device:TPU:2 before, /device:TPU:32 now
where the time goes in v1:
time: 159 us; the launch traced here: 158 us
  waiting for transfers between devices  71.2 us (45%)
  starting transfers between devices  39.6 us (25%)
  blocking collectives  19.7 us (12%)
  between operations  13.5 us (8%)
  Pallas kernels  8.93 us (6%)
  local copies, waits for them, and re-layouts  4.83 us (3%)
    all_to_all x1, waiting for transfers between devices, shards(): parts = lax.all_to_all(parts, ('xh', 'z'), 0, 0)  24.1 us
    all_to_all x1, waiting for transfers between devices, shards(): dots = lax.all_to_all(dots, PIPE, 0, 0)  15.8 us
    all_to_all x1, starting transfers between devices, shards(): parts = lax.all_to_all(parts, ('xh', 'z'), 0, 0)  15.2 us
    all_to_all x1, starting transfers between devices, shards(): payload = lax.all_to_all(payload, 'z', 0, 0)  15.2 us
    all_to_all x1, waiting for transfers between devices, shards(): payload = lax.all_to_all(payload, 'z', 0, 0)  12.5 us
    all_gather x1, waiting for transfers between devices, shards(): pair = lax.all_gather(parts, 'c')  11.2 us
    all_to_all x1, blocking collectives, shards(): sums = lax.all_to_all(sums, PIPE, 0, 0)  10.4 us
    pallas_call x7, Pallas kernels, call(): pl.pallas_call(kernel, out_shape=outs, in_specs=specs, out_specs=out_spec...  8.93 us
  transfers between devices with their start and end apart: 5, of which 5 were waited for; matrix products, arithmetic and copies ran while one was open for 1% of the time, Pallas kernels for 0%

profile of v1, /device:TPU:32, one launch (start us, length us, event | category | flops | bytes accessed | tf_op | source)
XLA Modules:
  0.0 157.9 jit_solution(17012279975857004549)
XLA Ops:
  6.5 0.0 copy-start
  6.5 1.0 copy-done
  7.6 0.0 copy-start.2
  7.6 0.9 copy-done.2
  8.5 0.0 copy-start.5
  8.5 0.7 copy-done.5
  9.2 0.0 copy-start.7
  9.2 0.0 copy-start.3
  9.2 0.0 copy-start.6
  9.2 1.3 shard_map.73
  10.5 5.4 %all-to-all-start = ((f32[8,72,128]{2,1,0:T(8,128)}), f32[8,72,128]{2,1,0:T(8,128)S(1)}, u32[]{:S(2)}, u32[]{:S(2)}) async-start(f32[8,72,128]{2,1,0:T(8,128)} %shard_map.73), calls=%async_computation | async-start | bytes 589824 | tf_op jit(solution)/shard_map/all_to_all | solution.py:315
  15.9 0.0 copy-done.7
  15.9 0.0 copy-start.1
  15.9 7.6 %all-to-all-done.sums_ref = f32[8,72,128]{2,1,0:T(8,128)S(1)} async-done(((f32[8,72,128]{2,1,0:T(8,128)}), f32[8,72,128]{2,1,0:T(8,128)S(1)}, u32[]{:S(2)}, u32[]{:S(2)}) %all-to-all-start) | async-done | bytes 294944 | tf_op jit(solution)/shard_map/all_to_all | solution.py:315
  23.5 0.0 copy-done.3
  23.5 0.0 copy-done.6
  23.5 0.9 shard_map.74
  24.4 15.2 %all-to-all-start.1 = ((bf16[16,32,128]{2,1,0:T(8,128)(2,1)}), bf16[16,32,128]{2,1,0:T(8,128)(2,1)S(1)}, u32[]{:S(2)}, u32[]{:S(2)}) async-start(bf16[16,32,128]{2,1,0:T(8,128)(2,1)} %get-tuple-element.10), calls=%async_computation.1 | async-start | bytes 262144 | tf_op jit(solution)/shard_map/all_to_all | solution.py:321
  39.6 12.5 %all-to-all-done.1 = bf16[16,32,128]{2,1,0:T(8,128)(2,1)S(1)} async-done(((bf16[16,32,128]{2,1,0:T(8,128)(2,1)}), bf16[16,32,128]{2,1,0:T(8,128)(2,1)S(1)}, u32[]{:S(2)}, u32[]{:S(2)}) %all-to-all-start.1) | async-done | bytes 131104 | tf_op jit(solution)/shard_map/all_to_all | solution.py:321
  52.1 7.1 %all-gather = bf16[32,32,128]{2,1,0:T(8,128)(2,1)S(1)} all-gather(bf16[16,32,128]{2,1,0:T(8,128)(2,1)S(1)} %all-to-all-done.1), channel_id=2, replica_groups=mesh['xh'=2,'z'=16,'c'=2,'y'=4,'xl'=2] {'xh'}, dimensions={0}, use_global_device_ids=true | all-gather | bytes 393216 | tf_op jit(solution)/shard_map/all_gather | solution.py:322
  59.2 2.2 %all-gather.1 = bf16[4,16,32,128]{3,2,1,0:T(8,128)(2,1)S(1)} all-gather(bf16[2,16,32,128]{3,2,1,0:T(8,128)(2,1)S(1)} %bitcast.37), channel_id=3, replica_groups=mesh['xh'=2,'z'=16,'c'=2,'y'=4,'xl'=2] {'c'}, dimensions={0}, use_global_device_ids=true | all-gather | bytes 786432 | tf_op jit(solution)/shard_map/all_gather | solution.py:323
  61.4 0.0 copy-done.1
  61.4 1.4 shard_map.75
  62.8 3.7 %all-to-all-start.2 = ((f32[8,264,128]{2,1,0:T(8,128)}), f32[8,264,128]{2,1,0:T(8,128)S(1)}, u32[]{:S(2)}, u32[]{:S(2)}) async-start(f32[8,264,128]{2,1,0:T(8,128)} %shard_map.75), calls=%async_computation.2 | async-start | bytes 2162688 | tf_op jit(solution)/shard_map/all_to_all | solution.py:328
  66.5 0.0 all-gather.5.cloned.1.call-start
  66.6 0.0 copy-done.10
  66.6 0.2 sub.43
  66.8 0.1 sub.45.target_ref
  66.9 0.0 copy-done.8
  67.0 0.1 copy.21
  67.1 0.1 copy.23
  67.2 0.0 copy-done.9
  67.2 0.1 copy.24
  67.3 0.1 copy.26
  67.4 15.8 %all-to-all-done.2.dots_ref = f32[8,264,128]{2,1,0:T(8,128)S(1)} async-done(((f32[8,264,128]{2,1,0:T(8,128)}), f32[8,264,128]{2,1,0:T(8,128)S(1)}, u32[]{:S(2)}, u32[]{:S(2)}) %all-to-all-start.2) | async-done | bytes 1081376 | tf_op jit(solution)/shard_map/all_to_all | solution.py:328
  83.2 2.3 %shard_map.76 = f32[128,1152]{1,0:T(8,128)} custom-call(f32[8,264,128]{2,1,0:T(8,128)S(1)} %all-to-all-done.2.dots_ref, f32[8,128]{1,0:T(8,128)S(1)} %get-tuple-element.11.stat_ref, bf16[256,1024]{1,0:T(8,128)(2,1)S(1)} %copy-done.1, bf16[16,1024]{1,0:T(8,128)(2,1)S(1)} %pad.4.keys_ref, s32[16,128]{1,0:T(8,128)S(1)} %bitcast.35, f32[16,128]{1,0:T(8,128)S(1)} %bitcast.36, ...), custom_call_target="tpu_custom_call" | custom-call | tf_op jit(solution)/shard_map/pallas_call | solution.py:69
  85.5 0.0 all-gather.5.cloned.1.call-update
  85.5 11.2 %all-gather.5.cloned.1.call-done = f32[256,1152]{1,0:T(8,128)} async-done(((f32[128,1152]{1,0:T(8,128)}), f32[256,1152]{1,0:T(8,128)}) %all-gather.5.cloned.1.call-update) | async-done | bytes 1179664 | tf_op jit(solution)/shard_map/all_gather | solution.py:332
  96.7 1.3 copy-done.4
  98.0 0.9 shard_map.77
  98.8 15.2 %all-to-all-start.3 = ((f32[32,2,1152]{2,1,0:T(2,128)}), f32[32,2,1152]{2,1,0:T(2,128)S(1)}, u32[]{:S(2)}, u32[]{:S(2)}) async-start(f32[32,2,1152]{2,1,0:T(2,128)} %shard_map.77), calls=%async_computation.3 | async-start | bytes 589824 | tf_op jit(solution)/shard_map/all_to_all | solution.py:334
  114.1 0.1 fusion.3
  114.2 0.1 copy.20
  114.3 0.1 reshape.50.place_ref
  114.4 24.1 %all-to-all-done.3.parts_ref = f32[32,2,1152]{2,1,0:T(2,128)S(1)} async-done(((f32[32,2,1152]{2,1,0:T(2,128)}), f32[32,2,1152]{2,1,0:T(2,128)S(1)}, u32[]{:S(2)}, u32[]{:S(2)}) %all-to-all-start.3) | async-done | bytes 294944 | tf_op jit(solution)/shard_map/all_to_all | solution.py:334
  138.5 1.2 shard_map.78
  139.6 10.4 %all_to_all.25.sums_ref = f32[8,8,128]{2,1,0:T(8,128)S(1)} all-to-all(f32[8,8,128]{2,1,0:T(8,128)S(1)} %get-tuple-element.13), channel_id=1, replica_groups=mesh['xh'=2,'z'=16,'c'=2,'y'=4,'xl'=2] {'y','xl'}, dimensions={0} | all-to-all | bytes 65536 | tf_op jit(solution)/shard_map/all_to_all | solution.py:340
  150.0 1.0 shard_map.79
  (13 shorter events, 0.1 us)
Async XLA Ops:
  6.5 1.0 copy-start
  7.6 0.9 copy-start.2
  8.5 0.7 copy-start.5
  9.2 6.7 %copy-start.7 = (bf16[2,1024]{1,0:T(2,128)(2,1)S(1)}, bf16[2,1024]{1,0:T(2,128)(2,1)}, u32[]{:S(2)}) copy-start(bf16[2,1024]{1,0:T(2,128)(2,1)} %param.9) | copy-start | bytes 12292
  9.2 14.3 %copy-start.3 = (bf16[2,64,1024]{2,1,0:T(8,128)(2,1)S(1)}, bf16[2,64,1024]{2,1,0:T(8,128)(2,1)}, u32[]{:S(2)}) copy-start(bf16[2,64,1024]{2,1,0:T(8,128)(2,1)} %param.7) | copy-start | bytes 786436
  9.2 14.3 %copy-start.6 = (f32[1024]{0:T(1024)S(1)}, f32[1024]{0:T(1024)}, u32[]{:S(2)}) copy-start(f32[1024]{0:T(1024)} %param.8) | copy-start | bytes 12292
  10.5 13.0 %all-to-all-start = ((f32[8,72,128]{2,1,0:T(8,128)}), f32[8,72,128]{2,1,0:T(8,128)S(1)}, u32[]{:S(2)}, u32[]{:S(2)}) async-start(f32[8,72,128]{2,1,0:T(8,128)} %shard_map.73), calls=%async_computation | async-start | bytes 589824 | tf_op jit(solution)/shard_map/all_to_all | solution.py:315
  15.9 45.5 %copy-start.1 = (bf16[256,1024]{1,0:T(8,128)(2,1)S(1)}, bf16[256,1024]{1,0:T(8,128)(2,1)}, u32[]{:S(2)}) copy-start(bf16[256,1024]{1,0:T(8,128)(2,1)} %queue_ref.5) | copy-start | bytes 1572868
  24.4 27.7 %all-to-all-start.1 = ((bf16[16,32,128]{2,1,0:T(8,128)(2,1)}), bf16[16,32,128]{2,1,0:T(8,128)(2,1)S(1)}, u32[]{:S(2)}, u32[]{:S(2)}) async-start(bf16[16,32,128]{2,1,0:T(8,128)(2,1)} %get-tuple-element.10), calls=%async_computation.1 | async-start | bytes 262144 | tf_op jit(solution)/shard_map/all_to_all | solution.py:321
  62.8 3.8 %copy-start.10 = (s32[128]{0:T(128)S(1)}, s32[128]{0:T(128)}, u32[]{:S(2)}) copy-start(s32[128]{0:T(128)} %param.11) | copy-start | bytes 1540
  62.8 4.1 %copy-start.8 = (s32[128,16]{0,1:T(8,128)S(1)}, s32[128,16]{0,1:T(8,128)}, u32[]{:S(2)}) copy-start(s32[128,16]{0,1:T(8,128)} %param.12) | copy-start | bytes 24580
  62.8 4.3 %copy-start.9 = (f32[128,16]{0,1:T(8,128)S(1)}, f32[128,16]{0,1:T(8,128)}, u32[]{:S(2)}) copy-start(f32[128,16]{0,1:T(8,128)} %param.13) | copy-start | bytes 24580
  62.8 20.3 %all-to-all-start.2 = ((f32[8,264,128]{2,1,0:T(8,128)}), f32[8,264,128]{2,1,0:T(8,128)S(1)}, u32[]{:S(2)}, u32[]{:S(2)}) async-start(f32[8,264,128]{2,1,0:T(8,128)} %shard_map.75), calls=%async_computation.2 | async-start | bytes 2162688 | tf_op jit(solution)/shard_map/all_to_all | solution.py:328
  66.5 30.2 %all-gather.5.cloned.1.call-start = ((), (), s32[]{:S(2)}) async-start(), calls=%async_computation.5 | async-start | bytes 1769472 | tf_op jit(solution)/shard_map/all_gather | solution.py:332
  96.7 1.3 copy-start.4
  98.8 39.6 %all-to-all-start.3 = ((f32[32,2,1152]{2,1,0:T(2,128)}), f32[32,2,1152]{2,1,0:T(2,128)S(1)}, u32[]{:S(2)}, u32[]{:S(2)}) async-start(f32[32,2,1152]{2,1,0:T(2,128)} %shard_map.77), calls=%async_computation.3 | async-start | bytes 589824 | tf_op jit(solution)/shard_map/all_to_all | solution.py:334
Sparse Core Ops, SparseCore 0:
  85.6 11.0 all-gather.4

commit v2 on v1

v2 whole, which is shorter than its diff:
```python
import functools

import jax
import jax.numpy as jnp
from jax import lax
from jax.experimental import pallas as pl
from jax.experimental.pallas import tpu as pltpu
from jax.sharding import Mesh, PartitionSpec as P

NORM_EPS = 1e-05
MIX_EPS = 1e-06
INV_TEMP = 20.0
LOSS_SCALE = 2048.0
WIDTH = 8192
PART = 1024
CHUNKS = 8
SEQ = 64
TOKENS = 128
QUERIES = 128
ROWS = 256
BANK = 264
SLOTS = 16
EXT = 1152
ABSENT = -30000.0
FINE = 65536.0
FULL = 32000.0
PIPE = ("y", "xl")
VMEM = 24 << 20

f32 = jnp.float32
bf16 = jnp.bfloat16


def dot_t(a, b):
    return lax.dot_general(a, b, (((1,), (1,)), ((), ())), preferred_element_type=f32)


def split(a):
    hi = a.astype(bf16)
    return hi, (a - hi.astype(f32)).astype(bf16)


def iota(shape, dim):
    return lax.broadcasted_iota(jnp.int32, shape, dim)


def padded(keys):
    return jnp.concatenate([keys.astype(f32), jnp.zeros((14, PART), f32)], axis=0).astype(bf16)


def reordered(rows):
    old, new = iota((128, 128), 0), iota((128, 128), 1)
    place = (new % 64) // 2 * 4 + new // 64 * 2 + new % 2
    chosen = jnp.where(old == place, 1.0, 0.0).astype(bf16)
    hi = rows.astype(bf16)
    rest = rows - hi.astype(f32)
    mid = rest.astype(bf16)
    low = (rest - mid.astype(f32)).astype(bf16)
    product = functools.partial(jnp.dot, preferred_element_type=f32)
    return product(hi, chosen) + (product(mid, chosen) + product(low, chosen))


def whole(a):
    return jnp.floor(a + 0.5).astype(jnp.int32)


def diagonal(square):
    n = square.shape[0]
    on = iota((n, n), 0) == iota((n, n), 1)
    return jnp.sum(jnp.where(on, square, 0.0), axis=0, keepdims=True)


def column(row):
    on = iota((128, 128), 0) == iota((128, 128), 1)
    return jnp.sum(jnp.where(on, row, 0.0), axis=1, keepdims=True)


def fold(row):
    return jnp.concatenate([row[:, c * 128:(c + 1) * 128] for c in range(CHUNKS)], axis=0)


def unfold(block):
    return jnp.concatenate([block[c:c + 1] for c in range(CHUNKS)], axis=1)


def call(kernel, outs, *args, smem=(), far=(), scratch=()):
    def space(i):
        return pltpu.SMEM if i in smem else pltpu.HBM if i in far else pltpu.VMEM

    specs = [pl.BlockSpec(memory_space=space(i)) for i in range(len(args))]
    many = isinstance(outs, (list, tuple))
    out_specs = [pl.BlockSpec(memory_space=pltpu.VMEM)] * len(outs) if many else pl.BlockSpec(memory_space=pltpu.VMEM)
    return pl.pallas_call(
        kernel,
        out_shape=outs,
        in_specs=specs,
        out_specs=out_specs,
        scratch_shapes=scratch,
        compiler_params=pltpu.CompilerParams(vmem_limit_bytes=VMEM),
    )(*args)


def squares_kernel(ids_ref, hidden_far, queue_far, gain_far, out_ref, hidden_ref, queue_ref, gain_ref, sems):
    copies = [
        pltpu.make_async_copy(gain_far, gain_ref, sems.at[0]),
        pltpu.make_async_copy(hidden_far, hidden_ref, sems.at[1]),
        pltpu.make_async_copy(queue_far, queue_ref, sems.at[2]),
    ]
    for copy in copies:
        copy.start()
    copies[0].wait()
    copies[1].wait()
    x = hidden_ref[...]
    weighted = x.astype(f32) * (gain_ref[...] * gain_ref[...])
    hi, lo = split(weighted)
    gram = dot_t(x, hi) + dot_t(x, lo)
    up = iota((SEQ, 128), 0) < iota((SEQ, 128), 1)
    both = jnp.where(up, gram[:SEQ], pltpu.roll(gram[SEQ:], SEQ, 1))
    left = iota((32, 128), 1) < SEQ
    packed = jnp.where(left, both[:32], pltpu.roll(both[32:], SEQ, 1))
    token = diagonal(dot_t(x, x))
    diag = diagonal(gram)
    copies[2].wait()
    low = queue_ref[:128]
    high = queue_ref[128:]
    first = diagonal(dot_t(low, low))
    second = diagonal(dot_t(high, high))
    row = iota((8, 128), 0)
    sums = jnp.where(
        row == 0,
        token,
        jnp.where(row == 1, first, jnp.where(row == 2, second, jnp.where(row == 3, diag, 0.0))),
    )
    for peer in range(8):
        out_ref[peer, :32] = packed
        out_ref[peer, 32:] = sums


def query_kernel(sums_ref, hidden_ref, gain_ref, keys_ref, payload_ref, query_ref, stat_ref):
    total = sums_ref[0]
    for peer in range(1, 8):
        total = total + sums_ref[peer]
    token = total[32:33]
    diag = total[35:36]
    inverse = lax.rsqrt(token / WIDTH + NORM_EPS)
    inverse_column = column(inverse)
    first = iota((1, 128), 1) < SEQ
    both = jnp.concatenate([total[:32], pltpu.roll(total[:32], SEQ, 1)], axis=0)
    t, u = iota((SEQ, 128), 0), iota((SEQ, 128), 1)
    second = pltpu.roll(jnp.broadcast_to(inverse, (8, 128)), SEQ, 1)[:1]
    pair = jnp.where(t < u, inverse_column[:SEQ] * inverse, inverse_column[SEQ:] * second)
    pair = jnp.where((t != u) & (u < SEQ), pair * both, 0.0)
    own = diag * inverse * inverse
    lengths = []
    for mask, on in ((first, t < u), (jnp.logical_not(first), t > u)):
        off = jnp.sum(jnp.where(on, pair, 0.0), axis=0, keepdims=True)
        square = jnp.sum(2.0 * off + jnp.where(mask, own, 0.0), axis=1, keepdims=True)
        lengths.append(jnp.sqrt(square) / SEQ)
    weighted = hidden_ref[...].astype(f32) * inverse_column
    gain = gain_ref[...]
    blocks = []
    for q in range(2):
        pooled = jnp.sum(weighted[q * SEQ:(q + 1) * SEQ], axis=0, keepdims=True) * gain / SEQ
        query = pooled / lengths[q]
        query_ref[q:q + 1] = query
        blocks.append(fold(query))
    keys = keys_ref[...].astype(f32)
    blocks += [fold(keys[0:1]), fold(keys[1:2])]
    half = jnp.concatenate(blocks, axis=0).astype(bf16)
    for z in range(16):
        payload_ref[z] = half
    length_row = jnp.where(first, lengths[0], lengths[1])
    row = iota((8, 128), 0)
    stat_ref[...] = jnp.where(
        row == 0,
        inverse,
        jnp.where(row == 1, total[33:34], jnp.where(row == 2, total[34:35], length_row)),
    )


def score_kernel(gathered_ref, queue_ref, keys_ref, out_ref, rows_ref):
    rows_ref[...] = gathered_ref[:, :16, :].astype(f32).reshape(QUERIES * CHUNKS, 128)
    queries = jnp.concatenate(
        [rows_ref[pl.ds(c, QUERIES, stride=CHUNKS), :].astype(bf16) for c in range(CHUNKS)], axis=1
    )
    queue_dots = dot_t(queue_ref[...], queries)
    key_dots = dot_t(padded(keys_ref[...]), queries)[:8]
    for peer in range(8):
        out_ref[peer, :ROWS] = queue_dots
        out_ref[peer, ROWS:] = key_dots


def grad_kernel(
    ids_ref, dots_ref, stat_ref, queue_ref, keys_ref, pick_ref, weight_ref, target_ref, keep_ref, send_ref, all_ref
):
    dots = dots_ref[0]
    for peer in range(1, 8):
        dots = dots + dots_ref[peer]
    queue_dots = dots[:ROWS]
    key_dots = dots[ROWS:]
    square = jnp.concatenate([column(stat_ref[1:2]), column(stat_ref[2:3])], axis=0)
    index = iota((ROWS, 128), 0)
    indices = jnp.concatenate(
        [
            pick_ref[...].astype(f32),
            weight_ref[...],
            jnp.broadcast_to(target_ref[...].astype(f32), (8, 128)),
        ],
        axis=0,
    )
    indices = reordered(indices)
    shard = ids_ref[0]
    pick = whole(indices[:16]) - shard * ROWS
    beta = indices[16:32]
    target = whole(indices[32:33]) - shard * 2
    cosines, squares = [], []
    for h in range(SLOTS):
        on = index == pick[h:h + 1]
        cosines.append(jnp.sum(jnp.where(on, queue_dots, 0.0), axis=0, keepdims=True))
        squares.append(jnp.sum(jnp.where(on, square, 0.0), axis=0, keepdims=True))
    cosine = jnp.concatenate(cosines, axis=0)
    picked = jnp.concatenate(squares, axis=0)
    present = (pick >= 0) & (pick < ROWS)
    rest = 1.0 - beta
    numer = beta + rest * cosine
    radius_sq = beta * beta + rest * rest * picked + 2.0 * beta * rest * cosine + MIX_EPS
    radius_sq = jnp.where(present, radius_sq, 1.0)
    radius = jnp.sqrt(radius_sq)
    mixed = numer * INV_TEMP / radius
    slope = (rest - numer * beta * rest / radius_sq) * INV_TEMP / radius
    low = -1e30
    mixed = jnp.where(present, mixed, low)
    queue_scores = queue_dots * INV_TEMP
    key_row = iota((8, 128), 0)
    own = key_row == target
    held = (target >= 0) & (target < 2)
    positive = jnp.sum(jnp.where(own, key_dots * INV_TEMP, 0.0), axis=0, keepdims=True)
    positive = jnp.where(held, positive, ABSENT)
    other = (key_row < 2) & jnp.logical_not(own)
    key_scores = jnp.where(other, key_dots * INV_TEMP, low)
    top = jnp.maximum(
        jnp.maximum(
            jnp.max(queue_scores, axis=0, keepdims=True), jnp.max(key_scores, axis=0, keepdims=True)
        ),
        jnp.max(mixed, axis=0, keepdims=True),
    )
    queue_exp = jnp.exp(queue_scores - top)
    key_exp = jnp.where(other, jnp.exp(key_scores - top), 0.0)
    mixed_exp = jnp.where(present, jnp.exp(mixed - top), 0.0)
    mass = (
        jnp.sum(queue_exp, axis=0, keepdims=True)
        + jnp.sum(key_exp, axis=0, keepdims=True)
        + jnp.sum(mixed_exp, axis=0, keepdims=True)
    )
    extra = jnp.where(present, mixed_exp * slope, 0.0)
    coef = queue_exp * INV_TEMP
    for h in range(SLOTS):
        coef = coef + jnp.where(index == pick[h:h + 1], extra[h:h + 1], 0.0)
    key_coef = jnp.concatenate([key_exp * INV_TEMP, jnp.zeros((8, 128), f32)], axis=0)
    hi, lo = split(jnp.transpose(coef))
    key_hi, key_lo = split(jnp.transpose(jnp.concatenate([key_coef, jnp.zeros((112, 128), f32)], axis=0)))
    bank = queue_ref[...]
    keys = padded(keys_ref[...])
    product = functools.partial(jnp.dot, preferred_element_type=f32)
    all_ref[:, :PART] = (
        product(hi, bank) + product(lo, bank)
        + (product(key_hi[:, :16], keys) + product(key_lo[:, :16], keys))
    )
    lane = iota((128, 128), 1)
    all_ref[:, PART:] = jnp.where(
        lane == 0, column(top), jnp.where(lane == 1, column(mass), jnp.where(lane == 2, column(positive), 0.0))
    )
    core = ids_ref[1]
    keep_ref[...] = all_ref[pl.ds(pl.multiple_of(core * 64, 64), 64), :]
    send_ref[...] = all_ref[pl.ds(pl.multiple_of((1 - core) * 64, 64), 64), :]


def merge_kernel(keep_ref, came_ref, out_ref):
    one = keep_ref[...]
    two = came_ref[...]
    top_one = one[:, PART:PART + 1]
    top_two = two[:, PART:PART + 1]
    top = jnp.maximum(top_one, top_two)
    up_one = jnp.exp(top_one - top)
    up_two = jnp.exp(top_two - top)
    sums = one[:, :PART] * up_one + two[:, :PART] * up_two
    mass = one[:, PART + 1:PART + 2] * up_one + two[:, PART + 1:PART + 2] * up_two
    positive = jnp.maximum(one[:, PART + 2:PART + 3], two[:, PART + 2:PART + 3])
    most = jnp.maximum(jnp.max(jnp.abs(sums), axis=1, keepdims=True), 1e-30)
    level = jnp.floor(jnp.log(most) * FINE + 0.5) / FINE
    out_ref[:, :PART] = whole(sums * (FULL * jnp.exp(-level))).astype(jnp.int16)
    lane = iota((64, 128), 1)
    stats = jnp.where(lane == 0, top, jnp.where(lane == 1, mass, jnp.where(lane == 2, positive, level)))
    pieces = jnp.floor(stats)
    rest = (stats - pieces) * FINE
    middle = jnp.floor(rest)
    last = jnp.floor((rest - middle) * FINE)
    middle = middle - 32768.0
    last = last - 32768.0
    block = jnp.where(lane < 4, pieces, jnp.where(lane < 8, pltpu.roll(middle, 4, 1), pltpu.roll(last, 8, 1)))
    out_ref[:, PART:] = jnp.where(lane < 12, block, 0.0).astype(jnp.int32).astype(jnp.int16)


def inner_kernel(ids_ref, positive_ref, parts_ref, query_ref, gathered_ref, hidden_ref, gain_ref, out_ref, grad_ref):
    pieces = parts_ref[:, PART:].astype(jnp.int32).astype(f32)
    middle = pltpu.roll(pieces, 124, 1) + 32768.0
    last = pltpu.roll(pieces, 120, 1) + 32768.0
    stats = pieces + (middle + last / FINE) / FINE
    tops = stats[:, 0:1]
    positives = stats[:, 2:3]
    even = iota((64, 1), 0) % 2 == 0
    both = jnp.maximum(tops, positives)
    top = jnp.where(
        even,
        jnp.max(jnp.where(even, both, ABSENT), axis=0, keepdims=True),
        jnp.max(jnp.where(even, ABSENT, both), axis=0, keepdims=True),
    )
    scale = jnp.exp(tops - top)
    mass = stats[:, 1:2] * scale
    own = jnp.exp(positives - top)
    weighted = parts_ref[:, :PART].astype(jnp.int32).astype(f32) * (scale * jnp.exp(stats[:, 3:4]) / FULL)
    folded = weighted[:8]
    for block in range(1, 8):
        folded = folded + weighted[8 * block:8 * block + 8]
    folded = (folded[0:2] + folded[2:4]) + (folded[4:6] + folded[6:8])
    others, full = [], []
    for mask in (even, jnp.logical_not(even)):
        others.append(jnp.sum(jnp.where(mask, mass, 0.0), axis=0, keepdims=True))
        full.append(others[-1] + jnp.sum(jnp.where(mask, own, 0.0), axis=0, keepdims=True))
    others = jnp.concatenate(others, axis=0)
    full = jnp.concatenate(full, axis=0)
    share = others / full
    sums = folded / full
    keys = []
    for q in range(2):
        row = positive_ref[2 * ids_ref[0] + q]
        block = gathered_ref[row // 2 % 2 * 32 + row // 4].astype(f32)
        keys.append(unfold(jnp.where(row % 2 == 0, block[16:24], block[24:32])))
    key = jnp.concatenate(keys, axis=0)
    grad = LOSS_SCALE * (sums - key * (share * INV_TEMP))
    grad_ref[...] = grad
    query = query_ref[...]
    gain = gain_ref[...]
    along = jnp.sum(query * grad, axis=1, keepdims=True)
    rows = jnp.concatenate([grad * gain, query * gain, jnp.zeros((4, PART), f32)], axis=0)
    hi = rows.astype(bf16)
    rest = rows - hi.astype(f32)
    mid = rest.astype(bf16)
    low = (rest - mid.astype(f32)).astype(bf16)
    x = hidden_ref[...]
    dots = dot_t(hi, x) + (dot_t(mid, x) + dot_t(low, x))
    first = iota((1, 128), 1) < SEQ
    of_grad = jnp.where(first, dots[0:1], dots[1:2])
    of_query = jnp.where(first, dots[2:3], dots[3:4])
    of_along = jnp.where(first, along[0:1], along[1:2])
    row = iota((8, 128), 0)
    block = jnp.where(row == 0, of_grad, jnp.where(row == 1, of_query, of_along))
    for peer in range(8):
        out_ref[peer] = block


def output_kernel(sums_ref, grad_ref, query_ref, stat_ref, hidden_ref, gain_ref, out_ref):
    total = sums_ref[0]
    for peer in range(1, 8):
        total = total + sums_ref[peer]
    inverse = stat_ref[0:1]
    length = stat_ref[3:4]
    along = total[2:3]
    inner = inverse * (total[0:1] - along * total[1:2]) / (length * WIDTH)
    inverse_column = column(inverse)
    slide = column(inverse * inverse * inner) / SEQ
    gain = gain_ref[...]
    for q in range(2):
        at = q * SEQ
        scaled = (
            gain * (grad_ref[q:q + 1] - along[:, at:at + 1] * query_ref[q:q + 1])
            / (length[:, at:at + 1] * SEQ)
        )
        out_ref[at:at + SEQ] = (
            inverse_column[at:at + SEQ] * scaled
            - hidden_ref[at:at + SEQ].astype(f32) * slide[at:at + SEQ]
        )


def shape(dims, kind=f32):
    return jax.ShapeDtypeStruct(dims, kind)


def shards(hidden, gain, keys, queue, positive, mix_rows, mix_weight):
    xh, z, core = lax.axis_index("xh"), lax.axis_index("z"), lax.axis_index("c")
    shard = (xh * 16 + z) * 2 + core
    tokens = hidden.reshape(TOKENS, PART)
    gain = gain.reshape(1, PART)
    ids = jnp.stack([shard, core]).astype(jnp.int32)

    squares = call(
        squares_kernel, shape((8, 40, 128)), ids, tokens, queue, gain, smem=(0,), far=(1, 2, 3),
        scratch=[
            pltpu.VMEM((TOKENS, PART), bf16),
            pltpu.VMEM((ROWS, PART), bf16),
            pltpu.VMEM((1, PART), f32),
            pltpu.SemaphoreType.DMA((3,)),
        ],
    )
    squares = lax.all_to_all(squares, PIPE, 0, 0)
    payload, query, stat = call(
        query_kernel,
        [shape((16, 32, 128), bf16), shape((2, PART)), shape((8, 128))],
        squares, tokens, gain, keys,
    )
    payload = lax.all_to_all(payload, "z", 0, 0)
    payload = lax.all_gather(payload, "xh")
    gathered = lax.all_gather(payload, "c").reshape(64, 32, 128)
    dots = call(
        score_kernel, shape((8, BANK, 128)), gathered, queue, keys,
        scratch=[pltpu.VMEM((QUERIES * CHUNKS, 128), f32)],
    )
    dots = lax.all_to_all(dots, PIPE, 0, 0)
    half = shape((QUERIES // 2, EXT))
    keep, send = call(
        grad_kernel, [half, half], ids, dots, stat, queue, keys, mix_rows.T, mix_weight.T,
        positive.reshape(1, QUERIES), smem=(0,), scratch=[pltpu.VMEM((QUERIES, EXT), f32)],
    )
    came = lax.ppermute(send, "c", [(0, 1), (1, 0)])
    parts = call(merge_kernel, shape((QUERIES // 2, EXT), jnp.int16), keep, came)
    parts = lax.all_to_all(parts.reshape(32, 2, EXT), ("xh", "z"), 0, 0).reshape(QUERIES // 2, EXT)
    sums, grad = call(
        inner_kernel,
        [shape((8, 8, 128)), shape((2, PART))],
        ids, positive, parts, query, gathered, tokens, gain, smem=(0, 1),
    )
    sums = lax.all_to_all(sums, PIPE, 0, 0)
    out = call(output_kernel, shape((TOKENS, PART)), sums, grad, query, stat, tokens, gain)
    return out.reshape(2, SEQ, PART)


def solution(mesh):
    fine = Mesh(mesh.devices.reshape(2, 16, 2, 4, 2), ("xh", "z", "c", "y", "xl"))
    dp = ("xh", "z", "c")
    placed = (P(dp, None, PIPE), P(PIPE), P(dp, PIPE), P(dp, PIPE), P(), P(), P())
    return jax.shard_map(
        shards, mesh=fine, in_specs=placed, out_specs=P(dp, None, PIPE), check_vma=False
    )
```

time: 159 us -> 116 us (0.73)
  the two profiles are of different devices: /device:TPU:32 before, /device:TPU:2 now
where the time goes in v2:
time: 116 us
  blocking collectives  102 us (88%)
  Pallas kernels  6.97 us (6%)
  local copies, waits for them, and re-layouts  2.84 us (2%)
  starting transfers between devices  1.92 us (2%)
  waiting for transfers between devices  1.55 us (1%)
    all_to_all x1, blocking collectives, shards(): payload = lax.all_to_all(payload, 'z', 0, 0)  25.9 us
    all_to_all x1, blocking collectives, shards(): lax.all_to_all(parts.reshape(32, 2, EXT), ('xh', 'z'), 0, 0)  24.5 us
    all_to_all x1, blocking collectives, shards(): dots = lax.all_to_all(dots, PIPE, 0, 0)  19.3 us
    all_to_all x1, blocking collectives, shards(): squares = lax.all_to_all(squares, PIPE, 0, 0)  14 us
    all_to_all x1, blocking collectives, shards(): sums = lax.all_to_all(sums, PIPE, 0, 0)  9.24 us
    all_gather x1, blocking collectives, shards(): payload = lax.all_gather(payload, 'xh')  7.14 us
    pallas_call x7, Pallas kernels, call(): pl.pallas_call(kernel, out_shape=outs, in_specs=specs, out_specs=out_spec...  6.97 us
    unnamed x20, local copies, waits for them, and re-layouts  2.72 us
  transfers between devices with their start and end apart: 1, of which 1 were waited for; matrix products, arithmetic and copies ran while one was open for 0% of the time, Pallas kernels for 0%

profile of v2, /device:TPU:2, one launch (start us, length us, event | category | flops | bytes accessed | tf_op | source)
XLA Modules:
  0.0 115.8 jit_solution(10174866574368889831)
XLA Ops:
  0.0 0.0 copy-start.6
  0.0 0.1 pad_add_fusion.ids_ref
  0.1 0.0 copy-start
  0.1 1.0 copy-done
  1.1 0.0 copy-start.2
  1.1 0.9 copy-done.2
  2.1 0.0 copy-start.4
  2.1 0.7 copy-done.4
  2.8 0.0 copy-start.3
  2.8 1.5 %shard_map.73 = f32[8,40,128]{2,1,0:T(8,128)S(1)} custom-call(s32[2]{0:T(128)S(1)} %pad_add_fusion.ids_ref, bf16[128,1024]{1,0:T(8,128)(2,1)S(1)} %bitcast.12, bf16[256,1024]{1,0:T(8,128)(2,1)S(1)} %copy-done, f32[1,1024]{1,0:T(1,128)S(1)} %bitcast.16), custom_call_target="tpu_custom_call" | custom-call | tf_op jit(solution)/shard_map/pallas_call | solution.py:93
  4.2 0.0 copy-start.1
  4.2 14.0 %all_to_all.25.sums_ref = f32[8,40,128]{2,1,0:T(8,128)S(1)} all-to-all(f32[8,40,128]{2,1,0:T(8,128)S(1)} %shard_map.73), channel_id=1, replica_groups=mesh['xh'=2,'z'=16,'c'=2,'y'=4,'xl'=2] {'y','xl'}, dimensions={0} | all-to-all | bytes 327680 | tf_op jit(solution)/shard_map/all_to_all | solution.py:405
  18.3 0.0 copy-done.6
  18.3 0.0 copy-done.3
  18.3 0.3 shard_map.74
  18.6 25.9 %all_to_all.26 = bf16[16,32,128]{2,1,0:T(8,128)(2,1)S(1)} all-to-all(bf16[16,32,128]{2,1,0:T(8,128)(2,1)S(1)} %get-tuple-element.12), channel_id=1, replica_groups=mesh['xh'=2,'z'=16,'c'=2,'y'=4,'xl'=2] {'z'}, dimensions={0} | all-to-all | bytes 262144 | tf_op jit(solution)/shard_map/all_to_all | solution.py:411
  44.4 7.1 %all-gather = bf16[32,32,128]{2,1,0:T(8,128)(2,1)S(1)} all-gather(bf16[16,32,128]{2,1,0:T(8,128)(2,1)S(1)} %all_to_all.26), channel_id=2, replica_groups=mesh['xh'=2,'z'=16,'c'=2,'y'=4,'xl'=2] {'xh'}, dimensions={0}, use_global_device_ids=true | all-gather | bytes 393216 | tf_op jit(solution)/shard_map/all_gather | solution.py:412
  51.6 2.2 %all-gather.1 = bf16[4,16,32,128]{3,2,1,0:T(8,128)(2,1)S(1)} all-gather(bf16[2,16,32,128]{3,2,1,0:T(8,128)(2,1)S(1)} %bitcast.23), channel_id=3, replica_groups=mesh['xh'=2,'z'=16,'c'=2,'y'=4,'xl'=2] {'c'}, dimensions={0}, use_global_device_ids=true | all-gather | bytes 786432 | tf_op jit(solution)/shard_map/all_gather | solution.py:413
  53.7 0.0 copy-done.1
  53.7 0.4 shard_map.75
  54.2 0.0 copy-start.7
  54.2 0.0 copy-start.8
  54.2 0.0 copy-start.9
  54.2 19.3 %all_to_all.27.dots_ref = f32[8,264,128]{2,1,0:T(8,128)S(1)} all-to-all(f32[8,264,128]{2,1,0:T(8,128)S(1)} %shard_map.75), channel_id=1, replica_groups=mesh['xh'=2,'z'=16,'c'=2,'y'=4,'xl'=2] {'y','xl'}, dimensions={0} | all-to-all | bytes 2162688 | tf_op jit(solution)/shard_map/all_to_all | solution.py:418
  73.5 0.0 copy-done.7
  73.5 0.0 copy-done.8
  73.5 0.0 copy-done.9
  73.5 2.2 %shard_map.76 = (f32[64,1152]{1,0:T(8,128)S(1)}, f32[64,1152]{1,0:T(8,128)S(1)}) custom-call(s32[2]{0:T(128)S(1)} %pad_add_fusion.ids_ref, f32[8,264,128]{2,1,0:T(8,128)S(1)} %all_to_all.27.dots_ref, f32[8,128]{1,0:T(8,128)S(1)} %get-tuple-element.13.stat_ref, bf16[256,1024]{1,0:T(8,128)(2,1)S(1)} %copy-done.1, bf16[2,1024]{1,0:T(2,128)(2,1)S(1)} %copy-done.6, ...), custom_call_target="tpu_custom_call" | custom-call | tf_op jit(solution)/shard_map/pallas_call | solution.py:93
  75.8 0.0 copy-start.5
  75.8 1.9 %collective-permute-start = (f32[64,1152]{1,0:T(8,128)S(1)}, f32[64,1152]{1,0:T(8,128)S(1)}, u32[]{:S(2)}, u32[]{:S(2)}) collective-permute-start(f32[64,1152]{1,0:T(8,128)S(1)} %get-tuple-element.15), channel_id=1, source_target_pairs={{0,8},{8,0},{1,9},{9,1},{2,10},{10,2},{3,11},{11,3},{4,12},{12,4},... | collective-permute-start | bytes 884744 | tf_op jit(solution)/shard_map/ppermute | solution.py:424
  77.7 1.5 %collective-permute-done.came_ref = f32[64,1152]{1,0:T(8,128)S(1)} collective-permute-done((f32[64,1152]{1,0:T(8,128)S(1)}, f32[64,1152]{1,0:T(8,128)S(1)}, u32[]{:S(2)}, u32[]{:S(2)}) %collective-permute-start) | collective-permute-done | bytes 294944 | tf_op jit(solution)/shard_map/ppermute | solution.py:424
  79.3 0.4 shard_map.77
  79.6 0.1 reshape.25
  79.7 24.5 %all_to_all.28 = s16[32,2,1152]{2,1,0:T(2,128)(2,1)S(1)} all-to-all(s16[32,2,1152]{2,1,0:T(2,128)(2,1)S(1)} %reshape.25), channel_id=1, replica_groups=mesh['xh'=2,'z'=16,'c'=2,'y'=4,'xl'=2] {'xh','z'}, dimensions={0} | all-to-all | bytes 294912 | tf_op jit(solution)/shard_map/all_to_all | solution.py:426
  104.2 0.1 reshape.26.parts_ref
  104.3 0.0 copy-done.5
  104.3 1.2 %shard_map.78 = (f32[8,8,128]{2,1,0:T(8,128)S(1)}, f32[2,1024]{1,0:T(2,128)S(1)}) custom-call(s32[2]{0:T(128)S(1)} %pad_add_fusion.ids_ref, s32[128]{0:T(128)S(1)} %copy-done.9, s16[64,1152]{1,0:T(8,128)(2,1)S(1)} %reshape.26.parts_ref, f32[2,1024]{1,0:T(2,128)S(1)} %get-tuple-element.16.query_ref, bf16[64,32,128]{2,1,0:T(8,128)(2,1)S(1)} %bitcast.11, ...), custom_call_target="tpu_custom_call" | custom-call | tf_op jit(solution)/shard_map/pallas_call | solution.py:93
  105.6 9.2 %all_to_all.29.sums_ref = f32[8,8,128]{2,1,0:T(8,128)S(1)} all-to-all(f32[8,8,128]{2,1,0:T(8,128)S(1)} %get-tuple-element.17), channel_id=1, replica_groups=mesh['xh'=2,'z'=16,'c'=2,'y'=4,'xl'=2] {'y','xl'}, dimensions={0} | all-to-all | bytes 65536 | tf_op jit(solution)/shard_map/all_to_all | solution.py:432
  114.8 1.0 shard_map.79
Async XLA Ops:
  0.0 18.3 %copy-start.6 = (bf16[2,1024]{1,0:T(2,128)(2,1)S(1)}, bf16[2,1024]{1,0:T(2,128)(2,1)}, u32[]{:S(2)}) copy-start(bf16[2,1024]{1,0:T(2,128)(2,1)} %keys_ref.5) | copy-start | bytes 12292
  0.1 1.0 copy-start
  1.1 0.9 copy-start.2
  2.1 0.7 copy-start.4
  2.8 15.5 %copy-start.3 = (bf16[2,64,1024]{2,1,0:T(8,128)(2,1)S(1)}, bf16[2,64,1024]{2,1,0:T(8,128)(2,1)}, u32[]{:S(2)}) copy-start(bf16[2,64,1024]{2,1,0:T(8,128)(2,1)} %param.7) | copy-start | bytes 786436
  4.2 49.5 %copy-start.1 = (bf16[256,1024]{1,0:T(8,128)(2,1)S(1)}, bf16[256,1024]{1,0:T(8,128)(2,1)}, u32[]{:S(2)}) copy-start(bf16[256,1024]{1,0:T(8,128)(2,1)} %queue_ref.3) | copy-start | bytes 1572868
  54.2 19.4 %copy-start.7 = (s32[128,16]{0,1:T(8,128)S(1)}, s32[128,16]{0,1:T(8,128)}, u32[]{:S(2)}) copy-start(s32[128,16]{0,1:T(8,128)} %param.12) | copy-start | bytes 24580
  54.2 19.4 %copy-start.8 = (f32[128,16]{0,1:T(8,128)S(1)}, f32[128,16]{0,1:T(8,128)}, u32[]{:S(2)}) copy-start(f32[128,16]{0,1:T(8,128)} %param.13) | copy-start | bytes 24580
  54.2 19.4 %copy-start.9 = (s32[128]{0:T(128)S(1)}, s32[128]{0:T(128)}, u32[]{:S(2)}) copy-start(s32[128]{0:T(128)} %positive_ref.1) | copy-start | bytes 1540
  75.8 28.5 %copy-start.5 = (f32[1024]{0:T(1024)S(1)}, f32[1024]{0:T(1024)}, u32[]{:S(2)}) copy-start(f32[1024]{0:T(1024)} %param.8) | copy-start | bytes 12292
  75.8 3.5 %collective-permute-start = (f32[64,1152]{1,0:T(8,128)S(1)}, f32[64,1152]{1,0:T(8,128)S(1)}, u32[]{:S(2)}, u32[]{:S(2)}) collective-permute-start(f32[64,1152]{1,0:T(8,128)S(1)} %get-tuple-element.15), channel_id=1, source_target_pairs={{0,8},{8,0},{1,9},{9,1},{2,10},{10,2},{3,11},{11,3},{4,12},{12,4},... | collective-permute-start | bytes 884744 | tf_op jit(solution)/shard_map/ppermute | solution.py:424

commit v3 on v2

v3 whole, which is shorter than its diff:
```python
import functools

import jax
import jax.numpy as jnp
from jax import lax
from jax.experimental import pallas as pl
from jax.experimental.pallas import tpu as pltpu
from jax.sharding import Mesh, PartitionSpec as P

NORM_EPS = 1e-05
MIX_EPS = 1e-06
INV_TEMP = 20.0
LOSS_SCALE = 2048.0
WIDTH = 8192
PART = 1024
CHUNKS = 8
SEQ = 64
TOKENS = 128
QUERIES = 128
ROWS = 256
KEYS = 16
BANK = ROWS + KEYS
BANKS = 4
OWN = 32
SLOTS = 16
EXT = 2 * PART + 128
ABSENT = -30000.0
FINE = 65536.0
FULL = 32000.0
PIPE = ("y", "xl")
VMEM = 24 << 20

f32 = jnp.float32
bf16 = jnp.bfloat16


def dot_t(a, b):
    return lax.dot_general(a, b, (((1,), (1,)), ((), ())), preferred_element_type=f32)


def split(a):
    hi = a.astype(bf16)
    return hi, (a - hi.astype(f32)).astype(bf16)


def iota(shape, dim):
    return lax.broadcasted_iota(jnp.int32, shape, dim)


def padded(keys):
    return jnp.concatenate([keys.astype(f32), jnp.zeros((KEYS - 2, PART), f32)], axis=0).astype(bf16)


def own_lanes(rows):
    old, new = iota((128, 128), 0), iota((128, 128), 1) % OWN
    place = ((lax.axis_index("xh") * 16 + new // 2) * 2 + lax.axis_index("c")) * 2 + new % 2
    chosen = jnp.where(old == place, 1.0, 0.0).astype(bf16)
    hi = rows.astype(bf16)
    rest = rows - hi.astype(f32)
    mid = rest.astype(bf16)
    low = (rest - mid.astype(f32)).astype(bf16)
    product = functools.partial(jnp.dot, preferred_element_type=f32)
    return product(hi, chosen) + (product(mid, chosen) + product(low, chosen))


def over_banks(op, row):
    block = jnp.broadcast_to(row, (8, 128))
    block = op(block, pltpu.roll(block, 64, 1))
    return op(block, pltpu.roll(block, 32, 1))[:1]


def whole(a):
    return jnp.floor(a + 0.5).astype(jnp.int32)


def diagonal(square):
    n = square.shape[0]
    on = iota((n, n), 0) == iota((n, n), 1)
    return jnp.sum(jnp.where(on, square, 0.0), axis=0, keepdims=True)


def flat(tall):
    on = iota((128, 128), 0) == iota((128, 128), 1)
    return jnp.sum(jnp.where(on, tall, 0.0), axis=0, keepdims=True)


def column(row):
    on = iota((128, 128), 0) == iota((128, 128), 1)
    return jnp.sum(jnp.where(on, row, 0.0), axis=1, keepdims=True)


def fold(row):
    return jnp.concatenate([row[:, c * 128:(c + 1) * 128] for c in range(CHUNKS)], axis=0)


def unfold(block):
    return jnp.concatenate([block[c:c + 1] for c in range(CHUNKS)], axis=1)


def call(kernel, outs, *args, far=(), far_outs=(), scratch=(), vmem=VMEM):
    def place(i, far):
        return pl.BlockSpec(memory_space=pltpu.HBM if i in far else pltpu.VMEM)

    many = isinstance(outs, (list, tuple))
    return pl.pallas_call(
        kernel,
        out_shape=outs,
        in_specs=[place(i, far) for i in range(len(args))],
        out_specs=[place(i, far_outs) for i in range(len(outs))] if many else place(0, far_outs),
        scratch_shapes=scratch,
        compiler_params=pltpu.CompilerParams(vmem_limit_bytes=vmem),
    )(*args)


def squares_kernel(
    hidden_far, queue_far, gain_far, keys_far, out_ref, bank_far, hidden_ref, gain_ref, keys_ref, padded_ref, sems
):
    copies = [
        pltpu.make_async_copy(keys_far, keys_ref, sems.at[0]),
        pltpu.make_async_copy(queue_far, bank_far.at[pl.ds(0, ROWS)], sems.at[1]),
        pltpu.make_async_copy(gain_far, gain_ref, sems.at[2]),
        pltpu.make_async_copy(hidden_far, hidden_ref, sems.at[3]),
    ]
    for copy in copies:
        copy.start()
    copies[0].wait()
    padded_ref[...] = padded(keys_ref[...])
    last = pltpu.make_async_copy(padded_ref, bank_far.at[pl.ds(ROWS, KEYS)], sems.at[4])
    last.start()
    copies[2].wait()
    copies[3].wait()
    x = hidden_ref[...]
    weighted = x.astype(f32) * (gain_ref[...] * gain_ref[...])
    hi, lo = split(weighted)
    products = dot_t(jnp.concatenate([hi, lo, x], axis=0), x)
    gram = products[:128] + products[128:256]
    up = iota((SEQ, 128), 0) < iota((SEQ, 128), 1)
    both = jnp.where(up, gram[:SEQ], pltpu.roll(gram[SEQ:], SEQ, 1))
    left = iota((32, 128), 1) < SEQ
    packed = jnp.where(left, both[:32], pltpu.roll(both[32:], SEQ, 1))
    token = diagonal(products[256:])
    diag = diagonal(gram)
    row = iota((8, 128), 0)
    sums = jnp.where(row == 0, token, jnp.where(row == 1, diag, 0.0))
    for peer in range(8):
        out_ref[peer, :32] = packed
        out_ref[peer, 32:] = sums
    copies[1].wait()
    last.wait()


def query_kernel(
    sums_ref, hidden_ref, gain_ref, pick_ref, weight_ref, positive_ref, payload_ref, query_ref, stat_ref, index_ref
):
    total = sums_ref[0]
    for peer in range(1, 8):
        total = total + sums_ref[peer]
    token = total[32:33]
    diag = total[33:34]
    inverse = lax.rsqrt(token / WIDTH + NORM_EPS)
    inverse_column = column(inverse)
    first = iota((1, 128), 1) < SEQ
    both = jnp.concatenate([total[:32], pltpu.roll(total[:32], SEQ, 1)], axis=0)
    t, u = iota((SEQ, 128), 0), iota((SEQ, 128), 1)
    second = pltpu.roll(jnp.broadcast_to(inverse, (8, 128)), SEQ, 1)[:1]
    pair = jnp.where(t < u, inverse_column[:SEQ] * inverse, inverse_column[SEQ:] * second)
    pair = jnp.where((t != u) & (u < SEQ), pair * both, 0.0)
    own = diag * inverse * inverse
    lengths = []
    for mask, on in ((first, t < u), (jnp.logical_not(first), t > u)):
        off = jnp.sum(jnp.where(on, pair, 0.0), axis=0, keepdims=True)
        square = jnp.sum(2.0 * off + jnp.where(mask, own, 0.0), axis=1, keepdims=True)
        lengths.append(jnp.sqrt(square) / SEQ)
    weighted = hidden_ref[...].astype(f32) * inverse_column
    gain = gain_ref[...]
    blocks = []
    for q in range(2):
        pooled = jnp.sum(weighted[q * SEQ:(q + 1) * SEQ], axis=0, keepdims=True) * gain / SEQ
        query = pooled / lengths[q]
        query_ref[q:q + 1] = query
        blocks.append(fold(query))
    half = jnp.concatenate(blocks, axis=0).astype(bf16)
    for z in range(16):
        payload_ref[z] = half
    length_row = jnp.where(first, lengths[0], lengths[1])
    stat_ref[...] = jnp.where(iota((8, 128), 0) == 0, inverse, length_row)
    indices = [
        pick_ref[...].astype(f32),
        weight_ref[...],
        jnp.broadcast_to(positive_ref[...].astype(f32), (8, 128)),
    ]
    index_ref[...] = own_lanes(jnp.concatenate(indices, axis=0))


def score_kernel(gathered_ref, bank_ref, out_ref, rows_ref):
    rows_ref[...] = gathered_ref[...].astype(f32).reshape(OWN * CHUNKS, 128)
    queries = jnp.concatenate(
        [rows_ref[pl.ds(c, OWN, stride=CHUNKS), :].astype(bf16) for c in range(CHUNKS)], axis=1
    )
    dots, squares = [], []
    for b in range(BANKS):
        dots.append(dot_t(bank_ref[b], queries))
        rows = bank_ref[b, :ROWS].astype(f32)
        part = rows[:, :128] * rows[:, :128]
        for c in range(1, CHUNKS):
            chunk = rows[:, c * 128:(c + 1) * 128]
            part = part + chunk * chunk
        total = jnp.sum(part, axis=1, keepdims=True)
        squares += [flat(total[:128]), flat(total[128:])]
    dots = jnp.concatenate(dots, axis=1)
    squares = jnp.concatenate(squares, axis=0)
    for peer in range(4):
        out_ref[peer, :ROWS + 8] = dots[:ROWS + 8]
        out_ref[peer, ROWS + 8:] = squares


def sum_kernel(parts_ref, out_ref):
    out_ref[...] = (parts_ref[0] + parts_ref[1]) + (parts_ref[2] + parts_ref[3])


def quantized(rows):
    most = jnp.maximum(jnp.max(jnp.abs(rows), axis=1, keepdims=True), 1e-30)
    level = jnp.floor(jnp.log(most) * FINE + 0.5) / FINE
    return whole(rows * (FULL * jnp.exp(-level))).astype(jnp.int16), level


def grad_kernel(dots_ref, index_ref, bank_ref, out_ref):
    dots = dots_ref[0] + dots_ref[1]
    queue_dots = dots[:ROWS]
    key_dots = dots[ROWS:ROWS + 8]
    z = lax.axis_index("z")
    group = iota((1, 128), 1) // OWN
    halves = []
    for half in range(2):
        wide = column(dots[ROWS + 8 + half:ROWS + 9 + half])
        for b in range(1, BANKS):
            at = ROWS + 8 + 2 * b + half
            wide = jnp.where(group == b, column(dots[at:at + 1]), wide)
        halves.append(wide)
    square = jnp.concatenate(halves, axis=0)
    index = iota((ROWS, 128), 0)
    rows = whole(index_ref[:16])
    shard = rows // ROWS
    present = (shard // 2 % 16 == z) & (shard // 32 * 2 + shard % 2 == group)
    pick = jnp.where(present, rows % ROWS, -1)
    beta = index_ref[16:32]
    target = whole(index_ref[32:33])
    shard = target // 2
    held = (shard // 2 % 16 == z) & (shard // 32 * 2 + shard % 2 == group)
    target = jnp.where(held, target % 2, -1)
    cosines, squares = [], []
    for h in range(SLOTS):
        on = index == pick[h:h + 1]
        cosines.append(jnp.sum(jnp.where(on, queue_dots, 0.0), axis=0, keepdims=True))
        squares.append(jnp.sum(jnp.where(on, square, 0.0), axis=0, keepdims=True))
    cosine = jnp.concatenate(cosines, axis=0)
    picked = jnp.concatenate(squares, axis=0)
    rest = 1.0 - beta
    numer = beta + rest * cosine
    radius_sq = beta * beta + rest * rest * picked + 2.0 * beta * rest * cosine + MIX_EPS
    radius_sq = jnp.where(present, radius_sq, 1.0)
    radius = jnp.sqrt(radius_sq)
    mixed = numer * INV_TEMP / radius
    slope = (rest - numer * beta * rest / radius_sq) * INV_TEMP / radius
    low = -1e30
    mixed = jnp.where(present, mixed, low)
    queue_scores = queue_dots * INV_TEMP
    key_row = iota((8, 128), 0)
    own = key_row == target
    positive = jnp.sum(jnp.where(own, key_dots * INV_TEMP, 0.0), axis=0, keepdims=True)
    positive = over_banks(jnp.maximum, jnp.where(held, positive, ABSENT))
    other = (key_row < 2) & jnp.logical_not(own)
    key_scores = jnp.where(other, key_dots * INV_TEMP, low)
    top = jnp.maximum(
        jnp.maximum(
            jnp.max(queue_scores, axis=0, keepdims=True), jnp.max(key_scores, axis=0, keepdims=True)
        ),
        jnp.max(mixed, axis=0, keepdims=True),
    )
    top = over_banks(jnp.maximum, top)
    queue_exp = jnp.exp(queue_scores - top)
    key_exp = jnp.where(other, jnp.exp(key_scores - top), 0.0)
    mixed_exp = jnp.where(present, jnp.exp(mixed - top), 0.0)
    mass = (
        jnp.sum(queue_exp, axis=0, keepdims=True)
        + jnp.sum(key_exp, axis=0, keepdims=True)
        + jnp.sum(mixed_exp, axis=0, keepdims=True)
    )
    mass = over_banks(jnp.add, mass)
    extra = jnp.where(present, mixed_exp * slope, 0.0)
    coef = queue_exp * INV_TEMP
    for h in range(SLOTS):
        coef = coef + jnp.where(index == pick[h:h + 1], extra[h:h + 1], 0.0)
    hi, lo = split(jnp.transpose(coef))
    blank = jnp.zeros((8, 128), f32)
    small = [key_exp * INV_TEMP, blank, jnp.where(own, 1.0, 0.0), blank, jnp.zeros((96, 128), f32)]
    small = jnp.transpose(jnp.concatenate(small, axis=0))
    key_hi, key_lo = split(small)
    chosen = pltpu.roll(small, 112, 1).astype(bf16)
    product = functools.partial(jnp.dot, preferred_element_type=f32)
    sums = jnp.zeros((2 * OWN, PART), f32)
    extras = jnp.zeros((3 * OWN, PART), f32)
    for b in range(BANKS):
        at = slice(b * OWN, (b + 1) * OWN)
        sums = sums + product(jnp.concatenate([hi[at], lo[at]], axis=0), bank_ref[b, :ROWS])
        few = jnp.concatenate([key_hi[at], key_lo[at], chosen[at]], axis=0)[:, :KEYS]
        extras = extras + product(few, bank_ref[b, ROWS:])
    sums = (sums[:OWN] + sums[OWN:]) + (extras[:OWN] + extras[OWN:2 * OWN])
    out_ref[:, :PART], level = quantized(sums)
    out_ref[:, PART:2 * PART], key_level = quantized(extras[2 * OWN:])
    lane = iota((OWN, 128), 1)
    stats = jnp.where(lane == 0, column(top)[:OWN], 0.0)
    stats = jnp.where(lane == 1, column(mass)[:OWN], stats)
    stats = jnp.where(lane == 2, column(positive)[:OWN], stats)
    stats = jnp.where(lane == 3, level, jnp.where(lane == 4, key_level, stats))
    pieces = jnp.floor(stats)
    rest = (stats - pieces) * FINE
    middle = jnp.floor(rest)
    last = jnp.floor((rest - middle) * FINE)
    middle = middle - 32768.0
    last = last - 32768.0
    block = jnp.where(lane < 8, pieces, jnp.where(lane < 16, pltpu.roll(middle, 8, 1), pltpu.roll(last, 16, 1)))
    out_ref[:, 2 * PART:] = jnp.where(lane < 24, block, 0.0).astype(jnp.int32).astype(jnp.int16)


def inner_kernel(parts_ref, query_ref, hidden_ref, gain_ref, out_ref, grad_ref):
    pieces = parts_ref[:, 2 * PART:].astype(jnp.int32).astype(f32)
    middle = pltpu.roll(pieces, 120, 1) + 32768.0
    last = pltpu.roll(pieces, 112, 1) + 32768.0
    stats = pieces + (middle + last / FINE) / FINE
    tops = stats[:, 0:1]
    positives = stats[:, 2:3]
    even = iota((OWN, 1), 0) % 2 == 0
    both = jnp.maximum(tops, positives)
    top = jnp.where(
        even,
        jnp.max(jnp.where(even, both, ABSENT), axis=0, keepdims=True),
        jnp.max(jnp.where(even, ABSENT, both), axis=0, keepdims=True),
    )
    scale = jnp.exp(tops - top)
    mass = stats[:, 1:2] * scale
    own = jnp.exp(positives - top)

    def folded(at, factor):
        rows = parts_ref[:, at:at + PART].astype(jnp.int32).astype(f32) * (factor / FULL)
        rows = (rows[:8] + rows[8:16]) + (rows[16:24] + rows[24:])
        return (rows[0:2] + rows[2:4]) + (rows[4:6] + rows[6:8])

    sums = folded(0, scale * jnp.exp(stats[:, 3:4]))
    key = folded(PART, jnp.exp(stats[:, 4:5]))
    others, full = [], []
    for mask in (even, jnp.logical_not(even)):
        others.append(jnp.sum(jnp.where(mask, mass, 0.0), axis=0, keepdims=True))
        full.append(others[-1] + jnp.sum(jnp.where(mask, own, 0.0), axis=0, keepdims=True))
    others = jnp.concatenate(others, axis=0)
    full = jnp.concatenate(full, axis=0)
    share = others / full
    sums = sums / full
    grad = LOSS_SCALE * (sums - key * (share * INV_TEMP))
    grad_ref[...] = grad
    query = query_ref[...]
    gain = gain_ref[...]
    along = jnp.sum(query * grad, axis=1, keepdims=True)
    rows = jnp.concatenate([grad * gain, query * gain, jnp.zeros((4, PART), f32)], axis=0)
    hi = rows.astype(bf16).astype(f32)
    mid = (rows - hi).astype(bf16).astype(f32)
    pieces = jnp.concatenate([hi, mid, rows - hi - mid, jnp.zeros((8, PART), f32)], axis=0).astype(bf16)
    dots = dot_t(pieces, hidden_ref[...])
    dots = dots[:8] + (dots[8:16] + dots[16:24])
    first = iota((1, 128), 1) < SEQ
    of_grad = jnp.where(first, dots[0:1], dots[1:2])
    of_query = jnp.where(first, dots[2:3], dots[3:4])
    of_along = jnp.where(first, along[0:1], along[1:2])
    row = iota((8, 128), 0)
    block = jnp.where(row == 0, of_grad, jnp.where(row == 1, of_query, of_along))
    for peer in range(8):
        out_ref[peer] = block


def output_kernel(sums_ref, grad_ref, query_ref, stat_ref, hidden_ref, gain_ref, out_ref):
    total = sums_ref[0]
    for peer in range(1, 8):
        total = total + sums_ref[peer]
    inverse = stat_ref[0:1]
    length = stat_ref[1:2]
    along = total[2:3]
    inner = inverse * (total[0:1] - along * total[1:2]) / (length * WIDTH)
    inverse_column = column(inverse)
    slide = column(inverse * inverse * inner) / SEQ
    gain = gain_ref[...]
    for q in range(2):
        at = q * SEQ
        scaled = (
            gain * (grad_ref[q:q + 1] - along[:, at:at + 1] * query_ref[q:q + 1])
            / (length[:, at:at + 1] * SEQ)
        )
        out_ref[at:at + SEQ] = (
            inverse_column[at:at + SEQ] * scaled
            - hidden_ref[at:at + SEQ].astype(f32) * slide[at:at + SEQ]
        )


def shape(dims, kind=f32):
    return jax.ShapeDtypeStruct(dims, kind)


def shards(hidden, gain, keys, queue, positive, mix_rows, mix_weight):
    tokens = hidden.reshape(TOKENS, PART)
    gain = gain.reshape(1, PART)
    squares, bank = call(
        squares_kernel, [shape((8, 40, 128)), shape((BANK, PART), bf16)], tokens, queue, gain, keys,
        far=(0, 1, 2, 3), far_outs=(1,), vmem=63 << 20,
        scratch=[
            pltpu.VMEM((TOKENS, PART), bf16),
            pltpu.VMEM((1, PART), f32),
            pltpu.VMEM((2, PART), bf16),
            pltpu.VMEM((KEYS, PART), bf16),
            pltpu.SemaphoreType.DMA((5,)),
        ],
    )
    bank = lax.all_gather(bank, ("xh", "c"))
    squares = lax.all_to_all(squares, PIPE, 0, 0)
    payload, query, stat, index = call(
        query_kernel,
        [shape((16, 16, 128), bf16), shape((2, PART)), shape((8, 128)), shape((40, 128))],
        squares, tokens, gain, mix_rows.T, mix_weight.T, positive.reshape(1, QUERIES),
    )
    gathered = lax.all_to_all(payload, "z", 0, 0)
    dots = call(
        score_kernel, shape((4, BANK, 128)), gathered, bank, scratch=[pltpu.VMEM((OWN * CHUNKS, 128), f32)]
    )
    dots = lax.all_to_all(dots, "y", 0, 0)
    dots = lax.all_gather(call(sum_kernel, shape((BANK, 128)), dots), "xl")
    parts = call(grad_kernel, shape((OWN, EXT), jnp.int16), dots, index, bank)
    parts = lax.all_to_all(parts.reshape(16, 2, EXT), "z", 0, 0).reshape(OWN, EXT)
    sums, grad = call(
        inner_kernel, [shape((8, 8, 128)), shape((2, PART))], parts, query, tokens, gain
    )
    sums = lax.all_to_all(sums, PIPE, 0, 0)
    out = call(output_kernel, shape((TOKENS, PART)), sums, grad, query, stat, tokens, gain)
    return out.reshape(2, SEQ, PART)


def solution(mesh):
    fine = Mesh(mesh.devices.reshape(2, 16, 2, 4, 2), ("xh", "z", "c", "y", "xl"))
    dp = ("xh", "z", "c")
    placed = (P(dp, None, PIPE), P(PIPE), P(dp, PIPE), P(dp, PIPE), P(), P(), P())
    return jax.shard_map(
        shards, mesh=fine, in_specs=placed, out_specs=P(dp, None, PIPE), check_vma=False
    )
```

time: 116 us -> 132 us (1.14)
  the two profiles are of different devices: /device:TPU:2 before, /device:TPU:32 now
where the time goes in v3:
time: 132 us; the launch traced here: 131 us
  blocking collectives  89.5 us (68%)
  Pallas kernels  22.6 us (17%)
  between operations  13.5 us (10%)
  local copies, waits for them, and re-layouts  5.44 us (4%)
    all_to_all x1, blocking collectives, shards(): gathered = lax.all_to_all(payload, 'z', 0, 0)  26.7 us
    all_to_all x1, blocking collectives, shards(): lax.all_to_all(parts.reshape(16, 2, EXT), 'z', 0, 0).reshape(OWN, EXT)  25.3 us
    pallas_call x7, Pallas kernels, call(): pl.pallas_call(kernel, out_shape=outs, in_specs=[place(i, far) for i in r...  22.6 us
    all_to_all x1, blocking collectives, shards(): squares = lax.all_to_all(squares, PIPE, 0, 0)  12.2 us
    all_to_all x1, blocking collectives, shards(): dots = lax.all_to_all(dots, 'y', 0, 0)  10.7 us
    all_to_all x1, blocking collectives, shards(): sums = lax.all_to_all(sums, PIPE, 0, 0)  8.63 us
    all_gather x1, blocking collectives, shards(): dots = lax.all_gather(call(sum_kernel, shape((BANK, 128)), dots), 'xl')  5.86 us
    unnamed x18, local copies, waits for them, and re-layouts  5.32 us
  transfers between devices with their start and end apart: 1, of which 0 were waited for; matrix products, arithmetic and copies ran while one was open for 0% of the time, Pallas kernels for 0%

profile of v3, /device:TPU:32, one launch (start us, length us, event | category | flops | bytes accessed | tf_op | source)
XLA Modules:
  0.0 131.0 jit_solution(3563527103470692620)
XLA Ops:
  6.5 0.0 all-gather.4.cloned.1.call-start
  6.5 17.7 %shard_map.73 = (f32[8,40,128]{2,1,0:T(8,128)}, bf16[272,1024]{1,0:T(8,128)(2,1)}) custom-call(bf16[128,1024]{1,0:T(8,128)(2,1)} %bitcast.10, bf16[256,1024]{1,0:T(8,128)(2,1)} %queue_far.1, f32[1,1024]{1,0:T(1,128)} %bitcast.15, bf16[2,1024]{1,0:T(2,128)(2,1)} %keys_far.1), custom_call_target="tpu_custom_call" | custom-call | tf_op jit(solution)/shard_map/pallas_call | solution.py:105
  24.2 0.0 all-gather.4.cloned.1.call-update
  24.3 12.2 %all_to_all.25.sums_ref = f32[8,40,128]{2,1,0:T(8,128)S(1)} all-to-all(f32[8,40,128]{2,1,0:T(8,128)} %get-tuple-element.13), channel_id=1, replica_groups=mesh['xh'=2,'z'=16,'c'=2,'y'=4,'xl'=2] {'y','xl'}, dimensions={0} | all-to-all | bytes 327680 | tf_op jit(solution)/shard_map/all_to_all | solution.py:422
  36.5 0.0 copy-start.2
  36.5 0.9 copy-done.2
  37.4 0.0 copy-start.4
  37.5 0.7 copy-done.4
  38.1 0.0 copy-start.6
  38.1 0.7 copy-done.6
  38.8 0.0 copy-start.7
  38.8 0.7 copy-done.7
  39.5 0.0 copy-start.8
  39.5 0.7 copy-done.8
  40.2 0.3 shard_map.74
  40.5 26.7 %all_to_all.26.gathered_ref = bf16[16,16,128]{2,1,0:T(8,128)(2,1)S(1)} all-to-all(bf16[16,16,128]{2,1,0:T(8,128)(2,1)S(1)} %get-tuple-element.14), channel_id=1, replica_groups=mesh['xh'=2,'z'=16,'c'=2,'y'=4,'xl'=2] {'z'}, dimensions={0} | all-to-all | bytes 131072 | tf_op jit(solution)/shard_map/all_to_all | solution.py:428
  67.2 0.0 all-gather.4.cloned.1.call-done
  67.2 0.0 copy-start
  67.2 1.6 %copy-done = bf16[1088,1024]{1,0:T(8,128)(2,1)S(1)} copy-done((bf16[1088,1024]{1,0:T(8,128)(2,1)S(1)}, bf16[1088,1024]{1,0:T(8,128)(2,1)}, u32[]{:S(2)}) %copy-start) | copy-done | bytes 2228248
  68.8 0.0 copy-start.1
  68.8 1.0 shard_map.75
  69.8 10.7 %all_to_all.27.parts_ref = f32[4,272,128]{2,1,0:T(8,128)S(1)} all-to-all(f32[4,272,128]{2,1,0:T(8,128)S(1)} %shard_map.75), channel_id=1, replica_groups=mesh['xh'=2,'z'=16,'c'=2,'y'=4,'xl'=2] {'y'}, dimensions={0} | all-to-all | bytes 1114112 | tf_op jit(solution)/shard_map/all_to_all | solution.py:432
  80.5 0.0 copy-start.3
  80.6 0.0 copy-start.5
  80.6 5.9 %all-gather.1 = f32[544,128]{1,0:T(8,128)S(1)} all-gather(f32[272,128]{1,0:T(8,128)S(1)} %shard_map.76), channel_id=3, replica_groups=mesh['xh'=2,'z'=16,'c'=2,'y'=4,'xl'=2] {'xl'}, dimensions={0}, use_global_device_ids=true | all-gather | bytes 417792 | tf_op jit(solution)/shard_map/all_gather | solution.py:433
  86.4 0.0 copy-done.1
  86.5 2.0 %shard_map.77 = s16[32,2176]{1,0:T(8,128)(2,1)S(1)} custom-call(f32[2,272,128]{2,1,0:T(8,128)S(1)} %bitcast.14, f32[40,128]{1,0:T(8,128)S(1)} %get-tuple-element.16.index_ref, bf16[4,272,1024]{2,1,0:T(8,128)(2,1)S(1)} %bitcast.9), custom_call_target="tpu_custom_call" | custom-call | tf_op jit(solution)/shard_map/pallas_call | solution.py:105
  88.5 0.1 reshape.21
  88.5 25.3 %all_to_all.28 = s16[16,2,2176]{2,1,0:T(2,128)(2,1)S(1)} all-to-all(s16[16,2,2176]{2,1,0:T(2,128)(2,1)S(1)} %reshape.21), channel_id=1, replica_groups=mesh['xh'=2,'z'=16,'c'=2,'y'=4,'xl'=2] {'z'}, dimensions={0} | all-to-all | bytes 278528 | tf_op jit(solution)/shard_map/all_to_all | solution.py:435
  113.9 0.1 reshape.22.parts_ref
  113.9 0.0 copy-done.3
  114.0 0.0 copy-done.5
  114.0 0.6 shard_map.78
  114.5 8.6 %all_to_all.29.sums_ref = f32[8,8,128]{2,1,0:T(8,128)S(1)} all-to-all(f32[8,8,128]{2,1,0:T(8,128)S(1)} %get-tuple-element.18), channel_id=1, replica_groups=mesh['xh'=2,'z'=16,'c'=2,'y'=4,'xl'=2] {'y','xl'}, dimensions={0} | all-to-all | bytes 65536 | tf_op jit(solution)/shard_map/all_to_all | solution.py:439
  123.2 1.0 shard_map.79
  (1 shorter events, 0.0 us)
Async XLA Ops:
  6.5 60.6 %all-gather.4.cloned.1.call-start = ((), (), s32[]{:S(2)}) async-start(), calls=%async_computation.5 | async-start | bytes 2785280 | tf_op jit(solution)/shard_map/all_gather | solution.py:421
  36.5 1.0 copy-start.2
  37.4 0.7 copy-start.4
  38.1 0.7 copy-start.6
  38.8 0.7 copy-start.7
  39.5 0.7 copy-start.8
  67.2 1.6 %copy-start = (bf16[1088,1024]{1,0:T(8,128)(2,1)S(1)}, bf16[1088,1024]{1,0:T(8,128)(2,1)}, u32[]{:S(2)}) copy-start(bf16[1088,1024]{1,0:T(8,128)(2,1)} %all-gather.4.cloned.1.call-done) | copy-start | bytes 6684676
  68.8 17.7 %copy-start.1 = (bf16[1088,1024]{1,0:T(8,128)(2,1)S(1)}, bf16[1088,1024]{1,0:T(8,128)(2,1)}, u32[]{:S(2)}) copy-start(bf16[1088,1024]{1,0:T(8,128)(2,1)} %all-gather.4.cloned.1.call-done) | copy-start | bytes 6684676
  80.5 33.4 %copy-start.3 = (bf16[2,64,1024]{2,1,0:T(8,128)(2,1)S(1)}, bf16[2,64,1024]{2,1,0:T(8,128)(2,1)}, u32[]{:S(2)}) copy-start(bf16[2,64,1024]{2,1,0:T(8,128)(2,1)} %param.7) | copy-start | bytes 786436
  80.6 33.4 %copy-start.5 = (f32[1024]{0:T(1024)S(1)}, f32[1024]{0:T(1024)}, u32[]{:S(2)}) copy-start(f32[1024]{0:T(1024)} %param.8) | copy-start | bytes 12292
Sparse Core Ops, SparseCore 0:
  24.4 39.1 all-gather.3

commit v4 on v3

--- a/solution.py
+++ b/solution.py
@@ -63,6 +63,14 @@
     return product(hi, chosen) + (product(mid, chosen) + product(low, chosen))
 
 
+def spread(rows, lanes):
+    hi = rows.astype(bf16).astype(f32)
+    mid = (rows - hi).astype(bf16).astype(f32)
+    pieces = jnp.concatenate([hi, mid, rows - hi - mid, jnp.zeros((8, 128), f32)], axis=0).astype(bf16)
+    chosen = jnp.where(iota((32, 128), 0) % 8 == lanes, 1.0, 0.0).astype(bf16)
+    return lax.dot_general(pieces, chosen, (((0,), (0,)), ((), ())), preferred_element_type=f32)
+
+
 def over_banks(op, row):
     block = jnp.broadcast_to(row, (8, 128))
     block = op(block, pltpu.roll(block, 64, 1))
@@ -113,22 +121,22 @@
 
 
 def squares_kernel(
-    hidden_far, queue_far, gain_far, keys_far, out_ref, bank_far, hidden_ref, gain_ref, keys_ref, padded_ref, sems
+    hidden_far, queue_far, gain_far, keys_far, out_ref, bank_ref, hidden_ref, gain_ref, keys_ref, sems
 ):
     copies = [
-        pltpu.make_async_copy(keys_far, keys_ref, sems.at[0]),
-        pltpu.make_async_copy(queue_far, bank_far.at[pl.ds(0, ROWS)], sems.at[1]),
-        pltpu.make_async_copy(gain_far, gain_ref, sems.at[2]),
-        pltpu.make_async_copy(hidden_far, hidden_ref, sems.at[3]),
+        pltpu.make_async_copy(source, target, sems.at[i])
+        for i, (source, target) in enumerate((
+            (keys_far, keys_ref),
+            (gain_far, gain_ref),
+            (hidden_far, hidden_ref),
+            (queue_far, bank_ref.at[pl.ds(0, ROWS)]),
+        ))
     ]
     for copy in copies:
         copy.start()
-    copies[0].wait()
-    padded_ref[...] = padded(keys_ref[...])
-    last = pltpu.make_async_copy(padded_ref, bank_far.at[pl.ds(ROWS, KEYS)], sems.at[4])
-    last.start()
-    copies[2].wait()
-    copies[3].wait()
+    for copy in copies[:-1]:
+        copy.wait()
+    bank_ref[ROWS:] = padded(keys_ref[...])
     x = hidden_ref[...]
     weighted = x.astype(f32) * (gain_ref[...] * gain_ref[...])
     hi, lo = split(weighted)
@@ -145,13 +153,10 @@
     for peer in range(8):
         out_ref[peer, :32] = packed
         out_ref[peer, 32:] = sums
-    copies[1].wait()
-    last.wait()
-
-
-def query_kernel(
-    sums_ref, hidden_ref, gain_ref, pick_ref, weight_ref, positive_ref, payload_ref, query_ref, stat_ref, index_ref
-):
+    copies[-1].wait()
+
+
+def query_kernel(sums_ref, hidden_ref, gain_ref, payload_ref, query_ref, stat_ref):
     total = sums_ref[0]
     for peer in range(1, 8):
         total = total + sums_ref[peer]
@@ -184,21 +189,17 @@
         payload_ref[z] = half
     length_row = jnp.where(first, lengths[0], lengths[1])
     stat_ref[...] = jnp.where(iota((8, 128), 0) == 0, inverse, length_row)
-    indices = [
-        pick_ref[...].astype(f32),
-        weight_ref[...],
-        jnp.broadcast_to(positive_ref[...].astype(f32), (8, 128)),
-    ]
-    index_ref[...] = own_lanes(jnp.concatenate(indices, axis=0))
-
-
-def score_kernel(gathered_ref, bank_ref, out_ref, rows_ref):
-    rows_ref[...] = gathered_ref[...].astype(f32).reshape(OWN * CHUNKS, 128)
-    queries = jnp.concatenate(
-        [rows_ref[pl.ds(c, OWN, stride=CHUNKS), :].astype(bf16) for c in range(CHUNKS)], axis=1
-    )
+
+
+def pair_kernel(own_ref, came_ref, after_ref, out_ref):
+    del after_ref
+    out_ref[0] = own_ref[...]
+    out_ref[1] = came_ref[...]
+
+
+def bank_dots(bank_ref, queries):
     dots, squares = [], []
-    for b in range(BANKS):
+    for b in range(2):
         dots.append(dot_t(bank_ref[b], queries))
         rows = bank_ref[b, :ROWS].astype(f32)
         part = rows[:, :128] * rows[:, :128]
@@ -207,10 +208,35 @@
             part = part + chunk * chunk
         total = jnp.sum(part, axis=1, keepdims=True)
         squares += [flat(total[:128]), flat(total[128:])]
-    dots = jnp.concatenate(dots, axis=1)
-    squares = jnp.concatenate(squares, axis=0)
+    return dots, squares
+
+
+def near_kernel(
+    gathered_ref, near_ref, pick_ref, weight_ref, positive_ref, out_ref, queries_ref, index_ref, rows_ref
+):
+    indices = [
+        pick_ref[...].astype(f32),
+        weight_ref[...],
+        jnp.broadcast_to(positive_ref[...].astype(f32), (8, 128)),
+    ]
+    index_ref[...] = own_lanes(jnp.concatenate(indices, axis=0))
+    rows_ref[...] = gathered_ref[...].astype(f32).reshape(OWN * CHUNKS, 128)
+    queries = jnp.concatenate(
+        [rows_ref[pl.ds(c, OWN, stride=CHUNKS), :].astype(bf16) for c in range(CHUNKS)], axis=1
+    )
+    queries_ref[...] = queries
+    dots, squares = bank_dots(near_ref, queries)
+    out_ref[:ROWS + 8] = jnp.concatenate([d[:ROWS + 8] for d in dots] * 2, axis=1)
+    out_ref[ROWS + 8:] = jnp.concatenate(squares * 2, axis=0)
+
+
+def far_kernel(part_ref, queries_ref, far_ref, out_ref):
+    dots, squares = bank_dots(far_ref, queries_ref[...])
+    dots = jnp.concatenate([d[:ROWS + 8] for d in dots] * 2, axis=1)
+    dots = jnp.where(iota((ROWS + 8, 128), 1) < 2 * OWN, part_ref[:ROWS + 8], dots)
+    squares = jnp.concatenate([part_ref[ROWS + 8:ROWS + 12]] + squares, axis=0)
     for peer in range(4):
-        out_ref[peer, :ROWS + 8] = dots[:ROWS + 8]
+        out_ref[peer, :ROWS + 8] = dots
         out_ref[peer, ROWS + 8:] = squares
 
 
@@ -224,35 +250,39 @@
     return whole(rows * (FULL * jnp.exp(-level))).astype(jnp.int16), level
 
 
-def grad_kernel(dots_ref, index_ref, bank_ref, out_ref):
+def bank_of(shard):
+    across = (shard // 32 != lax.axis_index("xh")).astype(jnp.int32)
+    beside = (shard % 2 != lax.axis_index("c")).astype(jnp.int32)
+    return jnp.where(shard // 2 % 16 == lax.axis_index("z"), across + 2 * beside, -1)
+
+
+def grad_kernel(dots_ref, index_ref, near_ref, far_ref, out_ref):
     dots = dots_ref[0] + dots_ref[1]
     queue_dots = dots[:ROWS]
     key_dots = dots[ROWS:ROWS + 8]
-    z = lax.axis_index("z")
     group = iota((1, 128), 1) // OWN
-    halves = []
-    for half in range(2):
-        wide = column(dots[ROWS + 8 + half:ROWS + 9 + half])
-        for b in range(1, BANKS):
-            at = ROWS + 8 + 2 * b + half
-            wide = jnp.where(group == b, column(dots[at:at + 1]), wide)
-        halves.append(wide)
-    square = jnp.concatenate(halves, axis=0)
+    square = jnp.concatenate([spread(dots[ROWS + 8:], 2 * group + half) for half in range(2)], axis=0)
     index = iota((ROWS, 128), 0)
     rows = whole(index_ref[:16])
-    shard = rows // ROWS
-    present = (shard // 2 % 16 == z) & (shard // 32 * 2 + shard % 2 == group)
-    pick = jnp.where(present, rows % ROWS, -1)
+    present = bank_of(rows // ROWS) == group
+    pick = jnp.where(present, rows % ROWS, -8)
     beta = index_ref[16:32]
     target = whole(index_ref[32:33])
-    shard = target // 2
-    held = (shard // 2 % 16 == z) & (shard // 32 * 2 + shard % 2 == group)
+    held = bank_of(target // 2) == group
     target = jnp.where(held, target % 2, -1)
+    tile, inside = pick // 8, pick % 8
+    sublane = iota((8, 128), 0)
     cosines, squares = [], []
     for h in range(SLOTS):
-        on = index == pick[h:h + 1]
-        cosines.append(jnp.sum(jnp.where(on, queue_dots, 0.0), axis=0, keepdims=True))
-        squares.append(jnp.sum(jnp.where(on, square, 0.0), axis=0, keepdims=True))
+        chosen = jnp.zeros((8, 128), f32)
+        scale = jnp.zeros((8, 128), f32)
+        for t in range(ROWS // 8):
+            on = tile[h:h + 1] == t
+            chosen = jnp.where(on, queue_dots[8 * t:8 * t + 8], chosen)
+            scale = jnp.where(on, square[8 * t:8 * t + 8], scale)
+        here = sublane == inside[h:h + 1]
+        cosines.append(jnp.sum(jnp.where(here, chosen, 0.0), axis=0, keepdims=True))
+        squares.append(jnp.sum(jnp.where(here, scale, 0.0), axis=0, keepdims=True))
     cosine = jnp.concatenate(cosines, axis=0)
     picked = jnp.concatenate(squares, axis=0)
     rest = 1.0 - beta
@@ -295,23 +325,27 @@
     blank = jnp.zeros((8, 128), f32)
     small = [key_exp * INV_TEMP, blank, jnp.where(own, 1.0, 0.0), blank, jnp.zeros((96, 128), f32)]
     small = jnp.transpose(jnp.concatenate(small, axis=0))
-    key_hi, key_lo = split(small)
-    chosen = pltpu.roll(small, 112, 1).astype(bf16)
+    lane = iota((OWN, 128), 1)
     product = functools.partial(jnp.dot, preferred_element_type=f32)
     sums = jnp.zeros((2 * OWN, PART), f32)
-    extras = jnp.zeros((3 * OWN, PART), f32)
+    few = jnp.zeros((OWN, 128), f32)
+    keys = []
     for b in range(BANKS):
         at = slice(b * OWN, (b + 1) * OWN)
-        sums = sums + product(jnp.concatenate([hi[at], lo[at]], axis=0), bank_ref[b, :ROWS])
-        few = jnp.concatenate([key_hi[at], key_lo[at], chosen[at]], axis=0)[:, :KEYS]
-        extras = extras + product(few, bank_ref[b, ROWS:])
+        bank_ref = (near_ref, far_ref)[b // 2]
+        sums = sums + product(jnp.concatenate([hi[at], lo[at]], axis=0), bank_ref[b % 2, :ROWS])
+        few = jnp.where(lane % KEYS // 2 == b, pltpu.roll(small[at], 2 * b, 1), few)
+        keys.append(bank_ref[b % 2, ROWS:].astype(f32)[:2])
+    keys = jnp.concatenate(keys + [jnp.zeros((KEYS - 8, PART), f32)], axis=0).astype(bf16)
+    chosen = pltpu.roll(few, 128 - KEYS, 1)
+    few_hi = few.astype(bf16).astype(f32)
+    few = jnp.concatenate([few_hi, few - few_hi, chosen], axis=0).astype(bf16)[:, :KEYS]
+    extras = product(few, keys)
     sums = (sums[:OWN] + sums[OWN:]) + (extras[:OWN] + extras[OWN:2 * OWN])
     out_ref[:, :PART], level = quantized(sums)
     out_ref[:, PART:2 * PART], key_level = quantized(extras[2 * OWN:])
-    lane = iota((OWN, 128), 1)
-    stats = jnp.where(lane == 0, column(top)[:OWN], 0.0)
-    stats = jnp.where(lane == 1, column(mass)[:OWN], stats)
-    stats = jnp.where(lane == 2, column(positive)[:OWN], stats)
+    rows = jnp.concatenate([top, mass, positive, jnp.zeros((5, 128), f32)], axis=0)
+    stats = spread(rows, jnp.where(iota((1, 128), 1) < 3, iota((1, 128), 1), -1))[:OWN]
     stats = jnp.where(lane == 3, level, jnp.where(lane == 4, key_level, stats))
     pieces = jnp.floor(stats)
     rest = (stats - pieces) * FINE
@@ -377,7 +411,7 @@
         out_ref[peer] = block
 
 
-def output_kernel(sums_ref, grad_ref, query_ref, stat_ref, hidden_ref, gain_ref, out_ref):
+def output_kernel(sums_ref, grad_ref, query_ref, stat_ref, hidden_ref, gain_ref, out_far, out_ref, sems):
     total = sums_ref[0]
     for peer in range(1, 8):
         total = total + sums_ref[peer]
@@ -388,6 +422,7 @@
     inverse_column = column(inverse)
     slide = column(inverse * inverse * inner) / SEQ
     gain = gain_ref[...]
+    copies = []
     for q in range(2):
         at = q * SEQ
         scaled = (
@@ -398,6 +433,11 @@
             inverse_column[at:at + SEQ] * scaled
             - hidden_ref[at:at + SEQ].astype(f32) * slide[at:at + SEQ]
         )
+        part = pl.ds(at, SEQ)
+        copies.append(pltpu.make_async_copy(out_ref.at[part], out_far.at[part], sems.at[q]))
+        copies[-1].start()
+    for copy in copies:
+        copy.wait()
 
 
 def shape(dims, kind=f32):
@@ -409,35 +449,42 @@
     gain = gain.reshape(1, PART)
     squares, bank = call(
         squares_kernel, [shape((8, 40, 128)), shape((BANK, PART), bf16)], tokens, queue, gain, keys,
-        far=(0, 1, 2, 3), far_outs=(1,), vmem=63 << 20,
+        far=range(4), vmem=63 << 20,
         scratch=[
             pltpu.VMEM((TOKENS, PART), bf16),
             pltpu.VMEM((1, PART), f32),
             pltpu.VMEM((2, PART), bf16),
-            pltpu.VMEM((KEYS, PART), bf16),
-            pltpu.SemaphoreType.DMA((5,)),
+            pltpu.SemaphoreType.DMA((4,)),
         ],
     )
-    bank = lax.all_gather(bank, ("xh", "c"))
+    swap = [(0, 1), (1, 0)]
     squares = lax.all_to_all(squares, PIPE, 0, 0)
-    payload, query, stat, index = call(
-        query_kernel,
-        [shape((16, 16, 128), bf16), shape((2, PART)), shape((8, 128)), shape((40, 128))],
-        squares, tokens, gain, mix_rows.T, mix_weight.T, positive.reshape(1, QUERIES),
+    own, squares = lax.optimization_barrier((bank, squares))
+    came = lax.ppermute(own, "xh", swap)
+    payload, query, stat = call(
+        query_kernel, [shape((16, 16, 128), bf16), shape((2, PART)), shape((8, 128))], squares, tokens, gain
     )
     gathered = lax.all_to_all(payload, "z", 0, 0)
-    dots = call(
-        score_kernel, shape((4, BANK, 128)), gathered, bank, scratch=[pltpu.VMEM((OWN * CHUNKS, 128), f32)]
-    )
+    near = call(pair_kernel, shape((2, BANK, PART), bf16), own, came, gathered)
+    far = lax.ppermute(near, "c", swap)
+    dots, queries, index = call(
+        near_kernel, [shape((BANK, 128)), shape((OWN, PART), bf16), shape((40, 128))],
+        gathered, near, mix_rows.T, mix_weight.T, positive.reshape(1, QUERIES),
+        scratch=[pltpu.VMEM((OWN * CHUNKS, 128), f32)],
+    )
+    dots = call(far_kernel, shape((4, BANK, 128)), dots, queries, far)
     dots = lax.all_to_all(dots, "y", 0, 0)
     dots = lax.all_gather(call(sum_kernel, shape((BANK, 128)), dots), "xl")
-    parts = call(grad_kernel, shape((OWN, EXT), jnp.int16), dots, index, bank)
+    parts = call(grad_kernel, shape((OWN, EXT), jnp.int16), dots, index, near, far)
     parts = lax.all_to_all(parts.reshape(16, 2, EXT), "z", 0, 0).reshape(OWN, EXT)
     sums, grad = call(
         inner_kernel, [shape((8, 8, 128)), shape((2, PART))], parts, query, tokens, gain
     )
     sums = lax.all_to_all(sums, PIPE, 0, 0)
-    out = call(output_kernel, shape((TOKENS, PART)), sums, grad, query, stat, tokens, gain)
+    out = call(
+        output_kernel, shape((TOKENS, PART)), sums, grad, query, stat, tokens, gain, far_outs=(0,),
+        scratch=[pltpu.VMEM((TOKENS, PART), f32), pltpu.SemaphoreType.DMA((2,))],
+    )
     return out.reshape(2, SEQ, PART)
 
 

time: 132 us -> 99.5 us (0.75)
  Pallas kernels: 22.6 us -> 7.3 us
  between operations: 13.5 us -> 0.15 us
  blocking collectives: 89.5 us -> 82.7 us
  starting transfers between devices: 0.01 us -> 6.55 us
  local copies, waits for them, and re-layouts: 5.44 us -> 0.15 us
  waiting for transfers between devices: 0.02 us -> 2.07 us
    pallas_call x7 -> x9, Pallas kernels: 22.6 us -> 7.3 us  [call(): pl.pallas_call(kernel, out_shape=outs, in_specs=[place(i, far) for i in r...]
    all_to_all x1, blocking collectives: 25.3 us -> 16.4 us  [shards(): lax.all_to_all(parts.reshape(16, 2, EXT), 'z', 0, 0).reshape(OWN, EXT)]
    ppermute x0 -> x2, starting transfers between devices: none -> 6.55 us  [the longest x1 4.63 us: shards(): came = lax.ppermute(own, 'xh', swap)]
    unnamed x18 -> x12, local copies, waits for them, and re-layouts: 5.32 us -> 0.02 us
    ppermute x0 -> x2, waiting for transfers between devices: none -> 2.07 us  [the longest x1 2.07 us: shards(): far = lax.ppermute(near, 'c', swap)]
    all_to_all x1, blocking collectives: 10.7 us -> 12.8 us  [shards(): dots = lax.all_to_all(dots, 'y', 0, 0)]
  transfers between devices with their start and end apart: 1 -> 2, of which waited for: 0 -> 1; matrix products, arithmetic and copies ran while one was open for 0% -> 0% of each run, Pallas kernels for 0% -> 1%
where the time goes in v4:
time: 99.5 us; the launch traced here: 98.9 us
  blocking collectives  82.7 us (83%)
  Pallas kernels  7.3 us (7%)
  starting transfers between devices  6.55 us (7%)
  waiting for transfers between devices  2.07 us (2%)
    all_to_all x1, blocking collectives, shards(): gathered = lax.all_to_all(payload, 'z', 0, 0)  26.8 us
    all_to_all x1, blocking collectives, shards(): lax.all_to_all(parts.reshape(16, 2, EXT), 'z', 0, 0).reshape(OWN, EXT)  16.4 us
    all_to_all x1, blocking collectives, shards(): dots = lax.all_to_all(dots, 'y', 0, 0)  12.8 us
    all_to_all x1, blocking collectives, shards(): squares = lax.all_to_all(squares, PIPE, 0, 0)  12.4 us
    all_to_all x1, blocking collectives, shards(): sums = lax.all_to_all(sums, PIPE, 0, 0)  8.63 us
    pallas_call x9, Pallas kernels, call(): pl.pallas_call(kernel, out_shape=outs, in_specs=[place(i, far) for i in r...  7.3 us
    all_gather x1, blocking collectives, shards(): dots = lax.all_gather(call(sum_kernel, shape((BANK, 128)), dots), 'xl')  5.73 us
    ppermute x1, starting transfers between devices, shards(): came = lax.ppermute(own, 'xh', swap)  4.63 us
  transfers between devices with their start and end apart: 2, of which 1 were waited for; matrix products, arithmetic and copies ran while one was open for 0% of the time, Pallas kernels for 1%

profile of v4, /device:TPU:32, one launch (start us, length us, event | category | flops | bytes accessed | tf_op | source)
XLA Modules:
  0.0 98.9 jit_solution(16658374053672259735)
XLA Ops:
  0.0 0.0 copy-start.2
  0.0 0.0 copy-start
  0.0 2.4 %shard_map.73 = (f32[8,40,128]{2,1,0:T(8,128)}, bf16[272,1024]{1,0:T(8,128)(2,1)}) custom-call(bf16[128,1024]{1,0:T(8,128)(2,1)} %bitcast.7, bf16[256,1024]{1,0:T(8,128)(2,1)} %queue_far.1, f32[1,1024]{1,0:T(1,128)} %bitcast.12, bf16[2,1024]{1,0:T(2,128)(2,1)} %keys_far.1), custom_call_target="tpu_custom_call" | custom-call | tf_op jit(solution)/shard_map/pallas_call | solution.py:113
  2.4 0.0 copy-start.1
  2.4 12.4 %all_to_all.25.sums_ref = f32[8,40,128]{2,1,0:T(8,128)S(1)} all-to-all(f32[8,40,128]{2,1,0:T(8,128)} %get-tuple-element.18), channel_id=1, replica_groups=mesh['xh'=2,'z'=16,'c'=2,'y'=4,'xl'=2] {'y','xl'}, dimensions={0} | all-to-all | bytes 327680 | tf_op jit(solution)/shard_map/all_to_all | solution.py:461
  14.8 4.6 %collective-permute-start = (bf16[272,1024]{1,0:T(8,128)(2,1)}, bf16[272,1024]{1,0:T(8,128)(2,1)S(1)}, u32[]{:S(2)}, u32[]{:S(2)}) collective-permute-start(bf16[272,1024]{1,0:T(8,128)(2,1)} %get-tuple-element.21.own_ref), channel_id=1, source_target_pairs={{0,256},{256,0},{1,257},{257,1},{2,258},{258,2},{3,259},{259,3},{4... | collective-permute-start | bytes 1671176 | tf_op jit(solution)/shard_map/ppermute | solution.py:463
  19.4 0.0 copy-done.2
  19.4 0.0 copy-done
  19.4 0.3 shard_map.74
  19.7 26.8 %all_to_all.26.after_ref.gathered_ref = bf16[16,16,128]{2,1,0:T(8,128)(2,1)S(1)} all-to-all(bf16[16,16,128]{2,1,0:T(8,128)(2,1)S(1)} %get-tuple-element.20), channel_id=1, replica_groups=mesh['xh'=2,'z'=16,'c'=2,'y'=4,'xl'=2] {'z'}, dimensions={0} | all-to-all | bytes 131072 | tf_op jit(solution)/shard_map/all_to_all | solution.py:467
  46.6 0.0 copy-start.3
  46.6 0.0 copy-start.4
  46.6 0.0 copy-start.5
  46.6 0.0 collective-permute-done.came_ref
  46.6 0.0 copy-done.1
  46.6 0.1 shard_map.75.near_ref
  46.7 1.9 %collective-permute-start.1 = (bf16[2,272,1024]{2,1,0:T(8,128)(2,1)S(1)}, bf16[2,272,1024]{2,1,0:T(8,128)(2,1)S(1)}, u32[]{:S(2)}, u32[]{:S(2)}) collective-permute-start(bf16[2,272,1024]{2,1,0:T(8,128)(2,1)S(1)} %shard_map.75.near_ref), channel_id=1, source_target_pairs={{0,8},{8,0},{1,9},{9,1},{2,10},{10,2},{3,11},{11,3},{4,12},{12,4},... | collective-permute-start | bytes 3342344 | tf_op jit(solution)/shard_map/ppermute | solution.py:469
  48.6 0.0 copy-done.3
  48.6 0.0 copy-done.4
  48.6 0.0 copy-done.5
  48.6 0.6 shard_map.76
  49.3 2.1 %collective-permute-done.1.far_ref = bf16[2,272,1024]{2,1,0:T(8,128)(2,1)S(1)} collective-permute-done((bf16[2,272,1024]{2,1,0:T(8,128)(2,1)S(1)}, bf16[2,272,1024]{2,1,0:T(8,128)(2,1)S(1)}, u32[]{:S(2)}, u32[]{:S(2)}) %collective-permute-start.1) | collective-permute-done | bytes 1114144 | tf_op jit(solution)/shard_map/ppermute | solution.py:469
  51.3 0.6 shard_map.77
  51.9 12.8 %all_to_all.27.parts_ref = f32[4,272,128]{2,1,0:T(8,128)S(1)} all-to-all(f32[4,272,128]{2,1,0:T(8,128)S(1)} %shard_map.77), channel_id=1, replica_groups=mesh['xh'=2,'z'=16,'c'=2,'y'=4,'xl'=2] {'y'}, dimensions={0} | all-to-all | bytes 1114112 | tf_op jit(solution)/shard_map/all_to_all | solution.py:476
  64.7 5.7 %all-gather = f32[544,128]{1,0:T(8,128)S(1)} all-gather(f32[272,128]{1,0:T(8,128)S(1)} %shard_map.78), channel_id=2, replica_groups=mesh['xh'=2,'z'=16,'c'=2,'y'=4,'xl'=2] {'xl'}, dimensions={0}, use_global_device_ids=true | all-gather | bytes 417792 | tf_op jit(solution)/shard_map/all_gather | solution.py:477
  70.4 1.8 %shard_map.79 = s16[32,2176]{1,0:T(8,128)(2,1)S(1)} custom-call(f32[2,272,128]{2,1,0:T(8,128)S(1)} %bitcast.11, f32[40,128]{1,0:T(8,128)S(1)} %get-tuple-element.24.index_ref, bf16[2,272,1024]{2,1,0:T(8,128)(2,1)S(1)} %shard_map.75.near_ref, bf16[2,272,1024]{2,1,0:T(8,128)(2,1)S(1)} %collective-permute-done.1.far_ref), custom_call_target="tpu_custom_call" | custom-call | tf_op jit(solution)/shard_map/pallas_call | solution.py:113
  72.2 0.1 reshape.21
  72.3 16.4 %all_to_all.28 = s16[16,2,2176]{2,1,0:T(2,128)(2,1)S(1)} all-to-all(s16[16,2,2176]{2,1,0:T(2,128)(2,1)S(1)} %reshape.21), channel_id=1, replica_groups=mesh['xh'=2,'z'=16,'c'=2,'y'=4,'xl'=2] {'z'}, dimensions={0} | all-to-all | bytes 278528 | tf_op jit(solution)/shard_map/all_to_all | solution.py:479
  88.7 0.1 reshape.22.parts_ref
  88.7 0.6 shard_map.80
  89.3 8.6 %all_to_all.29.sums_ref = f32[8,8,128]{2,1,0:T(8,128)S(1)} all-to-all(f32[8,8,128]{2,1,0:T(8,128)S(1)} %get-tuple-element.26), channel_id=1, replica_groups=mesh['xh'=2,'z'=16,'c'=2,'y'=4,'xl'=2] {'y','xl'}, dimensions={0} | all-to-all | bytes 65536 | tf_op jit(solution)/shard_map/all_to_all | solution.py:483
  97.9 1.0 shard_map.81
  (1 shorter events, 0.0 us)
Async XLA Ops:
  0.0 19.4 %copy-start.2 = (f32[1024]{0:T(1024)S(1)}, f32[1024]{0:T(1024)}, u32[]{:S(2)}) copy-start(f32[1024]{0:T(1024)} %param.8) | copy-start | bytes 12292
  0.0 19.4 %copy-start = (bf16[2,64,1024]{2,1,0:T(8,128)(2,1)S(1)}, bf16[2,64,1024]{2,1,0:T(8,128)(2,1)}, u32[]{:S(2)}) copy-start(bf16[2,64,1024]{2,1,0:T(8,128)(2,1)} %param.7) | copy-start | bytes 786436
  2.4 44.2 %copy-start.1 = (bf16[272,1024]{1,0:T(8,128)(2,1)S(1)}, bf16[272,1024]{1,0:T(8,128)(2,1)}, u32[]{:S(2)}) copy-start(bf16[272,1024]{1,0:T(8,128)(2,1)} %get-tuple-element.21.own_ref) | copy-start | bytes 1671172
  14.8 31.8 %collective-permute-start = (bf16[272,1024]{1,0:T(8,128)(2,1)}, bf16[272,1024]{1,0:T(8,128)(2,1)S(1)}, u32[]{:S(2)}, u32[]{:S(2)}) collective-permute-start(bf16[272,1024]{1,0:T(8,128)(2,1)} %get-tuple-element.21.own_ref), channel_id=1, source_target_pairs={{0,256},{256,0},{1,257},{257,1},{2,258},{258,2},{3,259},{259,3},{4... | collective-permute-start | bytes 1671176 | tf_op jit(solution)/shard_map/ppermute | solution.py:463
  46.6 2.0 %copy-start.3 = (s32[128,16]{0,1:T(8,128)S(1)}, s32[128,16]{0,1:T(8,128)}, u32[]{:S(2)}) copy-start(s32[128,16]{0,1:T(8,128)} %param.12) | copy-start | bytes 24580
  46.6 2.0 %copy-start.4 = (f32[128,16]{0,1:T(8,128)S(1)}, f32[128,16]{0,1:T(8,128)}, u32[]{:S(2)}) copy-start(f32[128,16]{0,1:T(8,128)} %param.13) | copy-start | bytes 24580
  46.6 2.1 %copy-start.5 = (s32[128]{0:T(128)S(1)}, s32[128]{0:T(128)}, u32[]{:S(2)}) copy-start(s32[128]{0:T(128)} %param.11) | copy-start | bytes 1540
  46.7 4.6 %collective-permute-start.1 = (bf16[2,272,1024]{2,1,0:T(8,128)(2,1)S(1)}, bf16[2,272,1024]{2,1,0:T(8,128)(2,1)S(1)}, u32[]{:S(2)}, u32[]{:S(2)}) collective-permute-start(bf16[2,272,1024]{2,1,0:T(8,128)(2,1)S(1)} %shard_map.75.near_ref), channel_id=1, source_target_pairs={{0,8},{8,0},{1,9},{9,1},{2,10},{10,2},{3,11},{11,3},{4,12},{12,4},... | collective-permute-start | bytes 3342344 | tf_op jit(solution)/shard_map/ppermute | solution.py:469

commit v5 on v4

--- a/solution.py
+++ b/solution.py
@@ -1,4 +1,5 @@
 import functools
+import math
 
 import jax
 import jax.numpy as jnp
@@ -27,6 +28,8 @@
 ABSENT = -30000.0
 FINE = 65536.0
 FULL = 32000.0
+SENT = ROWS + 48
+MOST = 0.5
 PIPE = ("y", "xl")
 VMEM = 24 << 20
 
@@ -230,18 +233,56 @@
     out_ref[ROWS + 8:] = jnp.concatenate(squares * 2, axis=0)
 
 
-def far_kernel(part_ref, queries_ref, far_ref, out_ref):
+def pieces_of(values):
+    whole_part = jnp.floor(values)
+    rest = (values - whole_part) * FINE
+    middle = jnp.floor(rest)
+    last = jnp.floor((rest - middle) * FINE)
+    return whole_part, middle - 32768.0, last - 32768.0
+
+
+def value_of(whole_part, middle, last):
+    return whole_part + (middle + 32768.0 + (last + 32768.0) / FINE) / FINE
+
+
+def far_kernel(part_ref, queries_ref, far_ref, out_ref, exact_ref):
     dots, squares = bank_dots(far_ref, queries_ref[...])
     dots = jnp.concatenate([d[:ROWS + 8] for d in dots] * 2, axis=1)
     dots = jnp.where(iota((ROWS + 8, 128), 1) < 2 * OWN, part_ref[:ROWS + 8], dots)
     squares = jnp.concatenate([part_ref[ROWS + 8:ROWS + 12]] + squares, axis=0)
-    for peer in range(4):
-        out_ref[peer, :ROWS + 8] = dots
-        out_ref[peer, ROWS + 8:] = squares
-
-
-def sum_kernel(parts_ref, out_ref):
-    out_ref[...] = (parts_ref[0] + parts_ref[1]) + (parts_ref[2] + parts_ref[3])
+    exact_ref[:ROWS + 8] = dots
+    exact_ref[ROWS + 8:] = squares
+    most = jnp.maximum(jnp.max(jnp.abs(dots), axis=0, keepdims=True), 1e-30)
+    level = jnp.floor(jnp.log(most) * FINE + 0.5) / FINE
+    coded = jnp.floor(dots * (FULL * jnp.exp(-level)) + 0.5)
+    scale = jnp.concatenate(list(pieces_of(level)) + [jnp.zeros((13, 128), f32)], axis=0)
+    tail = jnp.concatenate([coded[ROWS:]] + list(pieces_of(squares)) + [scale], axis=0)
+    coded = coded[:ROWS].astype(jnp.int32).astype(jnp.int16)
+    tail = tail.astype(jnp.int32).astype(jnp.int16)
+    for peer in range(8):
+        out_ref[peer, :ROWS] = coded
+        out_ref[peer, ROWS:] = tail
+
+
+def levels_of(coded_ref):
+    levels = []
+    for peer in range(8):
+        tail = coded_ref[peer, ROWS:].astype(jnp.int32).astype(f32)
+        levels.append(value_of(tail[32:33], tail[33:34], tail[34:35]))
+    return levels, jnp.max(functools.reduce(jnp.maximum, levels), axis=1, keepdims=True) > math.log(MOST)
+
+
+def decoded(coded_ref):
+    levels, over = levels_of(coded_ref)
+    queue_dots = jnp.zeros((ROWS, 128), f32)
+    rest = jnp.zeros((16, 128), f32)
+    for peer in range(8):
+        tail = coded_ref[peer, ROWS:].astype(jnp.int32).astype(f32)
+        factor = jnp.exp(levels[peer]) / FULL
+        queue_dots = queue_dots + coded_ref[peer, :ROWS].astype(jnp.int32).astype(f32) * factor
+        squares = value_of(tail[8:16], tail[16:24], tail[24:32])
+        rest = rest + jnp.concatenate([tail[:8] * factor, squares], axis=0)
+    return jnp.concatenate([queue_dots, rest], axis=0), over
 
 
 def quantized(rows):
@@ -256,8 +297,16 @@
     return jnp.where(shard // 2 % 16 == lax.axis_index("z"), across + 2 * beside, -1)
 
 
-def grad_kernel(dots_ref, index_ref, near_ref, far_ref, out_ref):
-    dots = dots_ref[0] + dots_ref[1]
+def coded_grad_kernel(coded_ref, index_ref, near_ref, far_ref, out_ref):
+    dots, over = decoded(coded_ref)
+    grad_parts(dots, jnp.where(over, 1.0, 0.0), index_ref, near_ref, far_ref, out_ref)
+
+
+def exact_grad_kernel(dots_ref, index_ref, near_ref, far_ref, out_ref):
+    grad_parts(dots_ref[...], jnp.zeros((1, 1), f32), index_ref, near_ref, far_ref, out_ref)
+
+
+def grad_parts(dots, over, index_ref, near_ref, far_ref, out_ref):
     queue_dots = dots[:ROWS]
     key_dots = dots[ROWS:ROWS + 8]
     group = iota((1, 128), 1) // OWN
@@ -346,7 +395,7 @@
     out_ref[:, PART:2 * PART], key_level = quantized(extras[2 * OWN:])
     rows = jnp.concatenate([top, mass, positive, jnp.zeros((5, 128), f32)], axis=0)
     stats = spread(rows, jnp.where(iota((1, 128), 1) < 3, iota((1, 128), 1), -1))[:OWN]
-    stats = jnp.where(lane == 3, level, jnp.where(lane == 4, key_level, stats))
+    stats = jnp.where(lane == 3, level, jnp.where(lane == 4, key_level, jnp.where(lane == 5, over, stats)))
     pieces = jnp.floor(stats)
     rest = (stats - pieces) * FINE
     middle = jnp.floor(rest)
@@ -406,23 +455,31 @@
     of_query = jnp.where(first, dots[2:3], dots[3:4])
     of_along = jnp.where(first, along[0:1], along[1:2])
     row = iota((8, 128), 0)
-    block = jnp.where(row == 0, of_grad, jnp.where(row == 1, of_query, of_along))
+    over = jnp.max(stats[:, 5:6], axis=0, keepdims=True)
+    block = jnp.where(
+        row == 0, of_grad, jnp.where(row == 1, of_query, jnp.where(row == 2, of_along, over))
+    )
     for peer in range(8):
         out_ref[peer] = block
 
 
-def output_kernel(sums_ref, grad_ref, query_ref, stat_ref, hidden_ref, gain_ref, out_far, out_ref, sems):
+def output_kernel(
+    sums_ref, grad_ref, query_ref, stat_ref, hidden_ref, gain_ref, out_far, over_far, out_ref, over_ref, sems
+):
     total = sums_ref[0]
     for peer in range(1, 8):
         total = total + sums_ref[peer]
     inverse = stat_ref[0:1]
     length = stat_ref[1:2]
     along = total[2:3]
+    over_ref[0] = (jnp.max(total[3:4]) > 0.5).astype(jnp.int32)
+    mark = pltpu.make_async_copy(over_ref, over_far, sems.at[2])
+    mark.start()
     inner = inverse * (total[0:1] - along * total[1:2]) / (length * WIDTH)
     inverse_column = column(inverse)
     slide = column(inverse * inverse * inner) / SEQ
     gain = gain_ref[...]
-    copies = []
+    copies = [mark]
     for q in range(2):
         at = q * SEQ
         scaled = (
@@ -472,19 +529,32 @@
         gathered, near, mix_rows.T, mix_weight.T, positive.reshape(1, QUERIES),
         scratch=[pltpu.VMEM((OWN * CHUNKS, 128), f32)],
     )
-    dots = call(far_kernel, shape((4, BANK, 128)), dots, queries, far)
-    dots = lax.all_to_all(dots, "y", 0, 0)
-    dots = lax.all_gather(call(sum_kernel, shape((BANK, 128)), dots), "xl")
-    parts = call(grad_kernel, shape((OWN, EXT), jnp.int16), dots, index, near, far)
-    parts = lax.all_to_all(parts.reshape(16, 2, EXT), "z", 0, 0).reshape(OWN, EXT)
-    sums, grad = call(
-        inner_kernel, [shape((8, 8, 128)), shape((2, PART))], parts, query, tokens, gain
-    )
-    sums = lax.all_to_all(sums, PIPE, 0, 0)
-    out = call(
-        output_kernel, shape((TOKENS, PART)), sums, grad, query, stat, tokens, gain, far_outs=(0,),
-        scratch=[pltpu.VMEM((TOKENS, PART), f32), pltpu.SemaphoreType.DMA((2,))],
-    )
+    coded, exact = call(
+        far_kernel, [shape((8, SENT, 128), jnp.int16), shape((BANK, 128))], dots, queries, far
+    )
+    coded = lax.all_to_all(coded, PIPE, 0, 0)
+    parts = call(coded_grad_kernel, shape((OWN, EXT), jnp.int16), coded, index, near, far)
+
+    def finish(parts):
+        parts = lax.all_to_all(parts.reshape(16, 2, EXT), "z", 0, 0).reshape(OWN, EXT)
+        sums, grad = call(
+            inner_kernel, [shape((8, 8, 128)), shape((2, PART))], parts, query, tokens, gain
+        )
+        sums = lax.all_to_all(sums, PIPE, 0, 0)
+        return call(
+            output_kernel, [shape((TOKENS, PART)), shape((1,), jnp.int32)],
+            sums, grad, query, stat, tokens, gain, far_outs=(0, 1),
+            scratch=[
+                pltpu.VMEM((TOKENS, PART), f32), pltpu.SMEM((1,), jnp.int32), pltpu.SemaphoreType.DMA((3,))
+            ],
+        )
+
+    def repeat(state):
+        dots = jnp.sum(lax.all_to_all(jnp.broadcast_to(state[2], (8, BANK, 128)), PIPE, 0, 0), axis=0)
+        parts = call(exact_grad_kernel, shape((OWN, EXT), jnp.int16), dots, index, near, far)
+        return (*finish(parts), dots)
+
+    out = lax.while_loop(lambda state: state[1][0] > 0, repeat, (*finish(parts), exact))[0]
     return out.reshape(2, SEQ, PART)
 
 

time: 99.5 us -> 145 us (1.46)
  blocking collectives: 82.7 us -> 123 us
  Pallas kernels: 7.3 us -> 10.9 us
    all_to_all x3 -> x6, blocking collectives: 37.8 us -> 83.6 us  [the longest x2 36.6 us: finish(): lax.all_to_all(parts.reshape(16, 2, EXT), 'z', 0, 0).reshape(OWN, EXT)]
    all_gather x1 -> x0, blocking collectives: 5.73 us -> none  [shards(): dots = lax.all_gather(call(sum_kernel, shape((BANK, 128)), dots), 'xl')]
    pallas_call x9 -> x11, Pallas kernels: 7.3 us -> 10.9 us  [call(): pl.pallas_call(kernel, out_shape=outs, in_specs=[place(i, far) for i in r...]
where the time goes in v5:
time: 145 us; the launch traced here: 144 us
  blocking collectives  123 us (85%)
  Pallas kernels  10.9 us (8%)
  starting transfers between devices  6.55 us (5%)
  waiting for transfers between devices  2.07 us (1%)
    all_to_all x2, blocking collectives, finish(): lax.all_to_all(parts.reshape(16, 2, EXT), 'z', 0, 0).reshape(OWN, EXT)  36.6 us
    all_to_all x1, blocking collectives, shards(): gathered = lax.all_to_all(payload, 'z', 0, 0)  26.8 us
    all_to_all x2, blocking collectives, finish(): sums = lax.all_to_all(sums, PIPE, 0, 0)  17.9 us
    all_to_all x1, blocking collectives, repeat(): lax.all_to_all(jnp.broadcast_to(state[2], (8, BANK, 128)), PIPE, 0, 0)  14.8 us
    all_to_all x1, blocking collectives, shards(): coded = lax.all_to_all(coded, PIPE, 0, 0)  14.2 us
    all_to_all x1, blocking collectives, shards(): squares = lax.all_to_all(squares, PIPE, 0, 0)  12.4 us
    pallas_call x11, Pallas kernels, call(): pl.pallas_call(kernel, out_shape=outs, in_specs=[place(i, far) for i in r...  10.9 us
    ppermute x1, starting transfers between devices, shards(): came = lax.ppermute(own, 'xh', swap)  4.63 us
  transfers between devices with their start and end apart: 2, of which 1 were waited for; matrix products, arithmetic and copies ran while one was open for 0% of the time, Pallas kernels for 1%

profile of v5, /device:TPU:32, one launch (start us, length us, event | category | flops | bytes accessed | tf_op | source)
XLA Modules:
  0.0 144.0 jit_solution(4709395488130022902)
XLA Ops:
  0.0 0.0 copy-start.7
  0.0 0.0 copy-start.4
  0.0 2.4 %shard_map.73 = (f32[8,40,128]{2,1,0:T(8,128)}, bf16[272,1024]{1,0:T(8,128)(2,1)}) custom-call(bf16[128,1024]{1,0:T(8,128)(2,1)} %bitcast.11, bf16[256,1024]{1,0:T(8,128)(2,1)} %queue_far.1, f32[1,1024]{1,0:T(1,128)} %bitcast.19, bf16[2,1024]{1,0:T(2,128)(2,1)} %keys_far.1), custom_call_target="tpu_custom_call" | custom-call | tf_op jit(solution)/shard_map/pallas_call | solution.py:116
  2.4 0.0 copy-start
  2.4 12.4 %all_to_all.43.sums_ref = f32[8,40,128]{2,1,0:T(8,128)S(1)} all-to-all(f32[8,40,128]{2,1,0:T(8,128)} %get-tuple-element.76), channel_id=1, replica_groups=mesh['xh'=2,'z'=16,'c'=2,'y'=4,'xl'=2] {'y','xl'}, dimensions={0} | all-to-all | bytes 327680 | tf_op jit(solution)/shard_map/all_to_all | solution.py:518
  14.8 4.6 %collective-permute-start = (bf16[272,1024]{1,0:T(8,128)(2,1)}, bf16[272,1024]{1,0:T(8,128)(2,1)S(1)}, u32[]{:S(2)}, u32[]{:S(2)}) collective-permute-start(bf16[272,1024]{1,0:T(8,128)(2,1)} %get-tuple-element.79.own_ref), channel_id=1, source_target_pairs={{0,256},{256,0},{1,257},{257,1},{2,258},{258,2},{3,259},{259,3},{4... | collective-permute-start | bytes 1671176 | tf_op jit(solution)/shard_map/ppermute | solution.py:520
  19.4 0.0 copy-done.7
  19.4 0.0 copy-done.4
  19.5 0.3 shard_map.74
  19.7 26.8 %all_to_all.44.after_ref.gathered_ref = bf16[16,16,128]{2,1,0:T(8,128)(2,1)S(1)} all-to-all(bf16[16,16,128]{2,1,0:T(8,128)(2,1)S(1)} %get-tuple-element.78), channel_id=1, replica_groups=mesh['xh'=2,'z'=16,'c'=2,'y'=4,'xl'=2] {'z'}, dimensions={0} | all-to-all | bytes 131072 | tf_op jit(solution)/shard_map/all_to_all | solution.py:524
  46.6 0.0 copy-start.1
  46.6 0.0 copy-start.2
  46.6 0.0 copy-start.3
  46.6 0.0 collective-permute-done.came_ref
  46.6 0.0 copy-done
  46.6 0.1 shard_map.75.near_ref
  46.7 1.9 %collective-permute-start.1 = (bf16[2,272,1024]{2,1,0:T(8,128)(2,1)S(1)}, bf16[2,272,1024]{2,1,0:T(8,128)(2,1)S(1)}, u32[]{:S(2)}, u32[]{:S(2)}) collective-permute-start(bf16[2,272,1024]{2,1,0:T(8,128)(2,1)S(1)} %shard_map.75.near_ref), channel_id=1, source_target_pairs={{0,8},{8,0},{1,9},{9,1},{2,10},{10,2},{3,11},{11,3},{4,12},{12,4},... | collective-permute-start | bytes 3342344 | tf_op jit(solution)/shard_map/ppermute | solution.py:526
  48.6 0.0 copy-done.1
  48.6 0.0 copy-done.2
  48.6 0.0 copy-done.3
  48.6 0.6 shard_map.76
  49.3 2.1 %collective-permute-done.1.far_ref = bf16[2,272,1024]{2,1,0:T(8,128)(2,1)S(1)} collective-permute-done((bf16[2,272,1024]{2,1,0:T(8,128)(2,1)S(1)}, bf16[2,272,1024]{2,1,0:T(8,128)(2,1)S(1)}, u32[]{:S(2)}, u32[]{:S(2)}) %collective-permute-start.1) | collective-permute-done | bytes 1114144 | tf_op jit(solution)/shard_map/ppermute | solution.py:526
  51.3 0.7 shard_map.77
  52.0 14.2 %all_to_all.45.coded_ref = s16[8,304,128]{2,1,0:T(8,128)(2,1)S(1)} all-to-all(s16[8,304,128]{2,1,0:T(8,128)(2,1)S(1)} %get-tuple-element.82), channel_id=1, replica_groups=mesh['xh'=2,'z'=16,'c'=2,'y'=4,'xl'=2] {'y','xl'}, dimensions={0} | all-to-all | bytes 1245184 | tf_op jit(solution)/shard_map/all_to_all | solution.py:535
  66.3 0.0 copy-start.5
  66.3 1.9 %shard_map.78 = s16[32,2176]{1,0:T(8,128)(2,1)S(1)} custom-call(s16[8,304,128]{2,1,0:T(8,128)(2,1)S(1)} %all_to_all.45.coded_ref, f32[40,128]{1,0:T(8,128)S(1)} %get-tuple-element.180.index_ref, bf16[2,272,1024]{2,1,0:T(8,128)(2,1)S(1)} %shard_map.75.near_ref, bf16[2,272,1024]{2,1,0:T(8,128)(2,1)S(1)} %collective-permute-done.1.far_ref), custom_call_target="tpu_custom_call" | custom-call | tf_op jit(solution)/shard_map/pallas_call | solution.py:116
  68.2 0.1 reshape.29
  68.3 17.7 %all_to_all.46 = s16[16,2,2176]{2,1,0:T(2,128)(2,1)S(1)} all-to-all(s16[16,2,2176]{2,1,0:T(2,128)(2,1)S(1)} %reshape.29), channel_id=1, replica_groups=mesh['xh'=2,'z'=16,'c'=2,'y'=4,'xl'=2] {'z'}, dimensions={0} | all-to-all | bytes 278528 | tf_op jit(solution)/shard_map/all_to_all | solution.py:539
  85.9 0.1 reshape.30.parts_ref
  86.0 0.0 copy-done.5
  86.0 0.6 shard_map.79
  86.6 9.1 %all_to_all.47.sums_ref = f32[8,8,128]{2,1,0:T(8,128)S(1)} all-to-all(f32[8,8,128]{2,1,0:T(8,128)S(1)} %get-tuple-element.85), channel_id=1, replica_groups=mesh['xh'=2,'z'=16,'c'=2,'y'=4,'xl'=2] {'y','xl'}, dimensions={0} | all-to-all | bytes 65536 | tf_op jit(solution)/shard_map/all_to_all | solution.py:543
  95.7 1.0 shard_map.80
  96.7 47.4 %while.12 = (f32[128,1024]{1,0:T(8,128)}, s32[1]{0:T(128)}, f32[272,128]{1,0:T(8,128)S(1)}, f32[40,128]{1,0:T(8,128)S(1)}, bf16[2,272,1024]{2,1,0:T(8,128)(2,1)S...) while((f32[128,1024]{1,0:T(8,128)}, s32[1]{0:T(128)}, ...), condition=%wide.region_2.0_spmd, body=%wide.region_0.0_spmd.sunk | while | flops 243713 | bytes 6684809 | solution.py:557
  97.2 0.1 broadcast_in_dim.4
  97.3 14.8 %all_to_all.48 = f32[8,272,128]{2,1,0:T(8,128)S(1)} all-to-all(f32[8,272,128]{2,1,0:T(8,128)S(1)} %broadcast_in_dim.4), channel_id=1, replica_groups=mesh['xh'=2,'z'=16,'c'=2,'y'=4,'xl'=2] {'y','xl'}, dimensions={0} | all-to-all | bytes 2228224 | tf_op jit(solution)/shard_map/while/body/all_to_all | solution.py:553
  112.1 0.1 reduce_sum.10.dots_ref
  112.1 0.0 copy-start.6
  112.2 1.8 %body.3 = s16[32,2176]{1,0:T(8,128)(2,1)S(1)} custom-call(f32[272,128]{1,0:T(8,128)S(1)} %reduce_sum.10.dots_ref, f32[40,128]{1,0:T(8,128)S(1)} %get-tuple-element.202.index_ref, bf16[2,272,1024]{2,1,0:T(8,128)(2,1)S(1)} %get-tuple-element.203.near_ref, bf16[2,272,1024]{2,1,0:T(8,128)(2,1)S(1)} %get-tuple-element.204.far_ref), custom_call_target="tpu_custom_call" | custom-call | tf_op jit(solution)/shard_map/while/body/pallas_call | solution.py:116
  113.9 0.1 reshape.34
  114.0 19.0 %all_to_all.49 = s16[16,2,2176]{2,1,0:T(2,128)(2,1)S(1)} all-to-all(s16[16,2,2176]{2,1,0:T(2,128)(2,1)S(1)} %reshape.34), channel_id=1, replica_groups=mesh['xh'=2,'z'=16,'c'=2,'y'=4,'xl'=2] {'z'}, dimensions={0} | all-to-all | bytes 278528 | tf_op jit(solution)/shard_map/while/body/all_to_all | solution.py:539
  133.0 0.1 reshape.35.parts_ref
  133.0 0.0 copy-done.6
  133.1 0.6 body.4
  133.6 8.9 %all_to_all.50.sums_ref = f32[8,8,128]{2,1,0:T(8,128)S(1)} all-to-all(f32[8,8,128]{2,1,0:T(8,128)S(1)} %get-tuple-element.173), channel_id=1, replica_groups=mesh['xh'=2,'z'=16,'c'=2,'y'=4,'xl'=2] {'y','xl'}, dimensions={0} | all-to-all | bytes 65536 | tf_op jit(solution)/shard_map/while/body/all_to_all | solution.py:543
  142.5 1.0 body.5
Async XLA Ops:
  0.0 19.4 %copy-start.7 = (f32[1024]{0:T(1024)S(1)}, f32[1024]{0:T(1024)}, u32[]{:S(2)}) copy-start(f32[1024]{0:T(1024)} %param.10) | copy-start | bytes 12292
  0.0 19.4 %copy-start.4 = (bf16[2,64,1024]{2,1,0:T(8,128)(2,1)S(1)}, bf16[2,64,1024]{2,1,0:T(8,128)(2,1)}, u32[]{:S(2)}) copy-start(bf16[2,64,1024]{2,1,0:T(8,128)(2,1)} %param.9) | copy-start | bytes 786436
  2.4 44.2 %copy-start = (bf16[272,1024]{1,0:T(8,128)(2,1)S(1)}, bf16[272,1024]{1,0:T(8,128)(2,1)}, u32[]{:S(2)}) copy-start(bf16[272,1024]{1,0:T(8,128)(2,1)} %get-tuple-element.79.own_ref) | copy-start | bytes 1671172
  14.8 31.8 %collective-permute-start = (bf16[272,1024]{1,0:T(8,128)(2,1)}, bf16[272,1024]{1,0:T(8,128)(2,1)S(1)}, u32[]{:S(2)}, u32[]{:S(2)}) collective-permute-start(bf16[272,1024]{1,0:T(8,128)(2,1)} %get-tuple-element.79.own_ref), channel_id=1, source_target_pairs={{0,256},{256,0},{1,257},{257,1},{2,258},{258,2},{3,259},{259,3},{4... | collective-permute-start | bytes 1671176 | tf_op jit(solution)/shard_map/ppermute | solution.py:520
  46.6 2.0 %copy-start.1 = (s32[128,16]{0,1:T(8,128)S(1)}, s32[128,16]{0,1:T(8,128)}, u32[]{:S(2)}) copy-start(s32[128,16]{0,1:T(8,128)} %param.14) | copy-start | bytes 24580
  46.6 2.0 %copy-start.2 = (f32[128,16]{0,1:T(8,128)S(1)}, f32[128,16]{0,1:T(8,128)}, u32[]{:S(2)}) copy-start(f32[128,16]{0,1:T(8,128)} %param.15) | copy-start | bytes 24580
  46.6 2.1 %copy-start.3 = (s32[128]{0:T(128)S(1)}, s32[128]{0:T(128)}, u32[]{:S(2)}) copy-start(s32[128]{0:T(128)} %param.13) | copy-start | bytes 1540
  46.7 4.6 %collective-permute-start.1 = (bf16[2,272,1024]{2,1,0:T(8,128)(2,1)S(1)}, bf16[2,272,1024]{2,1,0:T(8,128)(2,1)S(1)}, u32[]{:S(2)}, u32[]{:S(2)}) collective-permute-start(bf16[2,272,1024]{2,1,0:T(8,128)(2,1)S(1)} %shard_map.75.near_ref), channel_id=1, source_target_pairs={{0,8},{8,0},{1,9},{9,1},{2,10},{10,2},{3,11},{11,3},{4,12},{12,4},... | collective-permute-start | bytes 3342344 | tf_op jit(solution)/shard_map/ppermute | solution.py:526
  66.3 19.7 %copy-start.5 = (bf16[2,64,1024]{2,1,0:T(8,128)(2,1)S(1)}, bf16[2,64,1024]{2,1,0:T(8,128)(2,1)}, u32[]{:S(2)}) copy-start(bf16[2,64,1024]{2,1,0:T(8,128)(2,1)} %param.9) | copy-start | bytes 786436
  112.1 20.9 %copy-start.6 = (bf16[2,64,1024]{2,1,0:T(8,128)(2,1)S(1)}, bf16[2,64,1024]{2,1,0:T(8,128)(2,1)}, u32[]{:S(2)}) copy-start(bf16[2,64,1024]{2,1,0:T(8,128)(2,1)} %get-tuple-element.225) | copy-start | bytes 786436 | tf_op jit(solution)/shard_map/while

commit v6 on v5

--- a/solution.py
+++ b/solution.py
@@ -28,7 +28,7 @@
 ABSENT = -30000.0
 FINE = 65536.0
 FULL = 32000.0
-SENT = ROWS + 48
+SENT = ROWS + 32
 MOST = 0.5
 PIPE = ("y", "xl")
 VMEM = 24 << 20
@@ -255,8 +255,9 @@
     most = jnp.maximum(jnp.max(jnp.abs(dots), axis=0, keepdims=True), 1e-30)
     level = jnp.floor(jnp.log(most) * FINE + 0.5) / FINE
     coded = jnp.floor(dots * (FULL * jnp.exp(-level)) + 0.5)
-    scale = jnp.concatenate(list(pieces_of(level)) + [jnp.zeros((13, 128), f32)], axis=0)
-    tail = jnp.concatenate([coded[ROWS:]] + list(pieces_of(squares)) + [scale], axis=0)
+    scale = list(pieces_of(level)[:2])
+    tail = list(pieces_of(squares)) + [coded[ROWS:ROWS + 2]] + scale + [jnp.zeros((4, 128), f32)]
+    tail = jnp.concatenate(tail, axis=0)
     coded = coded[:ROWS].astype(jnp.int32).astype(jnp.int16)
     tail = tail.astype(jnp.int32).astype(jnp.int16)
     for peer in range(8):
@@ -268,7 +269,7 @@
     levels = []
     for peer in range(8):
         tail = coded_ref[peer, ROWS:].astype(jnp.int32).astype(f32)
-        levels.append(value_of(tail[32:33], tail[33:34], tail[34:35]))
+        levels.append(tail[26:27] + (tail[27:28] + 32768.0) / FINE)
     return levels, jnp.max(functools.reduce(jnp.maximum, levels), axis=1, keepdims=True) > math.log(MOST)
 
 
@@ -280,8 +281,8 @@
         tail = coded_ref[peer, ROWS:].astype(jnp.int32).astype(f32)
         factor = jnp.exp(levels[peer]) / FULL
         queue_dots = queue_dots + coded_ref[peer, :ROWS].astype(jnp.int32).astype(f32) * factor
-        squares = value_of(tail[8:16], tail[16:24], tail[24:32])
-        rest = rest + jnp.concatenate([tail[:8] * factor, squares], axis=0)
+        squares = value_of(tail[:8], tail[8:16], tail[16:24])
+        rest = rest + jnp.concatenate([tail[24:] * factor, squares], axis=0)
     return jnp.concatenate([queue_dots, rest], axis=0), over
 
 

time: 145 us -> 145 us (level)
  no operation moved by 1% of the time
where the time goes in v6:
time: 145 us
  blocking collectives  123 us (85%)
  Pallas kernels  10.9 us (8%)
  starting transfers between devices  6.55 us (5%)
  waiting for transfers between devices  2.07 us (1%)
    all_to_all x2, blocking collectives, finish(): lax.all_to_all(parts.reshape(16, 2, EXT), 'z', 0, 0).reshape(OWN, EXT)  36.9 us
    all_to_all x1, blocking collectives, shards(): gathered = lax.all_to_all(payload, 'z', 0, 0)  26.8 us
    all_to_all x2, blocking collectives, finish(): sums = lax.all_to_all(sums, PIPE, 0, 0)  18.1 us
    all_to_all x1, blocking collectives, repeat(): lax.all_to_all(jnp.broadcast_to(state[2], (8, BANK, 128)), PIPE, 0, 0)  15.3 us
    all_to_all x1, blocking collectives, shards(): coded = lax.all_to_all(coded, PIPE, 0, 0)  13.9 us
    all_to_all x1, blocking collectives, shards(): squares = lax.all_to_all(squares, PIPE, 0, 0)  12.4 us
    pallas_call x11, Pallas kernels, call(): pl.pallas_call(kernel, out_shape=outs, in_specs=[place(i, far) for i in r...  10.9 us
    ppermute x1, starting transfers between devices, shards(): came = lax.ppermute(own, 'xh', swap)  4.63 us
  transfers between devices with their start and end apart: 2, of which 1 were waited for; matrix products, arithmetic and copies ran while one was open for 0% of the time, Pallas kernels for 1%

profile of v6, /device:TPU:32, one launch (start us, length us, event | category | flops | bytes accessed | tf_op | source)
XLA Modules:
  0.0 144.5 jit_solution(13247356481046446440)
XLA Ops:
  0.0 0.0 copy-start.7
  0.0 0.0 copy-start.4
  0.0 2.4 %shard_map.73 = (f32[8,40,128]{2,1,0:T(8,128)}, bf16[272,1024]{1,0:T(8,128)(2,1)}) custom-call(bf16[128,1024]{1,0:T(8,128)(2,1)} %bitcast.11, bf16[256,1024]{1,0:T(8,128)(2,1)} %queue_far.1, f32[1,1024]{1,0:T(1,128)} %bitcast.19, bf16[2,1024]{1,0:T(2,128)(2,1)} %keys_far.1), custom_call_target="tpu_custom_call" | custom-call | tf_op jit(solution)/shard_map/pallas_call | solution.py:116
  2.4 0.0 copy-start
  2.4 12.4 %all_to_all.43.sums_ref = f32[8,40,128]{2,1,0:T(8,128)S(1)} all-to-all(f32[8,40,128]{2,1,0:T(8,128)} %get-tuple-element.76), channel_id=1, replica_groups=mesh['xh'=2,'z'=16,'c'=2,'y'=4,'xl'=2] {'y','xl'}, dimensions={0} | all-to-all | bytes 327680 | tf_op jit(solution)/shard_map/all_to_all | solution.py:519
  14.8 4.6 %collective-permute-start = (bf16[272,1024]{1,0:T(8,128)(2,1)}, bf16[272,1024]{1,0:T(8,128)(2,1)S(1)}, u32[]{:S(2)}, u32[]{:S(2)}) collective-permute-start(bf16[272,1024]{1,0:T(8,128)(2,1)} %get-tuple-element.79.own_ref), channel_id=1, source_target_pairs={{0,256},{256,0},{1,257},{257,1},{2,258},{258,2},{3,259},{259,3},{4... | collective-permute-start | bytes 1671176 | tf_op jit(solution)/shard_map/ppermute | solution.py:521
  19.4 0.0 copy-done.7
  19.4 0.0 copy-done.4
  19.5 0.3 shard_map.74
  19.7 26.8 %all_to_all.44.after_ref.gathered_ref = bf16[16,16,128]{2,1,0:T(8,128)(2,1)S(1)} all-to-all(bf16[16,16,128]{2,1,0:T(8,128)(2,1)S(1)} %get-tuple-element.78), channel_id=1, replica_groups=mesh['xh'=2,'z'=16,'c'=2,'y'=4,'xl'=2] {'z'}, dimensions={0} | all-to-all | bytes 131072 | tf_op jit(solution)/shard_map/all_to_all | solution.py:525
  46.6 0.0 copy-start.1
  46.6 0.0 copy-start.2
  46.6 0.0 copy-start.3
  46.6 0.0 collective-permute-done.came_ref
  46.6 0.0 copy-done
  46.6 0.1 shard_map.75.near_ref
  46.7 1.9 %collective-permute-start.1 = (bf16[2,272,1024]{2,1,0:T(8,128)(2,1)S(1)}, bf16[2,272,1024]{2,1,0:T(8,128)(2,1)S(1)}, u32[]{:S(2)}, u32[]{:S(2)}) collective-permute-start(bf16[2,272,1024]{2,1,0:T(8,128)(2,1)S(1)} %shard_map.75.near_ref), channel_id=1, source_target_pairs={{0,8},{8,0},{1,9},{9,1},{2,10},{10,2},{3,11},{11,3},{4,12},{12,4},... | collective-permute-start | bytes 3342344 | tf_op jit(solution)/shard_map/ppermute | solution.py:527
  48.6 0.0 copy-done.1
  48.6 0.0 copy-done.2
  48.6 0.0 copy-done.3
  48.6 0.6 shard_map.76
  49.3 2.1 %collective-permute-done.1.far_ref = bf16[2,272,1024]{2,1,0:T(8,128)(2,1)S(1)} collective-permute-done((bf16[2,272,1024]{2,1,0:T(8,128)(2,1)S(1)}, bf16[2,272,1024]{2,1,0:T(8,128)(2,1)S(1)}, u32[]{:S(2)}, u32[]{:S(2)}) %collective-permute-start.1) | collective-permute-done | bytes 1114144 | tf_op jit(solution)/shard_map/ppermute | solution.py:527
  51.3 0.7 shard_map.77
  52.0 13.9 %all_to_all.45.coded_ref = s16[8,288,128]{2,1,0:T(8,128)(2,1)S(1)} all-to-all(s16[8,288,128]{2,1,0:T(8,128)(2,1)S(1)} %get-tuple-element.82), channel_id=1, replica_groups=mesh['xh'=2,'z'=16,'c'=2,'y'=4,'xl'=2] {'y','xl'}, dimensions={0} | all-to-all | bytes 1179648 | tf_op jit(solution)/shard_map/all_to_all | solution.py:536
  65.9 0.0 copy-start.5
  65.9 1.9 %shard_map.78 = s16[32,2176]{1,0:T(8,128)(2,1)S(1)} custom-call(s16[8,288,128]{2,1,0:T(8,128)(2,1)S(1)} %all_to_all.45.coded_ref, f32[40,128]{1,0:T(8,128)S(1)} %get-tuple-element.180.index_ref, bf16[2,272,1024]{2,1,0:T(8,128)(2,1)S(1)} %shard_map.75.near_ref, bf16[2,272,1024]{2,1,0:T(8,128)(2,1)S(1)} %collective-permute-done.1.far_ref), custom_call_target="tpu_custom_call" | custom-call | tf_op jit(solution)/shard_map/pallas_call | solution.py:116
  67.8 0.1 reshape.29
  67.9 17.6 %all_to_all.46 = s16[16,2,2176]{2,1,0:T(2,128)(2,1)S(1)} all-to-all(s16[16,2,2176]{2,1,0:T(2,128)(2,1)S(1)} %reshape.29), channel_id=1, replica_groups=mesh['xh'=2,'z'=16,'c'=2,'y'=4,'xl'=2] {'z'}, dimensions={0} | all-to-all | bytes 278528 | tf_op jit(solution)/shard_map/all_to_all | solution.py:540
  85.5 0.1 reshape.30.parts_ref
  85.5 0.0 copy-done.5
  85.6 0.6 shard_map.79
  86.1 9.2 %all_to_all.47.sums_ref = f32[8,8,128]{2,1,0:T(8,128)S(1)} all-to-all(f32[8,8,128]{2,1,0:T(8,128)S(1)} %get-tuple-element.85), channel_id=1, replica_groups=mesh['xh'=2,'z'=16,'c'=2,'y'=4,'xl'=2] {'y','xl'}, dimensions={0} | all-to-all | bytes 65536 | tf_op jit(solution)/shard_map/all_to_all | solution.py:544
  95.3 1.0 shard_map.80
  96.3 48.3 %while.12 = (f32[128,1024]{1,0:T(8,128)}, s32[1]{0:T(128)}, f32[272,128]{1,0:T(8,128)S(1)}, f32[40,128]{1,0:T(8,128)S(1)}, bf16[2,272,1024]{2,1,0:T(8,128)(2,1)S...) while((f32[128,1024]{1,0:T(8,128)}, s32[1]{0:T(128)}, ...), condition=%wide.region_2.0_spmd, body=%wide.region_0.0_spmd.sunk | while | flops 243713 | bytes 6684809 | solution.py:558
  96.8 0.1 broadcast_in_dim.4
  96.9 15.3 %all_to_all.48 = f32[8,272,128]{2,1,0:T(8,128)S(1)} all-to-all(f32[8,272,128]{2,1,0:T(8,128)S(1)} %broadcast_in_dim.4), channel_id=1, replica_groups=mesh['xh'=2,'z'=16,'c'=2,'y'=4,'xl'=2] {'y','xl'}, dimensions={0} | all-to-all | bytes 2228224 | tf_op jit(solution)/shard_map/while/body/all_to_all | solution.py:554
  112.2 0.1 reduce_sum.10.dots_ref
  112.3 0.0 copy-start.6
  112.3 1.8 %body.3 = s16[32,2176]{1,0:T(8,128)(2,1)S(1)} custom-call(f32[272,128]{1,0:T(8,128)S(1)} %reduce_sum.10.dots_ref, f32[40,128]{1,0:T(8,128)S(1)} %get-tuple-element.202.index_ref, bf16[2,272,1024]{2,1,0:T(8,128)(2,1)S(1)} %get-tuple-element.203.near_ref, bf16[2,272,1024]{2,1,0:T(8,128)(2,1)S(1)} %get-tuple-element.204.far_ref), custom_call_target="tpu_custom_call" | custom-call | tf_op jit(solution)/shard_map/while/body/pallas_call | solution.py:116
  114.1 0.1 reshape.34
  114.2 19.3 %all_to_all.49 = s16[16,2,2176]{2,1,0:T(2,128)(2,1)S(1)} all-to-all(s16[16,2,2176]{2,1,0:T(2,128)(2,1)S(1)} %reshape.34), channel_id=1, replica_groups=mesh['xh'=2,'z'=16,'c'=2,'y'=4,'xl'=2] {'z'}, dimensions={0} | all-to-all | bytes 278528 | tf_op jit(solution)/shard_map/while/body/all_to_all | solution.py:540
  133.4 0.1 reshape.35.parts_ref
  133.5 0.0 copy-done.6
  133.5 0.6 body.4
  134.1 8.9 %all_to_all.50.sums_ref = f32[8,8,128]{2,1,0:T(8,128)S(1)} all-to-all(f32[8,8,128]{2,1,0:T(8,128)S(1)} %get-tuple-element.173), channel_id=1, replica_groups=mesh['xh'=2,'z'=16,'c'=2,'y'=4,'xl'=2] {'y','xl'}, dimensions={0} | all-to-all | bytes 65536 | tf_op jit(solution)/shard_map/while/body/all_to_all | solution.py:544
  143.0 1.0 body.5
Async XLA Ops:
  0.0 19.4 %copy-start.7 = (f32[1024]{0:T(1024)S(1)}, f32[1024]{0:T(1024)}, u32[]{:S(2)}) copy-start(f32[1024]{0:T(1024)} %param.10) | copy-start | bytes 12292
  0.0 19.4 %copy-start.4 = (bf16[2,64,1024]{2,1,0:T(8,128)(2,1)S(1)}, bf16[2,64,1024]{2,1,0:T(8,128)(2,1)}, u32[]{:S(2)}) copy-start(bf16[2,64,1024]{2,1,0:T(8,128)(2,1)} %param.9) | copy-start | bytes 786436
  2.4 44.2 %copy-start = (bf16[272,1024]{1,0:T(8,128)(2,1)S(1)}, bf16[272,1024]{1,0:T(8,128)(2,1)}, u32[]{:S(2)}) copy-start(bf16[272,1024]{1,0:T(8,128)(2,1)} %get-tuple-element.79.own_ref) | copy-start | bytes 1671172
  14.8 31.8 %collective-permute-start = (bf16[272,1024]{1,0:T(8,128)(2,1)}, bf16[272,1024]{1,0:T(8,128)(2,1)S(1)}, u32[]{:S(2)}, u32[]{:S(2)}) collective-permute-start(bf16[272,1024]{1,0:T(8,128)(2,1)} %get-tuple-element.79.own_ref), channel_id=1, source_target_pairs={{0,256},{256,0},{1,257},{257,1},{2,258},{258,2},{3,259},{259,3},{4... | collective-permute-start | bytes 1671176 | tf_op jit(solution)/shard_map/ppermute | solution.py:521
  46.6 2.0 %copy-start.1 = (s32[128,16]{0,1:T(8,128)S(1)}, s32[128,16]{0,1:T(8,128)}, u32[]{:S(2)}) copy-start(s32[128,16]{0,1:T(8,128)} %param.14) | copy-start | bytes 24580
  46.6 2.0 %copy-start.2 = (f32[128,16]{0,1:T(8,128)S(1)}, f32[128,16]{0,1:T(8,128)}, u32[]{:S(2)}) copy-start(f32[128,16]{0,1:T(8,128)} %param.15) | copy-start | bytes 24580
  46.6 2.1 %copy-start.3 = (s32[128]{0:T(128)S(1)}, s32[128]{0:T(128)}, u32[]{:S(2)}) copy-start(s32[128]{0:T(128)} %param.13) | copy-start | bytes 1540
  46.7 4.6 %collective-permute-start.1 = (bf16[2,272,1024]{2,1,0:T(8,128)(2,1)S(1)}, bf16[2,272,1024]{2,1,0:T(8,128)(2,1)S(1)}, u32[]{:S(2)}, u32[]{:S(2)}) collective-permute-start(bf16[2,272,1024]{2,1,0:T(8,128)(2,1)S(1)} %shard_map.75.near_ref), channel_id=1, source_target_pairs={{0,8},{8,0},{1,9},{9,1},{2,10},{10,2},{3,11},{11,3},{4,12},{12,4},... | collective-permute-start | bytes 3342344 | tf_op jit(solution)/shard_map/ppermute | solution.py:527
  65.9 19.7 %copy-start.5 = (bf16[2,64,1024]{2,1,0:T(8,128)(2,1)S(1)}, bf16[2,64,1024]{2,1,0:T(8,128)(2,1)}, u32[]{:S(2)}) copy-start(bf16[2,64,1024]{2,1,0:T(8,128)(2,1)} %param.9) | copy-start | bytes 786436
  112.3 21.2 %copy-start.6 = (bf16[2,64,1024]{2,1,0:T(8,128)(2,1)S(1)}, bf16[2,64,1024]{2,1,0:T(8,128)(2,1)}, u32[]{:S(2)}) copy-start(bf16[2,64,1024]{2,1,0:T(8,128)(2,1)} %get-tuple-element.225) | copy-start | bytes 786436 | tf_op jit(solution)/shard_map/while

commit v7 on v6

--- a/solution.py
+++ b/solution.py
@@ -129,17 +129,16 @@
     copies = [
         pltpu.make_async_copy(source, target, sems.at[i])
         for i, (source, target) in enumerate((
+            (hidden_far, hidden_ref),
+            (gain_far, gain_ref),
             (keys_far, keys_ref),
-            (gain_far, gain_ref),
-            (hidden_far, hidden_ref),
             (queue_far, bank_ref.at[pl.ds(0, ROWS)]),
         ))
     ]
     for copy in copies:
         copy.start()
-    for copy in copies[:-1]:
-        copy.wait()
-    bank_ref[ROWS:] = padded(keys_ref[...])
+    copies[0].wait()
+    copies[1].wait()
     x = hidden_ref[...]
     weighted = x.astype(f32) * (gain_ref[...] * gain_ref[...])
     hi, lo = split(weighted)
@@ -156,7 +155,9 @@
     for peer in range(8):
         out_ref[peer, :32] = packed
         out_ref[peer, 32:] = sums
-    copies[-1].wait()
+    copies[2].wait()
+    bank_ref[ROWS:] = padded(keys_ref[...])
+    copies[3].wait()
 
 
 def query_kernel(sums_ref, hidden_ref, gain_ref, payload_ref, query_ref, stat_ref):
@@ -474,7 +475,7 @@
     length = stat_ref[1:2]
     along = total[2:3]
     over_ref[0] = (jnp.max(total[3:4]) > 0.5).astype(jnp.int32)
-    mark = pltpu.make_async_copy(over_ref, over_far, sems.at[2])
+    mark = pltpu.make_async_copy(over_ref, over_far, sems.at[0])
     mark.start()
     inner = inverse * (total[0:1] - along * total[1:2]) / (length * WIDTH)
     inverse_column = column(inverse)
@@ -487,13 +488,12 @@
             gain * (grad_ref[q:q + 1] - along[:, at:at + 1] * query_ref[q:q + 1])
             / (length[:, at:at + 1] * SEQ)
         )
-        out_ref[at:at + SEQ] = (
-            inverse_column[at:at + SEQ] * scaled
-            - hidden_ref[at:at + SEQ].astype(f32) * slide[at:at + SEQ]
-        )
-        part = pl.ds(at, SEQ)
-        copies.append(pltpu.make_async_copy(out_ref.at[part], out_far.at[part], sems.at[q]))
-        copies[-1].start()
+        for half in range(2):
+            part = slice(at + half * 32, at + half * 32 + 32)
+            out_ref[part] = inverse_column[part] * scaled - hidden_ref[part].astype(f32) * slide[part]
+            rows = pl.ds(at + half * 32, 32)
+            copies.append(pltpu.make_async_copy(out_ref.at[rows], out_far.at[rows], sems.at[1 + 2 * q + half]))
+            copies[-1].start()
     for copy in copies:
         copy.wait()
 
@@ -546,7 +546,7 @@
             output_kernel, [shape((TOKENS, PART)), shape((1,), jnp.int32)],
             sums, grad, query, stat, tokens, gain, far_outs=(0, 1),
             scratch=[
-                pltpu.VMEM((TOKENS, PART), f32), pltpu.SMEM((1,), jnp.int32), pltpu.SemaphoreType.DMA((3,))
+                pltpu.VMEM((TOKENS, PART), f32), pltpu.SMEM((1,), jnp.int32), pltpu.SemaphoreType.DMA((5,))
             ],
         )
 

time: 145 us -> 145 us (level)
  no operation moved by 1% of the time
where the time goes in v7:
time: 145 us
  blocking collectives  123 us (85%)
  Pallas kernels  10.9 us (8%)
  starting transfers between devices  6.55 us (5%)
  waiting for transfers between devices  2.07 us (1%)
    all_to_all x2, blocking collectives, finish(): lax.all_to_all(parts.reshape(16, 2, EXT), 'z', 0, 0).reshape(OWN, EXT)  36.9 us
    all_to_all x1, blocking collectives, shards(): gathered = lax.all_to_all(payload, 'z', 0, 0)  26.8 us
    all_to_all x2, blocking collectives, finish(): sums = lax.all_to_all(sums, PIPE, 0, 0)  18.1 us
    all_to_all x1, blocking collectives, repeat(): lax.all_to_all(jnp.broadcast_to(state[2], (8, BANK, 128)), PIPE, 0, 0)  15.3 us
    all_to_all x1, blocking collectives, shards(): coded = lax.all_to_all(coded, PIPE, 0, 0)  13.8 us
    all_to_all x1, blocking collectives, shards(): squares = lax.all_to_all(squares, PIPE, 0, 0)  12.4 us
    pallas_call x11, Pallas kernels, call(): pl.pallas_call(kernel, out_shape=outs, in_specs=[place(i, far) for i in r...  10.9 us
    ppermute x1, starting transfers between devices, shards(): came = lax.ppermute(own, 'xh', swap)  4.63 us
  transfers between devices with their start and end apart: 2, of which 1 were waited for; matrix products, arithmetic and copies ran while one was open for 0% of the time, Pallas kernels for 1%

profile of v7, /device:TPU:32, one launch (start us, length us, event | category | flops | bytes accessed | tf_op | source)
XLA Modules:
  0.0 144.5 jit_solution(2640614002758503741)
XLA Ops:
  0.0 0.0 copy-start.7
  0.0 0.0 copy-start.4
  0.0 2.4 %shard_map.73 = (f32[8,40,128]{2,1,0:T(8,128)}, bf16[272,1024]{1,0:T(8,128)(2,1)}) custom-call(bf16[128,1024]{1,0:T(8,128)(2,1)} %bitcast.11, bf16[256,1024]{1,0:T(8,128)(2,1)} %queue_far.1, f32[1,1024]{1,0:T(1,128)} %bitcast.19, bf16[2,1024]{1,0:T(2,128)(2,1)} %keys_far.1), custom_call_target="tpu_custom_call" | custom-call | tf_op jit(solution)/shard_map/pallas_call | solution.py:116
  2.4 0.0 copy-start
  2.4 12.4 %all_to_all.43.sums_ref = f32[8,40,128]{2,1,0:T(8,128)S(1)} all-to-all(f32[8,40,128]{2,1,0:T(8,128)} %get-tuple-element.76), channel_id=1, replica_groups=mesh['xh'=2,'z'=16,'c'=2,'y'=4,'xl'=2] {'y','xl'}, dimensions={0} | all-to-all | bytes 327680 | tf_op jit(solution)/shard_map/all_to_all | solution.py:519
  14.8 4.6 %collective-permute-start = (bf16[272,1024]{1,0:T(8,128)(2,1)}, bf16[272,1024]{1,0:T(8,128)(2,1)S(1)}, u32[]{:S(2)}, u32[]{:S(2)}) collective-permute-start(bf16[272,1024]{1,0:T(8,128)(2,1)} %get-tuple-element.79.own_ref), channel_id=1, source_target_pairs={{0,256},{256,0},{1,257},{257,1},{2,258},{258,2},{3,259},{259,3},{4... | collective-permute-start | bytes 1671176 | tf_op jit(solution)/shard_map/ppermute | solution.py:521
  19.4 0.0 copy-done.7
  19.5 0.0 copy-done.4
  19.5 0.3 shard_map.74
  19.8 26.8 %all_to_all.44.after_ref.gathered_ref = bf16[16,16,128]{2,1,0:T(8,128)(2,1)S(1)} all-to-all(bf16[16,16,128]{2,1,0:T(8,128)(2,1)S(1)} %get-tuple-element.78), channel_id=1, replica_groups=mesh['xh'=2,'z'=16,'c'=2,'y'=4,'xl'=2] {'z'}, dimensions={0} | all-to-all | bytes 131072 | tf_op jit(solution)/shard_map/all_to_all | solution.py:525
  46.6 0.0 copy-start.1
  46.6 0.0 copy-start.2
  46.6 0.0 copy-start.3
  46.6 0.0 collective-permute-done.came_ref
  46.6 0.0 copy-done
  46.6 0.1 shard_map.75.near_ref
  46.7 1.9 %collective-permute-start.1 = (bf16[2,272,1024]{2,1,0:T(8,128)(2,1)S(1)}, bf16[2,272,1024]{2,1,0:T(8,128)(2,1)S(1)}, u32[]{:S(2)}, u32[]{:S(2)}) collective-permute-start(bf16[2,272,1024]{2,1,0:T(8,128)(2,1)S(1)} %shard_map.75.near_ref), channel_id=1, source_target_pairs={{0,8},{8,0},{1,9},{9,1},{2,10},{10,2},{3,11},{11,3},{4,12},{12,4},... | collective-permute-start | bytes 3342344 | tf_op jit(solution)/shard_map/ppermute | solution.py:527
  48.6 0.0 copy-done.1
  48.6 0.0 copy-done.2
  48.6 0.0 copy-done.3
  48.6 0.6 shard_map.76
  49.3 2.1 %collective-permute-done.1.far_ref = bf16[2,272,1024]{2,1,0:T(8,128)(2,1)S(1)} collective-permute-done((bf16[2,272,1024]{2,1,0:T(8,128)(2,1)S(1)}, bf16[2,272,1024]{2,1,0:T(8,128)(2,1)S(1)}, u32[]{:S(2)}, u32[]{:S(2)}) %collective-permute-start.1) | collective-permute-done | bytes 1114144 | tf_op jit(solution)/shard_map/ppermute | solution.py:527
  51.3 0.7 shard_map.77
  52.1 13.8 %all_to_all.45.coded_ref = s16[8,288,128]{2,1,0:T(8,128)(2,1)S(1)} all-to-all(s16[8,288,128]{2,1,0:T(8,128)(2,1)S(1)} %get-tuple-element.82), channel_id=1, replica_groups=mesh['xh'=2,'z'=16,'c'=2,'y'=4,'xl'=2] {'y','xl'}, dimensions={0} | all-to-all | bytes 1179648 | tf_op jit(solution)/shard_map/all_to_all | solution.py:536
  65.9 0.0 copy-start.5
  65.9 1.9 %shard_map.78 = s16[32,2176]{1,0:T(8,128)(2,1)S(1)} custom-call(s16[8,288,128]{2,1,0:T(8,128)(2,1)S(1)} %all_to_all.45.coded_ref, f32[40,128]{1,0:T(8,128)S(1)} %get-tuple-element.180.index_ref, bf16[2,272,1024]{2,1,0:T(8,128)(2,1)S(1)} %shard_map.75.near_ref, bf16[2,272,1024]{2,1,0:T(8,128)(2,1)S(1)} %collective-permute-done.1.far_ref), custom_call_target="tpu_custom_call" | custom-call | tf_op jit(solution)/shard_map/pallas_call | solution.py:116
  67.8 0.1 reshape.29
  67.9 17.6 %all_to_all.46 = s16[16,2,2176]{2,1,0:T(2,128)(2,1)S(1)} all-to-all(s16[16,2,2176]{2,1,0:T(2,128)(2,1)S(1)} %reshape.29), channel_id=1, replica_groups=mesh['xh'=2,'z'=16,'c'=2,'y'=4,'xl'=2] {'z'}, dimensions={0} | all-to-all | bytes 278528 | tf_op jit(solution)/shard_map/all_to_all | solution.py:540
  85.5 0.1 reshape.30.parts_ref
  85.6 0.0 copy-done.5
  85.6 0.6 shard_map.79
  86.1 9.2 %all_to_all.47.sums_ref = f32[8,8,128]{2,1,0:T(8,128)S(1)} all-to-all(f32[8,8,128]{2,1,0:T(8,128)S(1)} %get-tuple-element.85), channel_id=1, replica_groups=mesh['xh'=2,'z'=16,'c'=2,'y'=4,'xl'=2] {'y','xl'}, dimensions={0} | all-to-all | bytes 65536 | tf_op jit(solution)/shard_map/all_to_all | solution.py:544
  95.3 1.0 shard_map.80
  96.3 48.3 %while.12 = (f32[128,1024]{1,0:T(8,128)}, s32[1]{0:T(128)}, f32[272,128]{1,0:T(8,128)S(1)}, f32[40,128]{1,0:T(8,128)S(1)}, bf16[2,272,1024]{2,1,0:T(8,128)(2,1)S...) while((f32[128,1024]{1,0:T(8,128)}, s32[1]{0:T(128)}, ...), condition=%wide.region_2.0_spmd, body=%wide.region_0.0_spmd.sunk | while | flops 243713 | bytes 6684809 | solution.py:558
  96.8 0.1 broadcast_in_dim.4
  96.9 15.3 %all_to_all.48 = f32[8,272,128]{2,1,0:T(8,128)S(1)} all-to-all(f32[8,272,128]{2,1,0:T(8,128)S(1)} %broadcast_in_dim.4), channel_id=1, replica_groups=mesh['xh'=2,'z'=16,'c'=2,'y'=4,'xl'=2] {'y','xl'}, dimensions={0} | all-to-all | bytes 2228224 | tf_op jit(solution)/shard_map/while/body/all_to_all | solution.py:554
  112.2 0.1 reduce_sum.10.dots_ref
  112.3 0.0 copy-start.6
  112.3 1.8 %body.3 = s16[32,2176]{1,0:T(8,128)(2,1)S(1)} custom-call(f32[272,128]{1,0:T(8,128)S(1)} %reduce_sum.10.dots_ref, f32[40,128]{1,0:T(8,128)S(1)} %get-tuple-element.202.index_ref, bf16[2,272,1024]{2,1,0:T(8,128)(2,1)S(1)} %get-tuple-element.203.near_ref, bf16[2,272,1024]{2,1,0:T(8,128)(2,1)S(1)} %get-tuple-element.204.far_ref), custom_call_target="tpu_custom_call" | custom-call | tf_op jit(solution)/shard_map/while/body/pallas_call | solution.py:116
  114.1 0.1 reshape.34
  114.2 19.3 %all_to_all.49 = s16[16,2,2176]{2,1,0:T(2,128)(2,1)S(1)} all-to-all(s16[16,2,2176]{2,1,0:T(2,128)(2,1)S(1)} %reshape.34), channel_id=1, replica_groups=mesh['xh'=2,'z'=16,'c'=2,'y'=4,'xl'=2] {'z'}, dimensions={0} | all-to-all | bytes 278528 | tf_op jit(solution)/shard_map/while/body/all_to_all | solution.py:540
  133.5 0.1 reshape.35.parts_ref
  133.5 0.0 copy-done.6
  133.5 0.6 body.4
  134.1 8.9 %all_to_all.50.sums_ref = f32[8,8,128]{2,1,0:T(8,128)S(1)} all-to-all(f32[8,8,128]{2,1,0:T(8,128)S(1)} %get-tuple-element.173), channel_id=1, replica_groups=mesh['xh'=2,'z'=16,'c'=2,'y'=4,'xl'=2] {'y','xl'}, dimensions={0} | all-to-all | bytes 65536 | tf_op jit(solution)/shard_map/while/body/all_to_all | solution.py:544
  143.0 1.0 body.5
Async XLA Ops:
  0.0 19.4 %copy-start.7 = (f32[1024]{0:T(1024)S(1)}, f32[1024]{0:T(1024)}, u32[]{:S(2)}) copy-start(f32[1024]{0:T(1024)} %param.10) | copy-start | bytes 12292
  0.0 19.5 %copy-start.4 = (bf16[2,64,1024]{2,1,0:T(8,128)(2,1)S(1)}, bf16[2,64,1024]{2,1,0:T(8,128)(2,1)}, u32[]{:S(2)}) copy-start(bf16[2,64,1024]{2,1,0:T(8,128)(2,1)} %param.9) | copy-start | bytes 786436
  2.4 44.2 %copy-start = (bf16[272,1024]{1,0:T(8,128)(2,1)S(1)}, bf16[272,1024]{1,0:T(8,128)(2,1)}, u32[]{:S(2)}) copy-start(bf16[272,1024]{1,0:T(8,128)(2,1)} %get-tuple-element.79.own_ref) | copy-start | bytes 1671172
  14.8 31.8 %collective-permute-start = (bf16[272,1024]{1,0:T(8,128)(2,1)}, bf16[272,1024]{1,0:T(8,128)(2,1)S(1)}, u32[]{:S(2)}, u32[]{:S(2)}) collective-permute-start(bf16[272,1024]{1,0:T(8,128)(2,1)} %get-tuple-element.79.own_ref), channel_id=1, source_target_pairs={{0,256},{256,0},{1,257},{257,1},{2,258},{258,2},{3,259},{259,3},{4... | collective-permute-start | bytes 1671176 | tf_op jit(solution)/shard_map/ppermute | solution.py:521
  46.6 2.0 %copy-start.1 = (s32[128,16]{0,1:T(8,128)S(1)}, s32[128,16]{0,1:T(8,128)}, u32[]{:S(2)}) copy-start(s32[128,16]{0,1:T(8,128)} %param.14) | copy-start | bytes 24580
  46.6 2.0 %copy-start.2 = (f32[128,16]{0,1:T(8,128)S(1)}, f32[128,16]{0,1:T(8,128)}, u32[]{:S(2)}) copy-start(f32[128,16]{0,1:T(8,128)} %param.15) | copy-start | bytes 24580
  46.6 2.1 %copy-start.3 = (s32[128]{0:T(128)S(1)}, s32[128]{0:T(128)}, u32[]{:S(2)}) copy-start(s32[128]{0:T(128)} %param.13) | copy-start | bytes 1540
  46.7 4.6 %collective-permute-start.1 = (bf16[2,272,1024]{2,1,0:T(8,128)(2,1)S(1)}, bf16[2,272,1024]{2,1,0:T(8,128)(2,1)S(1)}, u32[]{:S(2)}, u32[]{:S(2)}) collective-permute-start(bf16[2,272,1024]{2,1,0:T(8,128)(2,1)S(1)} %shard_map.75.near_ref), channel_id=1, source_target_pairs={{0,8},{8,0},{1,9},{9,1},{2,10},{10,2},{3,11},{11,3},{4,12},{12,4},... | collective-permute-start | bytes 3342344 | tf_op jit(solution)/shard_map/ppermute | solution.py:527
  65.9 19.7 %copy-start.5 = (bf16[2,64,1024]{2,1,0:T(8,128)(2,1)S(1)}, bf16[2,64,1024]{2,1,0:T(8,128)(2,1)}, u32[]{:S(2)}) copy-start(bf16[2,64,1024]{2,1,0:T(8,128)(2,1)} %param.9) | copy-start | bytes 786436
  112.3 21.2 %copy-start.6 = (bf16[2,64,1024]{2,1,0:T(8,128)(2,1)S(1)}, bf16[2,64,1024]{2,1,0:T(8,128)(2,1)}, u32[]{:S(2)}) copy-start(bf16[2,64,1024]{2,1,0:T(8,128)(2,1)} %get-tuple-element.225) | copy-start | bytes 786436 | tf_op jit(solution)/shard_map/while
